TPU v7x, 128 devices: a whole 4x4x4 slice. The times are simulated.
128 devices in a mesh: lat: 4 (over z_hi, core), lon: 32 (over x, y, z_lo).
Axes of the slice: x: 4, y: 4, z: 4 (z_hi: 2, z_lo: 2; z = z_hi * 2 + z_lo), core: 2. Of those that a mesh axis runs over, the one named last changes fastest.
Arguments:
- latent: bfloat16 [48, 768, 2, 512], P('lat', 'lon'), may hold values from -8 to 8
- grad_fields: bfloat16 [48, 768, 13, 80], P('lat', 'lon'), may hold values from -6 to 6
- region_ids: int32 [48, 768], P('lat', 'lon'), may hold values from 0 to 2
- level_ids: int32 [13], replicated, may hold values from 0 to 36
- w_qkv: bfloat16 [512, 1536], replicated, may hold values from -0.25 to 0.25
- w_proj: bfloat16 [512, 512], replicated, may hold values from -0.25 to 0.25
- gain: float32 [512], replicated, may hold values from 0.5 to 1.5
- level_table: bfloat16 [37, 512], replicated, may hold values from -6 to 6
- w_key: bfloat16 [512, 512], replicated, may hold values from -0.25 to 0.25
- w_value: bfloat16 [512, 512], replicated, may hold values from -0.25 to 0.25
- w_out: bfloat16 [512, 80], replicated, may hold values from -0.25 to 0.25
Outputs:
- d_latent: bfloat16 [48, 768, 2, 512], P('lat', 'lon')
- grad_qkv: float32 [512, 1536], replicated
- grad_proj: float32 [512, 512], replicated
- grad_gain: float32 [512], replicated
- grad_table: float32 [37, 512], replicated
- grad_key: float32 [512, 512], replicated
- grad_value: float32 [512, 512], replicated
- grad_out: float32 [512, 80], replicated
All inputs are finite; a program needn't handle non-finite values.
Results may differ from a plain program's by a relative error of at most 0.024.
The roundings to bfloat16 on the way count: a program that leaves them out, or rounds other values in their place, can miss the bound.
Values may be sent and summed in bfloat16 or wider, within the bound.
No kernel may reach another device: no remote copies, remote signals or barrier semaphores. Data moves between devices by JAX's collectives and lax.ppermute only.
A program may use at most 128 MiB of HBM per device.

v0:
```python
import functools
import jax
import jax.numpy as jnp
from jax import lax
from jax.experimental import pallas as pl
from jax.experimental.pallas import tpu as pltpu

HEADS = 8
WH = 6
WW = 12
LV = 2
SH = 3
SW = 6
EPS = 1e-05
MASKED = -1e30
F32 = jnp.float32
BF16 = jnp.bfloat16


def dot_nn(a, b):
    return lax.dot_general(a, b, (((1,), (0,)), ((), ())), preferred_element_type=F32)


def dot_nt(a, b):
    return lax.dot_general(a, b, (((1,), (1,)), ((), ())), preferred_element_type=F32)


def dot_tn(a, b):
    return lax.dot_general(a, b, (((0,), (0,)), ((), ())), preferred_element_type=F32)


def swap_rows(a):
    rows, lanes = a.shape
    blocks = a.reshape(rows // 8, 8, lanes)
    later = pltpu.roll(blocks, 7, 1)
    earlier = pltpu.roll(blocks, 1, 1)
    even = lax.broadcasted_iota(jnp.int32, blocks.shape, 1) % 2 == 0
    return jnp.where(even, later, earlier).reshape(rows, lanes)


def section_kernel(
    core_ref, x_ref, f_ref, idc_ref, idr_ref, q_ref, wqkv_ref, wproj_ref, gain_ref, wkey_ref, wval_ref, wout_ref,
    out_ref, grads_ref,
    xw32, xw, pk, probs, at, nrm, inv, mix32, mixb, kk, vv, uu, ww, cc, ds, gg, dkd, dvd, dm32, dp32, dpb, dat, dpk, hs,
):
    n_win = 4
    tok = 144
    rows = 576
    core = core_ref[0, 0]

    def put(half_no, block, matrix):
        for c in range(matrix.shape[1] // 128):
            at_row = 512 * (block + c)
            piece = matrix[:, 128 * c:128 * c + 128].astype(BF16)
            grads_ref[half_no ^ core, at_row:at_row + 512, :] = piece

    lane = lax.broadcasted_iota(jnp.int32, (1, 128), 1)
    half = ((lane < 64).astype(BF16), (lane >= 64).astype(BF16))
    low = lax.broadcasted_iota(jnp.int32, (tok, 128), 1) < 64
    gain = gain_ref[...]

    for h in range(12):
        piece = x_ref[48 * h:48 * h + 48, :].astype(F32)
        for b in range(2):
            xw32[(h // 6) * 2 + b, 24 * (h % 6):24 * (h % 6) + 24, :] = piece[24 * b:24 * b + 24]
    for w in range(n_win):
        xw[w] = xw32[w].astype(BF16)
    flat_x = xw[...].reshape(rows, 512)
    for n in range(6):
        part = dot_nn(flat_x, wqkv_ref[:, 256 * n:256 * n + 256]).astype(BF16)
        pk[:, :, 256 * n:256 * n + 256] = part.reshape(n_win, tok, 256)

    def attend(w, carry):
        bias = jnp.where(idc_ref[w] == idr_ref[w], 0.0, MASKED)
        for hp in range(4):
            q = pk[w, :, 128 * hp:128 * hp + 128]
            k = pk[w, :, 512 + 128 * hp:512 + 128 * hp + 128]
            v = pk[w, :, 1024 + 128 * hp:1024 + 128 * hp + 128]
            outs = []
            for e in range(2):
                s = dot_nt(q * half[e], k) * 0.125 + bias
                p = jnp.exp(s - jnp.max(s, axis=-1, keepdims=True))
                p = p / jnp.sum(p, axis=-1, keepdims=True)
                probs[w, 2 * hp + e] = p
                outs.append(dot_nn(p.astype(BF16), v))
            at[w, :, 128 * hp:128 * hp + 128] = jnp.where(low, outs[0], outs[1]).astype(BF16)
        return carry

    lax.fori_loop(0, n_win, attend, 0)

    flat_at = at[...].reshape(rows, 512)
    nrm[...] = dot_nn(flat_at, wproj_ref[...]).reshape(n_win, tok, 512)
    for w in range(n_win):
        for i in range(6):
            at_row = 48 * (6 * (w // 2) + i) + 24 * (w % 2)
            p = nrm[w, 24 * i:24 * i + 24, :]
            c = p - jnp.mean(p, axis=-1, keepdims=True)
            r = lax.rsqrt(jnp.mean(c * c, axis=-1, keepdims=True) + EPS)
            n = c * r
            nrm[w, 24 * i:24 * i + 24, :] = n
            inv[w, 24 * i:24 * i + 24, :] = jnp.broadcast_to(r, (24, 128))
            mix32[at_row:at_row + 24, :] = xw32[w, 24 * i:24 * i + 24, :] + n * gain
    mixb[...] = mix32[...].astype(BF16)

    mixed = mixb[...]
    for hp in range(4):
        cols = slice(128 * hp, 128 * hp + 128)
        for w_ref, pair in ((wkey_ref, kk), (wval_ref, vv)):
            part = dot_nn(mixed, w_ref[:, cols]).astype(BF16)
            other = swap_rows(part.astype(F32))
            pair[hp, :, 0:128] = part
            pair[hp, :, 128:256] = (-other).astype(BF16)

    row16 = lax.broadcasted_iota(jnp.int32, (16, 128), 0)
    lane16 = lax.broadcasted_iota(jnp.int32, (16, 128), 1)
    own = (row16 // 2 == lane16 % 8).astype(F32)[None]
    zero64 = jnp.zeros((64, 128), BF16)
    for hp in range(4):
        cols = slice(128 * hp, 128 * hp + 128)
        q = q_ref[:, cols] * jnp.asarray(0.125, BF16)
        q_e, q_o = q * half[0], q * half[1]
        rhs = jnp.concatenate(
            [jnp.concatenate([q_e, q_e], axis=1), jnp.concatenate([q_o, q_o], axis=1)], axis=0
        )
        diff = dot_nt(kk[hp], rhs)
        wo = wout_ref[cols, :]
        top = jnp.concatenate(
            [jnp.concatenate([wo[:64], zero64], axis=0), jnp.concatenate([zero64, wo[64:]], axis=0)], axis=1
        )
        u = dot_nn(vv[hp], jnp.concatenate([top, top], axis=0)).astype(BF16)
        for e in range(2):
            d = diff[:, 128 * e:128 * e + 128].reshape(36, 16, 128)
            small = jnp.exp(-jnp.abs(d))
            big = 1.0 / (1.0 + small)
            small = small * big
            weight = jnp.where(d >= 0, big, small)
            ww[2 * hp + e] = (weight * own).astype(BF16).reshape(rows, 128)
            cc[2 * hp + e] = (small * big * (own * 0.125)).reshape(rows, 128)
            uu[2 * hp + e] = u[:, 128 * e:128 * e + 128]

    def group(h, carry):
        line = f_ref[h].astype(F32)
        for o in range(3):
            g16 = pl.ds(pl.multiple_of(48 * h + 16 * o, 16), 16)
            f = line[:, 8 * o:8 * o + 8, :].reshape(104, 128)
            f = jnp.concatenate([f, jnp.zeros((24, 128), F32)], axis=0).astype(BF16)
            dw = dot_nt(uu[:, g16, :].reshape(128, 128), f)
            d = (dw * cc[:, g16, :].reshape(128, 128)).astype(BF16)
            ds[:, g16, :] = d.reshape(8, 16, 128)
            g = dot_nn(ww[:, g16, :].reshape(128, 128), f).astype(BF16)
            gg[:, g16, :] = g.reshape(8, 16, 128)
        return carry

    lax.fori_loop(0, 12, group, 0)

    fold_row = lax.broadcasted_iota(jnp.int32, (128, 128), 0)
    fold_lane = lax.broadcasted_iota(jnp.int32, (128, 128), 1)
    fold = (fold_row // 8 == fold_lane - 80).astype(BF16)
    for hp in range(4):
        cols = slice(128 * hp, 128 * hp + 128)
        q = q_ref[:, cols]
        d = jnp.concatenate([ds[2 * hp], ds[2 * hp + 1]], axis=1)
        g = jnp.concatenate([gg[2 * hp], gg[2 * hp + 1]], axis=1)
        dkd[:, cols] = dot_nn(d, jnp.concatenate([q * half[0], q * half[1]], axis=0)).astype(BF16)
        wo = wout_ref[cols, :]
        top = jnp.concatenate(
            [jnp.concatenate([wo[:64], zero64], axis=0), jnp.concatenate([zero64, wo[64:]], axis=0)], axis=1
        )
        dvd[:, cols] = dot_nt(g, top).astype(BF16)
        dq = dot_tn(kk[hp, :, 0:128], d)
        dq = jnp.concatenate([dq[:64, :128], dq[64:, 128:]], axis=0)
        go = dot_tn(vv[hp, :, 0:128], g)
        go = jnp.concatenate([go[:64, :128], go[64:, 128:]], axis=0)
        dq_hi = dq.astype(BF16)
        dq_lo = (dq - dq_hi.astype(F32)).astype(BF16)
        hs[:, cols] = go + dot_nn(dq_hi, fold) + dot_nn(dq_lo, fold)

    d_mix = dot_nt(dkd[...], wkey_ref[...]) + dot_nt(dvd[...], wval_ref[...])
    dm32[...] = d_mix.astype(BF16).astype(F32)
    put(1, 4, dot_tn(mixed, dkd[...]))
    put(1, 8, dot_tn(mixed, dvd[...]))

    total_gain = jnp.zeros((8, 512), F32)
    for w in range(n_win):
        for i in range(6):
            at_row = 48 * (6 * (w // 2) + i) + 24 * (w % 2)
            g = dm32[at_row:at_row + 24, :]
            n = nrm[w, 24 * i:24 * i + 24, :]
            total_gain = total_gain + jnp.sum((g * n).reshape(3, 8, 512), axis=0)
            gn = g * gain
            m1 = jnp.mean(gn, axis=-1, keepdims=True)
            m2 = jnp.mean(gn * n, axis=-1, keepdims=True)
            r = inv[w, 24 * i:24 * i + 24, 0:1]
            dp32[w, 24 * i:24 * i + 24, :] = r * (gn - m1 - n * m2)
    row_gain = jnp.broadcast_to(jnp.sum(total_gain, axis=0, keepdims=True), (128, 512))
    for hp in range(4):
        cols = slice(128 * hp, 128 * hp + 128)
        column = row_gain[:, cols].T
        lanes = lax.broadcasted_iota(jnp.int32, (128, 128), 1)
        tail = jnp.where(lanes == 96, column, hs[:, cols]).astype(BF16)
        at_row = 6144 + 128 * (hp % 2)
        grads_ref[(hp // 2) ^ core, at_row:at_row + 128, :] = tail
    for half_no in range(2):
        grads_ref[half_no, 6400:6656, :] = jnp.zeros((256, 128), BF16)
    for w in range(n_win):
        dpb[w] = dp32[w].astype(BF16)
    flat_dp = dpb[...].reshape(rows, 512)
    put(1, 0, dot_tn(flat_at, flat_dp))
    dat[...] = dot_nt(flat_dp, wproj_ref[...]).astype(BF16).reshape(n_win, tok, 512)

    def unattend(w, carry):
        for hp in range(4):
            q = pk[w, :, 128 * hp:128 * hp + 128]
            k = pk[w, :, 512 + 128 * hp:512 + 128 * hp + 128]
            v = pk[w, :, 1024 + 128 * hp:1024 + 128 * hp + 128]
            da = dat[w, :, 128 * hp:128 * hp + 128]
            dqs, dks, dvs = [], [], []
            for e in range(2):
                p = probs[w, 2 * hp + e]
                dvs.append(dot_tn(p.astype(BF16), da))
                dw = dot_nt(da * half[e], v)
                s = p * (dw - jnp.sum(p * dw, axis=-1, keepdims=True)) * 0.125
                s = s.astype(BF16)
                dqs.append(dot_nn(s, k))
                dks.append(dot_tn(s, q))
            for at_col, pair in ((0, dqs), (512, dks), (1024, dvs)):
                merged = jnp.where(low, pair[0], pair[1]).astype(BF16)
                dpk[w, :, at_col + 128 * hp:at_col + 128 * hp + 128] = merged
        return carry

    lax.fori_loop(0, n_win, unattend, 0)

    flat_d = dpk[...].reshape(rows, 1536)
    for n in range(3):
        put(0, 4 * n, dot_tn(flat_x, flat_d[:, 512 * n:512 * n + 512]))
    dp32[...] = dot_nt(flat_d, wqkv_ref[...]).reshape(n_win, tok, 512)
    for h in range(12):
        parts = []
        for b in range(2):
            at_row = 48 * h + 24 * b
            parts.append(
                dp32[(h // 6) * 2 + b, 24 * (h % 6):24 * (h % 6) + 24, :] + dm32[at_row:at_row + 24, :]
            )
        out_ref[48 * h:48 * h + 48, :] = jnp.concatenate(parts, axis=0).astype(BF16)


def section(core, x, fields, ids, q128, w_qkv, w_proj, gain, w_key, w_value, w_out):
    vm = lambda shape, kind: pltpu.VMEM(shape, kind)
    scratch = [
        vm((4, 144, 512), F32), vm((4, 144, 512), BF16), vm((4, 144, 1536), BF16), vm((4, 8, 144, 144), F32),
        vm((4, 144, 512), BF16), vm((4, 144, 512), F32), vm((4, 144, 128), F32), vm((576, 512), F32),
        vm((576, 512), BF16), vm((4, 576, 256), BF16), vm((4, 576, 256), BF16), vm((8, 576, 128), BF16),
        vm((8, 576, 128), BF16), vm((8, 576, 128), F32), vm((8, 576, 128), BF16), vm((8, 576, 128), BF16),
        vm((576, 512), BF16), vm((576, 512), BF16), vm((576, 512), F32), vm((4, 144, 512), F32),
        vm((4, 144, 512), BF16), vm((4, 144, 512), BF16), vm((4, 144, 1536), BF16), vm((128, 512), F32),
    ]
    return pl.pallas_call(
        section_kernel,
        out_shape=(jax.ShapeDtypeStruct((576, 512), BF16), jax.ShapeDtypeStruct((2, 6656, 128), BF16)),
        in_specs=[pl.BlockSpec(memory_space=pltpu.SMEM)] + [pl.BlockSpec(memory_space=pltpu.VMEM)] * 11,
        out_specs=[pl.BlockSpec(memory_space=pltpu.VMEM)] * 2,
        scratch_shapes=scratch,
        compiler_params=pltpu.CompilerParams(vmem_limit_bytes=56 * 1024 * 1024),
        cost_estimate=pl.CostEstimate(flops=15_000_000_000, bytes_accessed=12_000_000, transcendentals=2_000_000),
        name="section",
    )(core, x, fields, ids[:, :, None], ids[:, None, :], q128, w_qkv, w_proj, gain[None], w_key, w_value, w_out)


from jax.sharding import Mesh, PartitionSpec as P

LAT = ("z_hi", "core")
LON = ("x", "y", "z_lo")
CHIPS = ("z_hi", "x", "y", "z_lo")


def neighbours(axes, by):
    count = 1
    for axis in axes:
        count *= lax.axis_size(axis)
    return [(i, (i + by) % count) for i in range(count)]


def corner_pairs(by):
    n_lat, n_lon = 4, 32
    return [
        (a * n_lon + b, ((a + by) % n_lat) * n_lon + (b + by) % n_lon) for a in range(n_lat) for b in range(n_lon)
    ]


def fetch(tile, lat_axis, lon_axis):
    h, w = tile.shape[lat_axis], tile.shape[lon_axis]
    first = lax.slice_in_dim(tile, 0, SH, axis=lat_axis)
    rest = lax.slice_in_dim(tile, SH, h, axis=lat_axis)
    below = lax.ppermute(lax.slice_in_dim(first, SW, w, axis=lon_axis), LAT, neighbours(LAT, -1))
    right = lax.ppermute(lax.slice_in_dim(rest, 0, SW, axis=lon_axis), LON, neighbours(LON, -1))
    corner = lax.ppermute(lax.slice_in_dim(first, 0, SW, axis=lon_axis), LAT + LON, corner_pairs(-1))
    inner = lax.slice_in_dim(rest, SW, w, axis=lon_axis)
    return lax.concatenate(
        [lax.concatenate([inner, right], lon_axis), lax.concatenate([below, corner], lon_axis)], lat_axis
    )


def send_back(tile):
    h, w = tile.shape[0], tile.shape[1]
    above = lax.ppermute(tile[h - SH:, :w - SW], LAT, neighbours(LAT, 1))
    left = lax.ppermute(tile[:h - SH, w - SW:], LON, neighbours(LON, 1))
    corner = lax.ppermute(tile[h - SH:, w - SW:], LAT + LON, corner_pairs(1))
    top = jnp.concatenate([corner, above], axis=1)
    bottom = jnp.concatenate([left, tile[:h - SH, :w - SW]], axis=1)
    return jnp.concatenate([top, bottom], axis=0)


def sum_all(grads, core):
    swap = [(0, 1), (1, 0)]
    other = lax.ppermute(grads[1], "core", swap)
    mine = (grads[0].astype(F32) + other.astype(F32)).astype(BF16)
    pieces = lax.all_to_all(mine.reshape(64, 104, 128), CHIPS, split_axis=0, concat_axis=0, tiled=True)
    piece = jnp.sum(pieces.astype(F32), axis=0).astype(BF16)
    spread = jnp.broadcast_to(piece[None], (64, 104, 128))
    mine = lax.all_to_all(spread, CHIPS, split_axis=0, concat_axis=0, tiled=True).reshape(6656, 128)
    other = lax.ppermute(mine, "core", swap)
    first = core == 0
    return jnp.where(first, mine, other), jnp.where(first, other, mine)


def matrix(blocks):
    return blocks.reshape(-1, 512, 128).transpose(1, 0, 2).reshape(512, -1).astype(F32)


def shards(
    latent, grad_fields, region_ids, level_ids, w_qkv, w_proj, gain, level_table, w_key, w_value, w_out
):
    core = lax.axis_index("core")
    tokens = fetch(latent, 0, 1)
    fields = fetch(grad_fields.transpose(0, 2, 1, 3), 0, 2)
    x = tokens.reshape(576, 512)
    f = jnp.pad(fields, ((0, 0), (0, 0), (0, 0), (0, 48)))
    ids = region_ids.reshape(2, 6, 2, 12).transpose(0, 2, 1, 3).reshape(4, 72)
    ids = jnp.repeat(ids, 2, axis=1)
    onehot = (level_ids[:, None] == jnp.arange(37, dtype=jnp.int32)[None, :]).astype(F32)
    q = jnp.sum(onehot[:, :, None] * level_table.astype(F32)[None], axis=1).astype(BF16)
    q128 = jnp.pad(jnp.repeat(q, 8, axis=0), ((0, 24), (0, 0)))
    out, grads = section(
        core.reshape(1, 1), x, f, ids, q128, w_qkv, w_proj, gain, w_key, w_value, jnp.pad(w_out, ((0, 0), (0, 48)))
    )
    d_latent = send_back(out.reshape(12, 24, 2, 512))
    lower, upper = sum_all(grads, core)
    tail = jnp.concatenate([lower[6144:6400], upper[6144:6400]], axis=0).astype(F32)
    d_query = tail[:, 80:93].T
    grad_table = jnp.sum(onehot[:, :, None] * d_query[:, None, :], axis=0)
    return (
        d_latent, matrix(lower[:6144]), matrix(upper[:2048]), tail[:, 96], grad_table, matrix(upper[2048:4096]),
        matrix(upper[4096:6144]), tail[:, :80],
    )


def solution(mesh):
    fine = Mesh(mesh.devices.reshape(2, 2, 4, 4, 2), LAT + LON)
    tile = P(LAT, LON, None, None)
    return jax.shard_map(
        shards,
        mesh=fine,
        in_specs=(tile, tile, P(LAT, LON)) + (P(),) * 8,
        out_specs=(tile,) + (P(),) * 7,
        check_vma=False,
    )
```

profile of v0, /device:TPU:1, one launch (start us, length us, event | category | flops | bytes accessed | tf_op | source)
XLA Modules:
  0.0 163.9 jit_solution(13702513210131528805)
XLA Ops:
  0.6 0.0 copy-start.4
  0.6 0.0 copy-start.3
  0.7 0.9 slice.84
  1.6 7.7 %collective-permute-start.2 = (bf16[3,6,2,512]{3,2,1,0:T(2,128)(2,1)S(1)}, bf16[3,6,2,512]{3,2,1,0:T(2,128)(2,1)S(1)}, u32[]{:S(2)}, u32[]{:S(2)}) collective-permute-start(bf16[3,6,2,512]{3,2,1,0:T(2,128)(2,1)S(1)} %slice.84), channel_id=1, source_target_pairs={{0,127},{1,96},{2,97},{3,98},{4,99},{5,100},{6,101},{7,102},{8,103... | collective-permute-start | bytes 110600 | tf_op jit(solution)/shard_map/ppermute | solution.py:296
  9.3 0.9 slice.107
  10.2 1.4 collective-permute-start.5
  11.6 1.0 slice.83
  12.5 1.3 collective-permute-start.1
  13.9 1.0 slice.82
  14.9 1.0 collective-permute-start
  15.9 1.0 slice.105
  16.8 0.8 collective-permute-start.3
  17.6 0.7 fusion.8
  18.4 0.8 convert_element_type.85
  19.2 0.2 multiply_reduce_fusion.1
  19.4 1.0 slice.106
  20.4 0.2 slice.81
  20.7 0.3 slice.104
  21.0 0.1 reshape.93
  21.1 0.1 reshape.94
  21.2 0.1 copy.49
  21.3 0.7 copy.52.idr_ref
  22.0 0.1 copy.50
  22.1 0.7 pad.13.q_ref
  22.8 0.7 pad.14.wout_ref
  23.5 1.7 %copy.51.idc_ref = s32[4,144,1]{2,1,0:T(8,128)} copy(s32[4,144,1]{0,1,2:T(8,128)S(1)} %bitcast.64) | data formatting | bytes 4608 | tf_op jit(solution)/shard_map/broadcast_in_dim;reshape | solution.py:266
  25.2 1.6 collective-permute-start.4
  26.9 0.9 maximum_maximum_fusion
  27.7 1.0 reshape.92.x_ref
  28.8 3.6 %collective-permute-done.4 = bf16[3,13,18,80]{3,2,1,0:T(8,128)(2,1)S(1)} collective-permute-done((bf16[3,13,18,80]{3,2,1,0:T(8,128)(2,1)S(1)}, bf16[3,13,18,80]{3,2,1,0:T(8,128)(2,1)S(1)}, u32[]{:S(2)}, u32[]{:S(2)}) %collective-permute-start.4) | collective-permute-done | bytes 112352 | tf_op jit(solution)/shard_map/ppermute | solution.py:294
  32.4 1.5 fusion.6.f_ref
  33.9 33.0 %section.1 = (bf16[576,512]{1,0:T(8,128)(2,1)}, bf16[2,6656,128]{2,1,0:T(8,128)(2,1)}) custom-call(s32[1,1]{1,0:T(1,128)} %bitcast.core_ref, bf16[576,512]{1,0:T(8,128)(2,1)} %reshape.92.x_ref, bf16[12,13,24,128]{3,2,1,0:T(8,128)(2,1)} %fusion.6.f_ref, s32[4,144,1]{2,1,0:T(8,128)} %copy.51.idc_ref, s32[4,1,144]{2,1,0:T(1,128)} %copy.52.idr_ref, ...), custom_call_target="tpu_custom_call" | custom-call | flops 15000000512 | bytes 12000000 | tf_op jit(solution)/shard_map/section/pallas_call | solution.py:257
  66.9 1.7 %slice_bitcast_fusion = bf16[6656,128]{1,0:T(8,128)(2,1)S(1)} fusion(bf16[2,6656,128]{2,1,0:T(8,128)(2,1)} %get-tuple-element.11), kind=kLoop, calls=%fused_computation.8 | loop fusion | bytes 3407872 | tf_op jit(solution)/shard_map/squeeze | solution.py:315
  68.6 0.1 collective-permute-start.9
  68.7 3.6 %collective-permute-done.9 = bf16[6656,128]{1,0:T(8,128)(2,1)S(1)} collective-permute-done((bf16[6656,128]{1,0:T(8,128)(2,1)S(1)}, bf16[6656,128]{1,0:T(8,128)(2,1)S(1)}, u32[]{:S(2)}, u32[]{:S(2)}) %collective-permute-start.9) | collective-permute-done | bytes 1703968 | tf_op jit(solution)/shard_map/ppermute | solution.py:315
  72.3 0.4 fusion
  72.7 28.1 %all_to_all.10 = bf16[64,104,128]{2,1,0:T(8,128)(2,1)S(1)} all-to-all(bf16[64,104,128]{2,1,0:T(8,128)(2,1)S(1)} %bitcast.52), channel_id=1, replica_groups=mesh['z_hi'=2,'core'=2,'x'=4,'y'=4,'z_lo'=2] {'z_hi','x','y','z_lo'}, dimensions={0} | all-to-all | bytes 3407872 | tf_op jit(solution)/shard_map/all_to_all | solution.py:317
  100.9 0.3 reduce_sum.31
  101.1 0.2 broadcast_in_dim.11
  101.4 0.0 copy-start.5
  101.4 29.5 %all_to_all.11 = bf16[64,104,128]{2,1,0:T(8,128)(2,1)S(1)} all-to-all(bf16[64,104,128]{2,1,0:T(8,128)(2,1)S(1)} %broadcast_in_dim.11), channel_id=1, replica_groups=mesh['z_hi'=2,'core'=2,'x'=4,'y'=4,'z_lo'=2] {'z_hi','x','y','z_lo'}, dimensions={0} | all-to-all | bytes 3407872 | tf_op jit(solution)/shard_map/all_to_all | solution.py:320
  130.8 3.1 %collective-permute-start.10 = (bf16[6656,128]{1,0:T(8,128)(2,1)S(1)}, bf16[6656,128]{1,0:T(8,128)(2,1)}, u32[]{:S(2)}, u32[]{:S(2)}) collective-permute-start(bf16[6656,128]{1,0:T(8,128)(2,1)S(1)} %bitcast.53), channel_id=1, source_target_pairs={{0,32},{32,0},{1,33},{33,1},{2,34},{34,2},{3,35},{35,3},{4,36},{36... | collective-permute-start | bytes 5111816 | tf_op jit(solution)/shard_map/ppermute | solution.py:321
  133.9 0.2 reshape.96
  134.1 0.1 slice.110
  134.2 0.1 slice.109
  134.3 2.0 %collective-permute-start.7 = (bf16[3,18,2,512]{3,2,1,0:T(2,128)(2,1)S(1)}, bf16[3,18,2,512]{3,2,1,0:T(2,128)(2,1)S(1)}, u32[]{:S(2)}, u32[]{:S(2)}) collective-permute-start(bf16[3,18,2,512]{3,2,1,0:T(2,128)(2,1)S(1)} %slice.109), channel_id=1, source_target_pairs={{0,32},{32,64},{64,96},{96,0},{1,33},{33,65},{65,97},{97,1},{2,34}... | collective-permute-start | bytes 331784 | tf_op jit(solution)/shard_map/ppermute | solution.py:305
  136.3 0.5 collective-permute-start.8
  136.8 0.9 collective-permute-start.6
  137.7 0.2 slice.111
  138.0 7.2 %collective-permute-done.6 = bf16[3,6,2,512]{3,2,1,0:T(2,128)(2,1)S(1)} collective-permute-done((bf16[3,6,2,512]{3,2,1,0:T(2,128)(2,1)S(1)}, bf16[3,6,2,512]{3,2,1,0:T(2,128)(2,1)S(1)}, u32[]{:S(2)}, u32[]{:S(2)}) %collective-permute-start.6) | collective-permute-done | bytes 36896 | tf_op jit(solution)/shard_map/ppermute | solution.py:307
  145.2 1.7 %maximum_maximum_fusion.1 = bf16[12,24,2,512]{3,2,1,0:T(2,128)(2,1)} fusion(bf16[9,18,2,512]{3,2,1,0:T(2,128)(2,1)S(1)} %slice.111, bf16[9,6,2,512]{3,2,1,0:T(2,128)(2,1)S(1)} %collective-permute-done.8, bf16[3,18,2,512]{3,2,1,0:T(2,128)(2,1)S(1)} %collective-permute-done.7, bf16[3,6,2,512]{3,2,1,0:T(2,128)(2,1)S(1)} %collective-permute-done.6), kind=kLoop, calls=%fused_computation.23 | loop fusion | flops 884736 | bytes 1179648 | tf_op jit(solution)/shard_map/concatenate | solution.py:310
  146.9 1.7 %broadcast_select_fusion = (bf16[6656,128]{1,0:T(8,128)(2,1)S(1)}, bf16[6656,128]{1,0:T(8,128)(2,1)S(1)}) fusion(bf16[6656,128]{1,0:T(8,128)(2,1)} %collective-permute-done.10, pred[]{:T(512)S(6)} %eq.23, bf16[64,104,128]{2,1,0:T(8,128)(2,1)S(1)} %all_to_all.11), kind=kLoop, calls=%fused_computation.9 | loop fusion | flops 1703936 | bytes 6815745 | tf_op jit(solution)/shard_map/jit(_where)/select_n | solution.py:323
  148.6 1.1 fusion.9
  149.6 1.2 slice.112
  150.9 0.8 slice_reduce_fusion
  151.7 0.1 slice_bitcast_fusion.1
  151.8 0.8 copy.59
  152.6 0.1 copy.55
  152.8 0.8 multiply_reduce_fusion
  153.5 1.1 copy_bitcast_fusion.2
  154.6 1.7 %convert_bitcast_fusion = f32[512,12,128]{2,0,1:T(8,128)S(1)} fusion(bf16[12,512,128]{2,1,0:T(8,128)(2,1)} %bitcast.54), kind=kLoop, calls=%fused_computation.2 | loop fusion | flops 786432 | bytes 4718592 | tf_op jit(solution)/shard_map/convert_element_type | solution.py:327
  156.3 2.3 %copy.53 = f32[512,12,128]{0,2,1:T(8,128)} copy(f32[512,12,128]{2,0,1:T(8,128)S(1)} %convert_bitcast_fusion) | data formatting | bytes 6291456 | tf_op jit(solution)/shard_map/convert_element_type | solution.py:327
  158.7 3.6 %copy.58 = f32[512,1536]{1,0:T(8,128)} copy(f32[512,1536]{0,1:T(8,128)} %bitcast.51) | data formatting | bytes 6291456
  162.3 1.6 copy_bitcast_fusion
  (28 shorter events, 0.2 us)
Async XLA Ops:
  0.6 19.8 %copy-start.4 = (bf16[12,24,2,512]{3,2,1,0:T(2,128)(2,1)S(1)}, bf16[12,24,2,512]{3,2,1,0:T(2,128)(2,1)}, u32[]{:S(2)}) copy-start(bf16[12,24,2,512]{3,2,1,0:T(2,128)(2,1)} %param.11) | copy-start | bytes 1769476
  0.6 20.0 %copy-start.3 = (bf16[12,24,13,80]{3,1,2,0:T(8,128)(2,1)S(1)}, bf16[12,24,13,80]{3,1,2,0:T(8,128)(2,1)}, u32[]{:S(2)}) copy-start(bf16[12,24,13,80]{3,1,2,0:T(8,128)(2,1)} %param.12) | copy-start | bytes 1797124
  1.6 23.6 %collective-permute-start.2 = (bf16[3,6,2,512]{3,2,1,0:T(2,128)(2,1)S(1)}, bf16[3,6,2,512]{3,2,1,0:T(2,128)(2,1)S(1)}, u32[]{:S(2)}, u32[]{:S(2)}) collective-permute-start(bf16[3,6,2,512]{3,2,1,0:T(2,128)(2,1)S(1)} %slice.84), channel_id=1, source_target_pairs={{0,127},{1,96},{2,97},{3,98},{4,99},{5,100},{6,101},{7,102},{8,103... | collective-permute-start | bytes 110600 | tf_op jit(solution)/shard_map/ppermute | solution.py:296
  10.2 18.6 %collective-permute-start.5 = (bf16[3,13,6,80]{3,2,1,0:T(8,128)(2,1)S(1)}, bf16[3,13,6,80]{3,2,1,0:T(8,128)(2,1)S(1)}, u32[]{:S(2)}, u32[]{:S(2)}) collective-permute-start(bf16[3,13,6,80]{3,2,1,0:T(8,128)(2,1)S(1)} %slice.107), channel_id=1, source_target_pairs={{0,127},{1,96},{2,97},{3,98},{4,99},{5,100},{6,101},{7,102},{8,103... | collective-permute-start | bytes 112328 | tf_op jit(solution)/shard_map/ppermute | solution.py:296
  12.5 14.3 %collective-permute-start.1 = (bf16[3,18,2,512]{3,2,1,0:T(2,128)(2,1)S(1)}, bf16[3,18,2,512]{3,2,1,0:T(2,128)(2,1)S(1)}, u32[]{:S(2)}, u32[]{:S(2)}) collective-permute-start(bf16[3,18,2,512]{3,2,1,0:T(2,128)(2,1)S(1)} %slice.83), channel_id=1, source_target_pairs={{0,96},{32,0},{64,32},{96,64},{1,97},{33,1},{65,33},{97,65},{2,98}... | collective-permute-start | bytes 331784 | tf_op jit(solution)/shard_map/ppermute | solution.py:294
  14.9 6.1 %copy-start.7 = (s32[12,24]{1,0:T(8,128)S(1)}, s32[12,24]{1,0:T(8,128)}, u32[]{:S(2)}) copy-start(s32[12,24]{1,0:T(8,128)} %param.13) | copy-start | bytes 3460
  14.9 12.0 %collective-permute-start = (bf16[9,6,2,512]{3,2,1,0:T(2,128)(2,1)S(1)}, bf16[9,6,2,512]{3,2,1,0:T(2,128)(2,1)S(1)}, u32[]{:S(2)}, u32[]{:S(2)}) collective-permute-start(bf16[9,6,2,512]{3,2,1,0:T(2,128)(2,1)S(1)} %slice.82), channel_id=1, source_target_pairs={{0,31},{1,0},{2,1},{3,2},{4,3},{5,4},{6,5},{7,6},{8,7},{9,8},{10,9... | collective-permute-start | bytes 331784 | tf_op jit(solution)/shard_map/ppermute | solution.py:295
  16.8 5.2 %copy-start.6 = (bf16[512,80]{0,1:T(8,128)(2,1)S(1)}, bf16[512,80]{0,1:T(8,128)(2,1)}, u32[]{:S(2)}) copy-start(bf16[512,80]{0,1:T(8,128)(2,1)} %param.21) | copy-start | bytes 245764
  16.8 11.9 %collective-permute-start.3 = (bf16[9,13,6,80]{3,2,1,0:T(8,128)(2,1)S(1)}, bf16[9,13,6,80]{3,2,1,0:T(8,128)(2,1)S(1)}, u32[]{:S(2)}, u32[]{:S(2)}) collective-permute-start(bf16[9,13,6,80]{3,2,1,0:T(8,128)(2,1)S(1)} %slice.105), channel_id=1, source_target_pairs={{0,31},{1,0},{2,1},{3,2},{4,3},{5,4},{6,5},{7,6},{8,7},{9,8},{10,9... | collective-permute-start | bytes 336968 | tf_op jit(solution)/shard_map/ppermute | solution.py:295
  25.2 7.2 %collective-permute-start.4 = (bf16[3,13,18,80]{3,2,1,0:T(8,128)(2,1)S(1)}, bf16[3,13,18,80]{3,2,1,0:T(8,128)(2,1)S(1)}, u32[]{:S(2)}, u32[]{:S(2)}) collective-permute-start(bf16[3,13,18,80]{3,2,1,0:T(8,128)(2,1)S(1)} %slice.106), channel_id=1, source_target_pairs={{0,96},{32,0},{64,32},{96,64},{1,97},{33,1},{65,33},{97,65},{2,98}... | collective-permute-start | bytes 336968 | tf_op jit(solution)/shard_map/ppermute | solution.py:294
  66.9 5.4 %copy-start = (bf16[2,6656,128]{2,1,0:T(8,128)(2,1)S(1)}, bf16[2,6656,128]{2,1,0:T(8,128)(2,1)}, u32[]{:S(2)}) copy-start(bf16[2,6656,128]{2,1,0:T(8,128)(2,1)} %get-tuple-element.11) | copy-start | bytes 10223620
  68.6 3.7 %collective-permute-start.9 = (bf16[6656,128]{1,0:T(8,128)(2,1)S(1)}, bf16[6656,128]{1,0:T(8,128)(2,1)S(1)}, u32[]{:S(2)}, u32[]{:S(2)}) collective-permute-start(bf16[6656,128]{1,0:T(8,128)(2,1)S(1)} %slice_bitcast_fusion), channel_id=1, source_target_pairs={{0,32},{32,0},{1,33},{33,1},{2,34},{34,2},{3,35},{35,3},{4,36},{36... | collective-permute-start | bytes 5111816 | tf_op jit(solution)/shard_map/ppermute | solution.py:315
  101.4 32.5 %copy-start.5 = (bf16[576,512]{1,0:T(8,128)(2,1)S(1)}, bf16[576,512]{1,0:T(8,128)(2,1)}, u32[]{:S(2)}) copy-start(bf16[576,512]{1,0:T(8,128)(2,1)} %get-tuple-element.10) | copy-start | bytes 1769476
  130.8 16.0 %collective-permute-start.10 = (bf16[6656,128]{1,0:T(8,128)(2,1)S(1)}, bf16[6656,128]{1,0:T(8,128)(2,1)}, u32[]{:S(2)}, u32[]{:S(2)}) collective-permute-start(bf16[6656,128]{1,0:T(8,128)(2,1)S(1)} %bitcast.53), channel_id=1, source_target_pairs={{0,32},{32,0},{1,33},{33,1},{2,34},{34,2},{3,35},{35,3},{4,36},{36... | collective-permute-start | bytes 5111816 | tf_op jit(solution)/shard_map/ppermute | solution.py:321
  134.3 10.9 %collective-permute-start.7 = (bf16[3,18,2,512]{3,2,1,0:T(2,128)(2,1)S(1)}, bf16[3,18,2,512]{3,2,1,0:T(2,128)(2,1)S(1)}, u32[]{:S(2)}, u32[]{:S(2)}) collective-permute-start(bf16[3,18,2,512]{3,2,1,0:T(2,128)(2,1)S(1)} %slice.109), channel_id=1, source_target_pairs={{0,32},{32,64},{64,96},{96,0},{1,33},{33,65},{65,97},{97,1},{2,34}... | collective-permute-start | bytes 331784 | tf_op jit(solution)/shard_map/ppermute | solution.py:305
  136.3 8.9 %collective-permute-start.8 = (bf16[9,6,2,512]{3,2,1,0:T(2,128)(2,1)S(1)}, bf16[9,6,2,512]{3,2,1,0:T(2,128)(2,1)S(1)}, u32[]{:S(2)}, u32[]{:S(2)}) collective-permute-start(bf16[9,6,2,512]{3,2,1,0:T(2,128)(2,1)S(1)} %slice.110), channel_id=1, source_target_pairs={{0,1},{1,2},{2,3},{3,4},{4,5},{5,6},{6,7},{7,8},{8,9},{9,10},{10,1... | collective-permute-start | bytes 331784 | tf_op jit(solution)/shard_map/ppermute | solution.py:306
  136.8 8.4 %collective-permute-start.6 = (bf16[3,6,2,512]{3,2,1,0:T(2,128)(2,1)S(1)}, bf16[3,6,2,512]{3,2,1,0:T(2,128)(2,1)S(1)}, u32[]{:S(2)}, u32[]{:S(2)}) collective-permute-start(bf16[3,6,2,512]{3,2,1,0:T(2,128)(2,1)S(1)} %slice.108), channel_id=1, source_target_pairs={{0,33},{1,34},{2,35},{3,36},{4,37},{5,38},{6,39},{7,40},{8,41},{9,... | collective-permute-start | bytes 110600 | tf_op jit(solution)/shard_map/ppermute | solution.py:307
  158.7 3.6 %copy-start.1 = (bf16[2048,128]{1,0:T(8,128)(2,1)S(1)}, bf16[2048,128]{1,0:T(8,128)(2,1)}, u32[]{:S(2)}) copy-start(bf16[2048,128]{1,0:T(8,128)(2,1)} %get-tuple-element.38) | copy-start | bytes 1572868
  158.7 3.6 %copy-start.2 = (bf16[2048,128]{1,0:T(8,128)(2,1)S(1)}, bf16[2048,128]{1,0:T(8,128)(2,1)}, u32[]{:S(2)}) copy-start(bf16[2048,128]{1,0:T(8,128)(2,1)} %get-tuple-element.39) | copy-start | bytes 1572868
where the time goes:
time: 164 us
  blocking collectives  57.6 us (35%)
  Pallas kernels  33 us (20%)
  local copies, waits for them, and re-layouts  24.3 us (15%)
  starting transfers between devices  20.4 us (12%)
  waiting for transfers between devices  14.4 us (9%)
  other arithmetic  13.3 us (8%)
    pallas_call x1, Pallas kernels, section(): pl.pallas_call(section_kernel, out_shape=(jax.ShapeDtypeStruct((576, 512)...  33 us
    all_to_all x1, blocking collectives, sum_all(): lax.all_to_all(spread, CHIPS, split_axis=0, concat_axis=0, tiled=True)  29.5 us
    all_to_all x1, blocking collectives, sum_all(): lax.all_to_all(mine.reshape(64, 104, 128), CHIPS, split_axis=0, concat_ax...  28.1 us
    ppermute x2, starting transfers between devices, fetch(): lax.ppermute(lax.slice_in_dim(first, 0, SW, axis=lon_axis), LAT + LON, co...  9.1 us
    ppermute x1, waiting for transfers between devices, send_back(): corner = lax.ppermute(tile[h - SH:, w - SW:], LAT + LON, corner_pairs(1))  7.24 us
    unnamed x19, local copies, waits for them, and re-layouts  4.58 us
    convert_element_type x3, other arithmetic, matrix(): blocks.reshape(-1, 512, 128).transpose(1, 0, 2).reshape(512, -1).astype(F32)  4.38 us
    ppermute x2, waiting for transfers between devices, fetch(): lax.ppermute(lax.slice_in_dim(first, SW, w, axis=lon_axis), LAT, neighbou...  3.6 us
  transfers between devices with their start and end apart: 11, of which 3 were waited for; matrix products, arithmetic and copies ran while one was open for 9% of the time, Pallas kernels for 0%

commit v1 on v0

v1 whole, which is shorter than its diff:
```python
import functools
import jax
import jax.numpy as jnp
from jax import lax
from jax.experimental import pallas as pl
from jax.experimental.pallas import tpu as pltpu

HEADS = 8
WH = 6
WW = 12
LV = 2
SH = 3
SW = 6
EPS = 1e-05
MASKED = -1e30
F32 = jnp.float32
BF16 = jnp.bfloat16


def dot_nn(a, b):
    return lax.dot_general(a, b, (((1,), (0,)), ((), ())), preferred_element_type=F32)


def dot_nt(a, b):
    return lax.dot_general(a, b, (((1,), (1,)), ((), ())), preferred_element_type=F32)


def dot_tn(a, b):
    return lax.dot_general(a, b, (((0,), (0,)), ((), ())), preferred_element_type=F32)


def swap_rows(a):
    rows, lanes = a.shape
    blocks = a.reshape(rows // 8, 8, lanes)
    later = pltpu.roll(blocks, 7, 1)
    earlier = pltpu.roll(blocks, 1, 1)
    even = lax.broadcasted_iota(jnp.int32, blocks.shape, 1) % 2 == 0
    return jnp.where(even, later, earlier).reshape(rows, lanes)


def nine_tiles(levels):
    lane = lax.broadcasted_iota(jnp.int32, levels.shape[1:], 1)
    tiles = [levels[p] for p in range(9)]
    for m in range(4):
        extra = levels[9 + m]
        tiles[2 * m] = jnp.where(lane < 80, tiles[2 * m], pltpu.roll(extra, 80, 1))
        tiles[2 * m + 1] = jnp.where(lane < 80, tiles[2 * m + 1], pltpu.roll(extra, 32, 1))
    return jnp.stack(tiles, axis=0)


def all_levels(tiles):
    lane = lax.broadcasted_iota(jnp.int32, tiles.shape[1:], 1)
    levels = [tiles[p] for p in range(9)]
    for m in range(4):
        levels.append(
            jnp.where(lane < 48, pltpu.roll(tiles[2 * m], 48, 1), pltpu.roll(tiles[2 * m + 1], 96, 1))
        )
    return jnp.stack(levels, axis=0)[:, :, :80]


def pack_kernel(x_ref, f_ref, below_ref, right_ref, corner_ref, wide):
    for c in range(4):
        cols = slice(128 * c, 128 * c + 128)
        below_ref[144 * c:144 * c + 144, :] = x_ref[0:144, cols]
        for h in range(3):
            corner_ref[16 * (3 * c + h):16 * (3 * c + h) + 16, :] = x_ref[48 * h:48 * h + 16, cols]
        for h in range(9):
            right_ref[16 * (9 * c + h):16 * (9 * c + h) + 16, :] = x_ref[48 * (h + 3):48 * (h + 3) + 16, cols]
    lines, sides = [], []
    for h in range(12):
        wide[h, :, :, 0:80] = f_ref[h].astype(F32)
        if h < 3:
            lines.append(nine_tiles(wide[h]).reshape(216, 128))
        sides.append(nine_tiles(wide[h, :, 0:8, :]).reshape(72, 128))
    below_ref[576:1224, :] = jnp.concatenate(lines, axis=0).astype(BF16)
    right_ref[576:1224, :] = jnp.concatenate(sides[3:], axis=0).astype(BF16)
    corner_ref[192:408, :] = jnp.concatenate(sides[:3], axis=0).astype(BF16)


def pack(x, fields):
    vmem = pl.BlockSpec(memory_space=pltpu.VMEM)
    return pl.pallas_call(
        pack_kernel,
        out_shape=tuple(jax.ShapeDtypeStruct((rows, 128), BF16) for rows in (1224, 1224, 408)),
        in_specs=[vmem, vmem],
        out_specs=[vmem] * 3,
        scratch_shapes=[pltpu.VMEM((12, 13, 24, 128), F32)],
        compiler_params=pltpu.CompilerParams(vmem_limit_bytes=16 * 1024 * 1024),
        cost_estimate=pl.CostEstimate(flops=2_000_000, bytes_accessed=3_000_000, transcendentals=0),
        name="pack",
    )(x, fields)


def section_kernel(
    core_ref, level_ref, x_ref, below_ref, right_ref, corner_ref, ids_ref, table_ref, gain_ref, wout_ref,
    wqkv_hbm, wproj_hbm, wkey_hbm, wval_hbm, f_hbm,
    out_hbm, keep_hbm, send_hbm,
    xw32, xw, pk, probs, at, nrm, inv, mix32, mixb, kk, vv, uu, ww, cc, ds, gg, dkd, dvd, dm32, dp32, dpb, dat, dpk, hs, at_t, x_t, hot, q32, qs, wo128, f_below, f_right, f_corner,
    wqkv_ref, wproj_ref, wkey_ref, wval_ref, f_ref, out_ref, grads_ref, in_sem, out_sem,
):
    n_win = 4
    tok = 144
    rows = 576
    core = core_ref[0, 0]
    loads = [
        pltpu.make_async_copy(source, target, in_sem.at[n])
        for n, (source, target) in enumerate(
            (
                (wqkv_hbm, wqkv_ref), (wproj_hbm, wproj_ref), (wkey_hbm, wkey_ref), (wval_hbm, wval_ref),
                (f_hbm, f_ref),
            )
        )
    ]
    for load in loads:
        load.start()

    def put(half_no, block, matrix):
        for c in range(matrix.shape[1] // 128):
            at_row = 512 * (block + c)
            piece = matrix[:, 128 * c:128 * c + 128].astype(BF16)
            grads_ref[half_no ^ core, at_row:at_row + 512, :] = piece

    lane = lax.broadcasted_iota(jnp.int32, (1, 128), 1)
    half = ((lane < 64).astype(BF16), (lane >= 64).astype(BF16))
    eighth = (half[0] * jnp.asarray(0.125, BF16), half[1] * jnp.asarray(0.125, BF16))
    low = lax.broadcasted_iota(jnp.int32, (tok, 128), 1) < 64
    gain = gain_ref[...]

    wide = table_ref[...].astype(F32)
    table_row = lax.broadcasted_iota(jnp.int32, wide.shape, 0)
    for p in range(13):
        q32[8 * p:8 * p + 8, :] = jnp.broadcast_to(
            jnp.sum(jnp.where(table_row == level_ref[p], wide, 0.0), axis=0, keepdims=True), (8, 512)
        )
    q32[104:128, :] = jnp.zeros((24, 512), F32)
    qs[...] = q32[...].astype(BF16)
    wo128[...] = jnp.zeros((512, 128), BF16)
    wo128[:, 0:80] = wout_ref[...].T

    ids = ids_ref[...].astype(F32)
    token = lax.broadcasted_iota(jnp.int32, (tok, 24), 0)
    spot = lax.broadcasted_iota(jnp.int32, (tok, 24), 1)
    tok12 = lax.broadcasted_iota(jnp.int32, (tok, 12), 0)
    row12 = lax.broadcasted_iota(jnp.int32, (tok, 12), 1)
    kind = lax.broadcasted_iota(jnp.int32, (tok, 128), 1).astype(F32)
    for w in range(n_win):
        pick = (tok12 // 24 + 6 * (w // 2) == row12).astype(F32)
        line = dot_nn(pick, ids)
        own_id = jnp.sum(
            jnp.where(spot == 12 * (w % 2) + (token % 24) // 2, line, 0.0), axis=1, keepdims=True
        )
        hot[w] = (own_id == kind).astype(BF16)

    f_below[...] = below_ref[576:1224, :].astype(F32).reshape(3, 9, 24, 128)
    f_right[...] = right_ref[576:1224, :].astype(F32).reshape(9, 9, 8, 128)
    f_corner[...] = corner_ref[192:408, :].astype(F32).reshape(3, 9, 8, 128)
    row8 = lax.broadcasted_iota(jnp.int32, (8, 128), 0)
    for h in range(12):
        for c in range(4):
            cols = slice(128 * c, 128 * c + 128)
            if h < 9:
                main = x_ref[48 * (h + 3):48 * (h + 3) + 48, cols]
                side = right_ref[16 * (9 * c + h):16 * (9 * c + h) + 16, :]
            else:
                main = below_ref[144 * c + 48 * (h - 9):144 * c + 48 * (h - 9) + 48, :]
                side = corner_ref[16 * (3 * c + h - 9):16 * (3 * c + h - 9) + 16, :]
            line = jnp.concatenate([main.astype(F32), side.astype(F32)], axis=0)
            turned = [pltpu.roll(line[8 * n:8 * n + 8], 4, 0) for n in range(1, 8)]
            piece = [jnp.where(row8 < 4, turned[n], turned[n + 1]) for n in range(6)]
            for b in range(2):
                xw32[(h // 6) * 2 + b, 24 * (h % 6):24 * (h % 6) + 24, cols] = jnp.concatenate(
                    piece[3 * b:3 * b + 3], axis=0
                )
    for w in range(n_win):
        xw[w] = xw32[w].astype(BF16)
    flat_x = xw[...].reshape(rows, 512)
    loads[0].wait()
    x_t[...] = flat_x.T
    for n in range(6):
        part = dot_nn(flat_x, wqkv_ref[:, 256 * n:256 * n + 256]).astype(BF16)
        pk[:, :, 256 * n:256 * n + 256] = part.reshape(n_win, tok, 256)

    def attend(w, carry):
        same = dot_nt(hot[w], hot[w])
        bias = (same - 1.0) * -MASKED
        for hp in range(4):
            cols = slice(128 * hp, 128 * hp + 128)
            q = pk[w, :, 128 * hp:128 * hp + 128]
            k = pk[w, :, 512 + 128 * hp:512 + 128 * hp + 128]
            v_t = pk[w, :, 1024 + 128 * hp:1024 + 128 * hp + 128].T
            outs = []
            both = dot_nt(jnp.concatenate([k * eighth[0], k * eighth[1]], axis=0), q)
            for e in range(2):
                s = both[tok * e:tok * e + tok] + bias
                p = jnp.exp(s - jnp.max(s, axis=0, keepdims=True))
                p = p * (1.0 / jnp.sum(p, axis=0, keepdims=True))
                probs[w, 2 * hp + e] = p
                outs.append(dot_nn(v_t[64 * e:64 * e + 64], p.astype(BF16)))
            o_t = jnp.concatenate(outs, axis=0).astype(BF16)
            at_t[w, cols, :] = o_t
            at[w, :, cols] = o_t.T
        return carry

    lax.fori_loop(0, n_win, attend, 0)

    flat_at = at[...].reshape(rows, 512)
    loads[1].wait()
    nrm[...] = dot_nn(flat_at, wproj_ref[...]).reshape(n_win, tok, 512)
    for w in range(n_win):
        for i in range(6):
            at_row = 48 * (6 * (w // 2) + i) + 24 * (w % 2)
            p = nrm[w, 24 * i:24 * i + 24, :]
            c = p - jnp.mean(p, axis=-1, keepdims=True)
            r = lax.rsqrt(jnp.mean(c * c, axis=-1, keepdims=True) + EPS)
            n = c * r
            nrm[w, 24 * i:24 * i + 24, :] = n
            inv[w, 24 * i:24 * i + 24, :] = jnp.broadcast_to(r, (24, 128))
            mix32[at_row:at_row + 24, :] = xw32[w, 24 * i:24 * i + 24, :] + n * gain
    mixb[...] = mix32[...].astype(BF16)

    mixed = mixb[...]
    for load in loads[2:]:
        load.wait()
    for hp in range(4):
        cols = slice(128 * hp, 128 * hp + 128)
        for w_ref, pair in ((wkey_ref, kk), (wval_ref, vv)):
            part = dot_nn(mixed, w_ref[:, cols]).astype(BF16)
            other = swap_rows(part.astype(F32))
            pair[hp, :, 0:128] = part
            pair[hp, :, 128:256] = (-other).astype(BF16)

    row16 = lax.broadcasted_iota(jnp.int32, (16, 128), 0)
    lane16 = lax.broadcasted_iota(jnp.int32, (16, 128), 1)
    own = (row16 // 2 == lane16 % 8).astype(F32)[None]
    zero64 = jnp.zeros((64, 128), BF16)
    for hp in range(4):
        cols = slice(128 * hp, 128 * hp + 128)
        q = qs[:, cols] * jnp.asarray(0.125, BF16)
        q_e, q_o = q * half[0], q * half[1]
        rhs = jnp.concatenate(
            [jnp.concatenate([q_e, q_e], axis=1), jnp.concatenate([q_o, q_o], axis=1)], axis=0
        )
        diff = dot_nt(kk[hp], rhs)
        wo = wo128[cols, :]
        top = jnp.concatenate(
            [jnp.concatenate([wo[:64], zero64], axis=0), jnp.concatenate([zero64, wo[64:]], axis=0)], axis=1
        )
        u = dot_nn(vv[hp], jnp.concatenate([top, top], axis=0)).astype(BF16)
        for e in range(2):
            d = diff[:, 128 * e:128 * e + 128].reshape(36, 16, 128)
            small = jnp.exp(-jnp.abs(d))
            big = 1.0 / (1.0 + small)
            small = small * big
            weight = jnp.where(d >= 0, big, small)
            ww[2 * hp + e] = (weight * own).astype(BF16).reshape(rows, 128)
            cc[2 * hp + e] = (small * big * (own * 0.125)).reshape(rows, 128)
            uu[2 * hp + e] = u[:, 128 * e:128 * e + 128]

    gg[...] = jnp.zeros((8, rows, 128), BF16)

    edge = lax.broadcasted_iota(jnp.int32, (13, 8, 80), 1) < 2

    def groups(h, tiles):
        turned = [pltpu.roll(tile, 2, 1) for tile in tiles]
        for o in range(3):
            g16 = pl.ds(pl.multiple_of(48 * h + 16 * o, 16), 16)
            f = jnp.where(edge, turned[o], turned[o + 1]).reshape(104, 80)
            f = jnp.concatenate([f, jnp.zeros((24, 80), F32)], axis=0).astype(BF16)
            dw = dot_nt(uu[:, g16, 0:80].reshape(128, 80), f)
            d = (dw * cc[:, g16, :].reshape(128, 128)).astype(BF16)
            ds[:, g16, :] = d.reshape(8, 16, 128)
            g = dot_nn(ww[:, g16, :].reshape(128, 128), f).astype(BF16)
            gg[:, g16, 0:80] = g.reshape(8, 16, 80)

    def near(h, carry):
        own = f_ref[h + 3].astype(F32)
        groups(h, [own[:, 0:8], own[:, 8:16], own[:, 16:24], all_levels(f_right[h])])
        return carry

    def far(h, carry):
        own = all_levels(f_below[h])
        groups(h + 9, [own[:, 0:8], own[:, 8:16], own[:, 16:24], all_levels(f_corner[h])])
        return carry

    lax.fori_loop(0, 9, near, 0, unroll=9)
    lax.fori_loop(0, 3, far, 0, unroll=3)

    fold_row = lax.broadcasted_iota(jnp.int32, (128, 128), 0)
    fold_lane = lax.broadcasted_iota(jnp.int32, (128, 128), 1)
    fold = (fold_row // 8 == fold_lane - 80).astype(BF16)
    for hp in range(4):
        cols = slice(128 * hp, 128 * hp + 128)
        q = qs[:, cols]
        d = jnp.concatenate([ds[2 * hp], ds[2 * hp + 1]], axis=1)
        g = jnp.concatenate([gg[2 * hp], gg[2 * hp + 1]], axis=1)
        dkd[:, cols] = dot_nn(d, jnp.concatenate([q * half[0], q * half[1]], axis=0)).astype(BF16)
        wo = wo128[cols, :]
        top = jnp.concatenate(
            [jnp.concatenate([wo[:64], zero64], axis=0), jnp.concatenate([zero64, wo[64:]], axis=0)], axis=1
        )
        dvd[:, cols] = dot_nt(g, top).astype(BF16)
        dq = dot_tn(kk[hp, :, 0:128], d)
        dq = jnp.concatenate([dq[:64, :128], dq[64:, 128:]], axis=0)
        go = dot_tn(vv[hp, :, 0:128], g)
        go = jnp.concatenate([go[:64, :128], go[64:, 128:]], axis=0)
        dq_hi = dq.astype(BF16)
        dq_lo = (dq - dq_hi.astype(F32)).astype(BF16)
        hs[:, cols] = go + dot_nn(dq_hi, fold) + dot_nn(dq_lo, fold)

    d_mix = dot_nt(dkd[...], wkey_ref[...]) + dot_nt(dvd[...], wval_ref[...])
    dm32[...] = d_mix.astype(BF16).astype(F32)
    mixed_t = mixed.T
    put(1, 4, dot_nn(mixed_t, dkd[...]))
    put(1, 8, dot_nn(mixed_t, dvd[...]))

    total_gain = jnp.zeros((8, 512), F32)
    for w in range(n_win):
        for i in range(6):
            at_row = 48 * (6 * (w // 2) + i) + 24 * (w % 2)
            g = dm32[at_row:at_row + 24, :]
            n = nrm[w, 24 * i:24 * i + 24, :]
            total_gain = total_gain + jnp.sum((g * n).reshape(3, 8, 512), axis=0)
            gn = g * gain
            m1 = jnp.mean(gn, axis=-1, keepdims=True)
            m2 = jnp.mean(gn * n, axis=-1, keepdims=True)
            r = inv[w, 24 * i:24 * i + 24, 0:1]
            dp32[w, 24 * i:24 * i + 24, :] = r * (gn - m1 - n * m2)
    row_gain = jnp.broadcast_to(jnp.sum(total_gain, axis=0, keepdims=True), (128, 512))
    for hp in range(4):
        cols = slice(128 * hp, 128 * hp + 128)
        column = row_gain[:, cols].T
        lanes = lax.broadcasted_iota(jnp.int32, (128, 128), 1)
        tail = jnp.where(lanes == 96, column, hs[:, cols]).astype(BF16)
        at_row = 6144 + 128 * (hp % 2)
        grads_ref[(hp // 2) ^ core, at_row:at_row + 128, :] = tail
    for half_no in range(2):
        grads_ref[half_no, 6400:6656, :] = jnp.zeros((256, 128), BF16)
    for w in range(n_win):
        dpb[w] = dp32[w].astype(BF16)
    flat_dp = dpb[...].reshape(rows, 512)
    total = dot_nn(at_t[0], dpb[0])
    for w in range(1, n_win):
        total = total + dot_nn(at_t[w], dpb[w])
    put(1, 0, total)
    dat[...] = dot_nt(flat_dp, wproj_ref[...]).astype(BF16).reshape(n_win, tok, 512)

    early_keep = pltpu.make_async_copy(grads_ref.at[0], keep_hbm, out_sem.at[0])
    early_send = pltpu.make_async_copy(grads_ref.at[1], send_hbm, out_sem.at[1])
    late_keep = pltpu.make_async_copy(grads_ref.at[0], keep_hbm, out_sem.at[2])
    late_send = pltpu.make_async_copy(grads_ref.at[1], send_hbm, out_sem.at[3])

    @pl.when(core == 1)
    def _():
        early_keep.start()

    @pl.when(core == 0)
    def _():
        early_send.start()

    def unattend(w, carry):
        for hp in range(4):
            cols = slice(128 * hp, 128 * hp + 128)
            q = pk[w, :, 128 * hp:128 * hp + 128]
            k_t = pk[w, :, 512 + 128 * hp:512 + 128 * hp + 128].T
            v = pk[w, :, 1024 + 128 * hp:1024 + 128 * hp + 128]
            da = dat[w, :, cols]
            both = dot_nt(jnp.concatenate([v * eighth[0], v * eighth[1]], axis=0), da)
            ps, ss, dqs = [], [], []
            for e in range(2):
                p = probs[w, 2 * hp + e]
                dw = both[tok * e:tok * e + tok]
                s = (p * (dw - jnp.sum(p * dw, axis=0, keepdims=True))).astype(BF16)
                ps.append(p.astype(BF16))
                ss.append(s)
                dqs.append(dot_nn(k_t[64 * e:64 * e + 64], s))
            dv = dot_nn(jnp.concatenate(ps, axis=0), da)
            dk = dot_nn(jnp.concatenate(ss, axis=0), q)
            dpk[w, :, cols] = jnp.concatenate(dqs, axis=0).astype(BF16).T
            dpk[w, :, 512 + 128 * hp:512 + 128 * hp + 128] = jnp.where(low, dk[:tok], dk[tok:]).astype(BF16)
            dpk[w, :, 1024 + 128 * hp:1024 + 128 * hp + 128] = jnp.where(low, dv[:tok], dv[tok:]).astype(BF16)
        return carry

    lax.fori_loop(0, n_win, unattend, 0)

    flat_d = dpk[...].reshape(rows, 1536)
    for n in range(3):
        put(0, 4 * n, dot_nn(x_t[...], flat_d[:, 512 * n:512 * n + 512]))

    @pl.when(core == 0)
    def _():
        late_keep.start()

    @pl.when(core == 1)
    def _():
        late_send.start()

    dp32[...] = dot_nt(flat_d, wqkv_ref[...]).reshape(n_win, tok, 512)
    for h in range(12):
        parts = []
        for b in range(2):
            at_row = 48 * h + 24 * b
            parts.append(
                dp32[(h // 6) * 2 + b, 24 * (h % 6):24 * (h % 6) + 24, :] + dm32[at_row:at_row + 24, :]
            )
        out_ref[48 * h:48 * h + 48, :] = jnp.concatenate(parts, axis=0).astype(BF16)
    result = pltpu.make_async_copy(out_ref, out_hbm, out_sem.at[4])
    result.start()

    @pl.when(core == 0)
    def _():
        early_send.wait()
        late_keep.wait()

    @pl.when(core == 1)
    def _():
        early_keep.wait()
        late_send.wait()

    result.wait()


def section(core, level_ids, x, fields, halo, ids, table, w_qkv, w_proj, gain, w_key, w_value, w_out):
    vm = lambda shape, kind: pltpu.VMEM(shape, kind)
    scratch = [
        vm((4, 144, 512), F32), vm((4, 144, 512), BF16), vm((4, 144, 1536), BF16), vm((4, 8, 144, 144), F32),
        vm((4, 144, 512), BF16), vm((4, 144, 512), F32), vm((4, 144, 128), F32), vm((576, 512), F32),
        vm((576, 512), BF16), vm((4, 576, 256), BF16), vm((4, 576, 256), BF16), vm((8, 576, 128), BF16),
        vm((8, 576, 128), BF16), vm((8, 576, 128), F32), vm((8, 576, 128), BF16), vm((8, 576, 128), BF16),
        vm((576, 512), BF16), vm((576, 512), BF16), vm((576, 512), F32), vm((4, 144, 512), F32),
        vm((4, 144, 512), BF16), vm((4, 144, 512), BF16), vm((4, 144, 1536), BF16), vm((128, 512), F32),
        vm((4, 512, 144), BF16), vm((512, 576), BF16), vm((4, 144, 128), BF16), vm((128, 512), F32),
        vm((128, 512), BF16), vm((512, 128), BF16), vm((3, 9, 24, 128), F32), vm((9, 9, 8, 128), F32),
        vm((3, 9, 8, 128), F32),
        vm((512, 1536), BF16), vm((512, 512), BF16), vm((512, 512), BF16), vm((512, 512), BF16),
        vm((12, 13, 24, 80), BF16), vm((576, 512), BF16), vm((2, 6656, 128), BF16),
        pltpu.SemaphoreType.DMA((5,)), pltpu.SemaphoreType.DMA((5,)),
    ]
    smem, vmem = pl.BlockSpec(memory_space=pltpu.SMEM), pl.BlockSpec(memory_space=pltpu.VMEM)
    hbm = pl.BlockSpec(memory_space=pl.ANY)
    half = jax.ShapeDtypeStruct((6656, 128), BF16)
    return pl.pallas_call(
        section_kernel,
        out_shape=(jax.ShapeDtypeStruct((576, 512), BF16), half, half),
        in_specs=[smem, smem] + [vmem] * 8 + [hbm] * 5,
        out_specs=[hbm] * 3,
        scratch_shapes=scratch,
        compiler_params=pltpu.CompilerParams(vmem_limit_bytes=58 * 1024 * 1024),
        cost_estimate=pl.CostEstimate(flops=15_000_000_000, bytes_accessed=12_000_000, transcendentals=2_000_000),
        name="section",
    )(core, level_ids, x, *halo, ids, table, gain[None], w_out, w_qkv, w_proj, w_key, w_value, fields)


from jax.sharding import Mesh, PartitionSpec as P

LAT = ("z_hi", "core")
LON = ("x", "y", "z_lo")
CHIPS = ("z_hi", "x", "y", "z_lo")


def neighbours(axes, by):
    count = 1
    for axis in axes:
        count *= lax.axis_size(axis)
    return [(i, (i + by) % count) for i in range(count)]


def corner_pairs(by):
    n_lat, n_lon = 4, 32
    return [
        (a * n_lon + b, ((a + by) % n_lat) * n_lon + (b + by) % n_lon) for a in range(n_lat) for b in range(n_lon)
    ]


def fetch(tokens, fields):
    below, right, corner = pack(tokens, fields)
    return (
        lax.ppermute(below, LAT, neighbours(LAT, -1)),
        lax.ppermute(right, LON, neighbours(LON, -1)),
        lax.ppermute(corner, LAT + LON, corner_pairs(-1)),
    )


def send_back(tile):
    h, w = tile.shape[0], tile.shape[1]
    above = lax.ppermute(tile[h - SH:, :w - SW], LAT, neighbours(LAT, 1))
    left = lax.ppermute(tile[:h - SH, w - SW:], LON, neighbours(LON, 1))
    corner = lax.ppermute(tile[h - SH:, w - SW:], LAT + LON, corner_pairs(1))
    return above, left, corner


def place_back(tile, above, left, corner):
    h, w = tile.shape[0], tile.shape[1]
    top = jnp.concatenate([corner, above], axis=1)
    bottom = jnp.concatenate([left, tile[:h - SH, :w - SW]], axis=1)
    return jnp.concatenate([top, bottom], axis=0)


def sum_all(keep, send, tile, sent):
    swap = [(0, 1), (1, 0)]
    other = lax.ppermute(send, "core", swap)
    mine = (keep.astype(F32) + other.astype(F32)).astype(BF16)
    pieces = lax.all_to_all(mine.reshape(64, 104, 128), CHIPS, split_axis=0, concat_axis=0, tiled=True)
    piece = jnp.sum(pieces.astype(F32), axis=0).astype(BF16)
    piece, sent = lax.optimization_barrier((piece, sent))
    spread = jnp.broadcast_to(piece[None], (64, 104, 128))
    mine = lax.all_to_all(spread, CHIPS, split_axis=0, concat_axis=0, tiled=True).reshape(6656, 128)
    mine, d_latent = lax.optimization_barrier((mine, place_back(tile, *sent)))
    other = lax.ppermute(mine, "core", swap)
    return mine, other, d_latent


def unpack_kernel(core_ref, level_ref, mine_ref, other_ref, qkv_ref, proj_ref, key_ref, value_ref, out_ref, gain_ref, table_ref, tail_ref):
    first = core_ref[0, 0] == 0

    def pick(half_no, at_row, count):
        mine, other = mine_ref[at_row:at_row + count, :], other_ref[at_row:at_row + count, :]
        chosen = jnp.where(first, mine, other) if half_no == 0 else jnp.where(first, other, mine)
        return chosen.astype(F32)

    for block in range(12):
        qkv_ref[:, 128 * block:128 * block + 128] = pick(0, 512 * block, 512)
    for n, ref in enumerate((proj_ref, key_ref, value_ref)):
        for c in range(4):
            ref[:, 128 * c:128 * c + 128] = pick(1, 512 * (4 * n + c), 512)
    for hp in range(4):
        tail_ref[:, 128 * hp:128 * hp + 128] = pick(hp // 2, 6144 + 128 * (hp % 2), 128).T
    out_ref[...] = tail_ref[0:80, :]
    gain_ref[...] = tail_ref[96:97, :]
    row = lax.broadcasted_iota(jnp.int32, (37, 512), 0)
    table = jnp.zeros((37, 512), F32)
    for p in range(13):
        table = table + jnp.where(row == level_ref[p], tail_ref[80 + p:81 + p, :], 0.0)
    table_ref[...] = table


def unpack(core, level_ids, mine, other):
    shape = lambda *dims: jax.ShapeDtypeStruct(dims, F32)
    smem, vmem = pl.BlockSpec(memory_space=pltpu.SMEM), pl.BlockSpec(memory_space=pltpu.VMEM)
    return pl.pallas_call(
        unpack_kernel,
        out_shape=(
            shape(512, 1536), shape(512, 512), shape(512, 512), shape(512, 512), shape(80, 512), shape(1, 512),
            shape(37, 512),
        ),
        in_specs=[smem, smem, vmem, vmem],
        out_specs=[vmem] * 7,
        scratch_shapes=[pltpu.VMEM((128, 512), F32)],
        compiler_params=pltpu.CompilerParams(vmem_limit_bytes=24 * 1024 * 1024),
        cost_estimate=pl.CostEstimate(flops=3_000_000, bytes_accessed=10_000_000, transcendentals=0),
        name="unpack",
    )(core, level_ids, mine, other)


def shards(
    latent, grad_fields, region_ids, level_ids, w_qkv, w_proj, gain, level_table, w_key, w_value, w_out
):
    core = lax.axis_index("core")
    tokens = latent.reshape(576, 512)
    fields = grad_fields.transpose(0, 2, 1, 3)
    out, keep, send = section(
        core.reshape(1, 1), level_ids, tokens, fields, fetch(tokens, fields), region_ids, level_table, w_qkv, w_proj,
        gain, w_key, w_value, w_out.T,
    )
    tile = out.reshape(12, 24, 2, 512)
    mine, other, d_latent = sum_all(keep, send, tile, send_back(tile))
    grad_qkv, grad_proj, grad_key, grad_value, out_t, grad_gain, table = unpack(core.reshape(1, 1), level_ids, mine, other)
    return d_latent, grad_qkv, grad_proj, grad_gain[0], table, grad_key, grad_value, out_t.T


def solution(mesh):
    fine = Mesh(mesh.devices.reshape(2, 2, 4, 4, 2), LAT + LON)
    tile = P(LAT, LON, None, None)
    return jax.shard_map(
        shards,
        mesh=fine,
        in_specs=(tile, tile, P(LAT, LON)) + (P(),) * 8,
        out_specs=(tile,) + (P(),) * 7,
        check_vma=False,
    )
```

time: 164 us -> 133 us (0.81)
  blocking collectives: 57.6 us -> 0 us
  waiting for transfers between devices: 14.4 us -> 55.6 us
  local copies, waits for them, and re-layouts: 24.3 us -> 4.93 us
  starting transfers between devices: 20.4 us -> 37.3 us
  other arithmetic: 13.3 us -> 5 us
  Pallas kernels: 33 us -> 28.7 us
    all_to_all x2 -> x0, blocking collectives: 57.6 us -> none  [the longest x1 29.5 us: sum_all(): lax.all_to_all(spread, CHIPS, split_axis=0, concat_axis=0, tiled=True)]
    all_to_all x0 -> x2, waiting for transfers between devices: none -> 38.3 us  [the longest x1 20.5 us: sum_all(): lax.all_to_all(spread, CHIPS, split_axis=0, concat_axis=0, tiled=True)]
    all_to_all x0 -> x2, starting transfers between devices: none -> 17.4 us  [the longest x1 10.4 us: sum_all(): lax.all_to_all(mine.reshape(64, 104, 128), CHIPS, split_axis=0, concat_ax...]
    slice x14 -> x1, local copies, waits for them, and re-layouts: 9.65 us -> 0.23 us  [place_back(): bottom = jnp.concatenate([left, tile[:h - SH, :w - SW]], axis=1)]
    pallas_call x1, Pallas kernels: 33 us -> 24.8 us  [section(): pl.pallas_call(section_kernel, out_shape=(jax.ShapeDtypeStruct((576, 512)...]
    pallas_call x0 -> x2, Pallas kernels: none -> 3.97 us  [the longest x1 3.78 us: unpack(): pl.pallas_call(unpack_kernel, out_shape=(shape(512, 1536), shape(512, 512...]
    unnamed x19 -> x14, local copies, waits for them, and re-layouts: 4.58 us -> 0.83 us
    convert_element_type x7 -> x1, other arithmetic: 6.35 us -> 3.08 us  [sum_all(): mine = (keep.astype(F32) + other.astype(F32)).astype(BF16)]
  transfers between devices with their start and end apart: 11 -> 10, of which waited for: 3 -> 7; matrix products, arithmetic and copies ran while one was open for 9% -> 2% of each run, Pallas kernels for 0% -> 0%
where the time goes in v1:
time: 133 us; the launch traced here: 132 us
  waiting for transfers between devices  55.6 us (42%)
  starting transfers between devices  37.3 us (28%)
  Pallas kernels  28.7 us (22%)
  other arithmetic  5 us (4%)
  local copies, waits for them, and re-layouts  4.93 us (4%)
    pallas_call x1, Pallas kernels, section(): pl.pallas_call(section_kernel, out_shape=(jax.ShapeDtypeStruct((576, 512)...  24.8 us
    all_to_all x1, waiting for transfers between devices, sum_all(): lax.all_to_all(spread, CHIPS, split_axis=0, concat_axis=0, tiled=True)  20.5 us
    all_to_all x1, waiting for transfers between devices, sum_all(): lax.all_to_all(mine.reshape(64, 104, 128), CHIPS, split_axis=0, concat_ax...  17.8 us
    all_to_all x1, starting transfers between devices, sum_all(): lax.all_to_all(mine.reshape(64, 104, 128), CHIPS, split_axis=0, concat_ax...  10.4 us
    all_to_all x1, starting transfers between devices, sum_all(): lax.all_to_all(spread, CHIPS, split_axis=0, concat_axis=0, tiled=True)  7.05 us
    ppermute x1, starting transfers between devices, fetch(): lax.ppermute(right, LON, neighbours(LON, -1))  6.37 us
    ppermute x1, waiting for transfers between devices, send_back(): corner = lax.ppermute(tile[h - SH:, w - SW:], LAT + LON, corner_pairs(1))  4.21 us
    pallas_call x1, Pallas kernels, unpack(): pl.pallas_call(unpack_kernel, out_shape=(shape(512, 1536), shape(512, 512...  3.78 us
  transfers between devices with their start and end apart: 10, of which 7 were waited for; matrix products, arithmetic and copies ran while one was open for 2% of the time, Pallas kernels for 0%

profile of v1, /device:TPU:1, one launch (start us, length us, event | category | flops | bytes accessed | tf_op | source)
XLA Modules:
  0.0 132.3 jit_solution(16371589400737798852)
XLA Ops:
  0.6 0.0 copy-start.1
  0.6 2.1 %reshape.34.x_ref = bf16[576,512]{1,0:T(8,128)(2,1)S(1)} reshape(bf16[12,24,2,512]{3,2,1,0:T(2,128)(2,1)} %param.11) | data formatting | bytes 1179648 | tf_op jit(solution)/shard_map/reshape | solution.py:558
  2.7 0.0 copy-start
  2.7 0.0 copy-done.1
  2.7 0.2 pack.1
  2.9 1.5 %collective-permute-start = (bf16[1224,128]{1,0:T(8,128)(2,1)S(1)}, bf16[1224,128]{1,0:T(8,128)(2,1)S(1)}, u32[]{:S(2)}, u32[]{:S(2)}) collective-permute-start(bf16[1224,128]{1,0:T(8,128)(2,1)S(1)} %get-tuple-element.27), channel_id=1, source_target_pairs={{0,96},{32,0},{64,32},{96,64},{1,97},{33,1},{65,33},{97,65},{2,98}... | collective-permute-start | bytes 940040 | tf_op jit(solution)/shard_map/ppermute | solution.py:477
  4.4 6.4 %collective-permute-start.1 = (bf16[1224,128]{1,0:T(8,128)(2,1)S(1)}, bf16[1224,128]{1,0:T(8,128)(2,1)S(1)}, u32[]{:S(2)}, u32[]{:S(2)}) collective-permute-start(bf16[1224,128]{1,0:T(8,128)(2,1)S(1)} %get-tuple-element.28), channel_id=1, source_target_pairs={{0,31},{1,0},{2,1},{3,2},{4,3},{5,4},{6,5},{7,6},{8,7},{9,8},{10,9... | collective-permute-start | bytes 940040 | tf_op jit(solution)/shard_map/ppermute | solution.py:478
  10.8 3.3 %collective-permute-start.2 = (bf16[408,128]{1,0:T(8,128)(2,1)S(1)}, bf16[408,128]{1,0:T(8,128)(2,1)S(1)}, u32[]{:S(2)}, u32[]{:S(2)}) collective-permute-start(bf16[408,128]{1,0:T(8,128)(2,1)S(1)} %get-tuple-element.29), channel_id=1, source_target_pairs={{0,127},{1,96},{2,97},{3,98},{4,99},{5,100},{6,101},{7,102},{8,103... | collective-permute-start | bytes 313352 | tf_op jit(solution)/shard_map/ppermute | solution.py:479
  14.1 3.2 %collective-permute-done.2.corner_ref = bf16[408,128]{1,0:T(8,128)(2,1)S(1)} collective-permute-done((bf16[408,128]{1,0:T(8,128)(2,1)S(1)}, bf16[408,128]{1,0:T(8,128)(2,1)S(1)}, u32[]{:S(2)}, u32[]{:S(2)}) %collective-permute-start.2) | collective-permute-done | bytes 104480 | tf_op jit(solution)/shard_map/ppermute | solution.py:479
  17.3 0.0 copy-start.6
  17.3 3.1 %collective-permute-done.below_ref = bf16[1224,128]{1,0:T(8,128)(2,1)S(1)} collective-permute-done((bf16[1224,128]{1,0:T(8,128)(2,1)S(1)}, bf16[1224,128]{1,0:T(8,128)(2,1)S(1)}, u32[]{:S(2)}, u32[]{:S(2)}) %collective-permute-start) | collective-permute-done | bytes 313376 | tf_op jit(solution)/shard_map/ppermute | solution.py:477
  20.4 0.0 copy-start.4
  20.4 0.0 collective-permute-done.1.right_ref
  20.4 0.0 copy-start.5
  20.4 0.0 copy-done
  20.4 0.0 copy-done.6
  20.4 0.7 copy-done.4
  21.1 0.1 copy-done.5
  21.2 24.8 %section.1 = (bf16[576,512]{1,0:T(8,128)(2,1)}, bf16[6656,128]{1,0:T(8,128)(2,1)}, bf16[6656,128]{1,0:T(8,128)(2,1)}) custom-call(s32[1,1]{1,0:T(1,128)} %bitcast.core_ref, s32[13]{0:T(128)} %level_ref.3, bf16[576,512]{1,0:T(8,128)(2,1)} %copy-done, bf16[1224,128]{1,0:T(8,128)(2,1)} %copy-done.4, bf16[1224,128]{1,0:T(8,128)(2,1)} %copy-done.5, ...), custom_call_target="tpu_custom_call" | custom-call | flops 15000000512 | bytes 12000000 | tf_op jit(solution)/shard_map/section/pallas_call | solution.py:441
  46.0 0.6 collective-permute-start.3
  46.6 3.6 %collective-permute-done.3 = bf16[6656,128]{1,0:T(8,128)(2,1)S(1)} collective-permute-done((bf16[6656,128]{1,0:T(8,128)(2,1)}, bf16[6656,128]{1,0:T(8,128)(2,1)S(1)}, u32[]{:S(2)}, u32[]{:S(2)}) %collective-permute-start.3) | collective-permute-done | bytes 1703968 | tf_op jit(solution)/shard_map/ppermute | solution.py:500
  50.1 3.1 %add_convert_fusion = bf16[6656,128]{1,0:T(8,128)(2,1)} fusion(bf16[6656,128]{1,0:T(8,128)(2,1)S(1)} %collective-permute-done.3, bf16[6656,128]{1,0:T(8,128)(2,1)} %get-tuple-element.30), kind=kLoop, calls=%fused_computation | loop fusion | flops 3407872 | bytes 5111808 | tf_op jit(solution)/shard_map/convert_element_type | solution.py:501
  53.2 0.0 copy-start.3
  53.2 10.4 %all-to-all-start = ((bf16[64,104,128]{2,1,0:T(8,128)(2,1)}), bf16[64,104,128]{2,1,0:T(8,128)(2,1)S(1)}, u32[]{:S(2)}, u32[]{:S(2)}) async-start(bf16[64,104,128]{2,1,0:T(8,128)(2,1)} %bitcast.4), calls=%async_computation | async-start | bytes 3407872 | tf_op jit(solution)/shard_map/all_to_all | solution.py:502
  63.6 0.0 copy-done.3
  63.6 0.2 reshape.36
  63.8 0.1 slice.17
  63.9 0.1 slice.16
  64.0 3.5 %collective-permute-start.4 = (bf16[3,18,2,512]{3,2,1,0:T(2,128)(2,1)S(1)}, bf16[3,18,2,512]{3,2,1,0:T(2,128)(2,1)S(1)}, u32[]{:S(2)}, u32[]{:S(2)}) collective-permute-start(bf16[3,18,2,512]{3,2,1,0:T(2,128)(2,1)S(1)} %slice.16), channel_id=1, source_target_pairs={{0,32},{32,64},{64,96},{96,0},{1,33},{33,65},{65,97},{97,1},{2,34}... | collective-permute-start | bytes 331784 | tf_op jit(solution)/shard_map/ppermute | solution.py:485
  67.5 0.3 collective-permute-start.5
  67.8 1.3 %collective-permute-start.6 = (bf16[3,6,2,512]{3,2,1,0:T(2,128)(2,1)S(1)}, bf16[3,6,2,512]{3,2,1,0:T(2,128)(2,1)S(1)}, u32[]{:S(2)}, u32[]{:S(2)}) collective-permute-start(bf16[3,6,2,512]{3,2,1,0:T(2,128)(2,1)S(1)} %slice.18), channel_id=1, source_target_pairs={{0,33},{1,34},{2,35},{3,36},{4,37},{5,38},{6,39},{7,40},{8,41},{9,... | collective-permute-start | bytes 110600 | tf_op jit(solution)/shard_map/ppermute | solution.py:487
  69.2 17.8 %all-to-all-done = bf16[64,104,128]{2,1,0:T(8,128)(2,1)S(1)} async-done(((bf16[64,104,128]{2,1,0:T(8,128)(2,1)}), bf16[64,104,128]{2,1,0:T(8,128)(2,1)S(1)}, u32[]{:S(2)}, u32[]{:S(2)}) %all-to-all-start) | async-done | bytes 1703968 | tf_op jit(solution)/shard_map/all_to_all | solution.py:502
  87.0 0.3 reduce_sum.12
  87.2 4.2 %collective-permute-done.6 = bf16[3,6,2,512]{3,2,1,0:T(2,128)(2,1)S(1)} collective-permute-done((bf16[3,6,2,512]{3,2,1,0:T(2,128)(2,1)S(1)}, bf16[3,6,2,512]{3,2,1,0:T(2,128)(2,1)S(1)}, u32[]{:S(2)}, u32[]{:S(2)}) %collective-permute-start.6) | collective-permute-done | bytes 36896 | tf_op jit(solution)/shard_map/ppermute | solution.py:487
  91.4 0.0 collective-permute-done.4
  91.4 0.0 collective-permute-done.5
  91.4 1.4 %broadcast_in_dim.10 = bf16[64,104,128]{2,1,0:T(8,128)(2,1)} broadcast(bf16[104,128]{1,0:T(8,128)(2,1)S(1)} %reduce_sum.12), dimensions={1,2} | broadcast | bytes 1730560 | tf_op jit(solution)/shard_map/broadcast_in_dim | solution.py:505
  92.8 7.0 %all-to-all-start.1 = ((bf16[64,104,128]{2,1,0:T(8,128)(2,1)}), bf16[64,104,128]{2,1,0:T(8,128)(2,1)S(1)}, u32[]{:S(2)}, u32[]{:S(2)}) async-start(bf16[64,104,128]{2,1,0:T(8,128)(2,1)} %broadcast_in_dim.10), calls=%async_computation.1 | async-start | bytes 3407872 | tf_op jit(solution)/shard_map/all_to_all | solution.py:506
  99.9 0.0 copy-start.2
  99.9 0.2 slice.19
  100.1 1.7 %maximum_maximum_fusion = bf16[12,24,2,512]{3,2,1,0:T(2,128)(2,1)} fusion(bf16[9,18,2,512]{3,2,1,0:T(2,128)(2,1)S(1)} %slice.19, bf16[9,6,2,512]{3,2,1,0:T(2,128)(2,1)S(1)} %collective-permute-done.5, bf16[3,18,2,512]{3,2,1,0:T(2,128)(2,1)S(1)} %collective-permute-done.4, bf16[3,6,2,512]{3,2,1,0:T(2,128)(2,1)S(1)} %collective-permute-done.6), kind=kLoop, calls=%fused_computation.1 | loop fusion | flops 884736 | bytes 1179648 | tf_op jit(solution)/shard_map/concatenate | solution.py:495
  101.8 20.5 %all-to-all-done.1 = bf16[64,104,128]{2,1,0:T(8,128)(2,1)S(1)} async-done(((bf16[64,104,128]{2,1,0:T(8,128)(2,1)}), bf16[64,104,128]{2,1,0:T(8,128)(2,1)S(1)}, u32[]{:S(2)}, u32[]{:S(2)}) %all-to-all-start.1) | async-done | bytes 1703968 | tf_op jit(solution)/shard_map/all_to_all | solution.py:506
  122.3 3.0 %collective-permute-start.7 = (bf16[6656,128]{1,0:T(8,128)(2,1)S(1)}, bf16[6656,128]{1,0:T(8,128)(2,1)S(1)}, u32[]{:S(2)}, u32[]{:S(2)}) collective-permute-start(bf16[6656,128]{1,0:T(8,128)(2,1)S(1)} %bitcast.8), channel_id=1, source_target_pairs={{0,32},{32,0},{1,33},{33,1},{2,34},{34,2},{3,35},{35,3},{4,36},{36... | collective-permute-start | bytes 5111816 | tf_op jit(solution)/shard_map/ppermute | solution.py:508
  125.3 3.2 %collective-permute-done.7.other_ref = bf16[6656,128]{1,0:T(8,128)(2,1)S(1)} collective-permute-done((bf16[6656,128]{1,0:T(8,128)(2,1)S(1)}, bf16[6656,128]{1,0:T(8,128)(2,1)S(1)}, u32[]{:S(2)}, u32[]{:S(2)}) %collective-permute-start.7) | collective-permute-done | bytes 1703968 | tf_op jit(solution)/shard_map/ppermute | solution.py:508
  128.5 0.0 copy-done.2
  128.5 3.8 %unpack.1 = (f32[512,1536]{1,0:T(8,128)}, f32[512,512]{1,0:T(8,128)}, f32[512,512]{1,0:T(8,128)}, f32[512,512]{1,0:T(8,128)}, f32[80,512]{1,0:T(8,128)}, /*index=5*/f32[1,512]{1,0:T(1,128)}, f32[37,512]{1,0:T(8,128)}) custom-call(s32[1,1]{1,0:T(1,128)} %bitcast.core_ref, s32[13]{0:T(128)S(1)} %copy-done.2, bf16[6656,128]{1,0:T(8,128)(2,1)S(1)} %bitcast.9, ...), custom_call_target="tpu_custom_call" | custom-call | flops 3000000 | bytes 10000000 | tf_op jit(solution)/shard_map/unpack/pallas_call | solution.py:539
  (1 shorter events, 0.0 us)
Async XLA Ops:
  0.6 2.1 %copy-start.1 = (bf16[12,24,13,80]{3,1,2,0:T(8,128)(2,1)S(1)}, bf16[12,24,13,80]{3,1,2,0:T(8,128)(2,1)}, u32[]{:S(2)}) copy-start(bf16[12,24,13,80]{3,1,2,0:T(8,128)(2,1)} %param.12) | copy-start | bytes 1797124
  2.7 17.7 %copy-start = (bf16[576,512]{1,0:T(8,128)(2,1)}, bf16[576,512]{1,0:T(8,128)(2,1)S(1)}, u32[]{:S(2)}) copy-start(bf16[576,512]{1,0:T(8,128)(2,1)S(1)} %reshape.34.x_ref) | copy-start | bytes 1769476
  2.9 17.5 %collective-permute-start = (bf16[1224,128]{1,0:T(8,128)(2,1)S(1)}, bf16[1224,128]{1,0:T(8,128)(2,1)S(1)}, u32[]{:S(2)}, u32[]{:S(2)}) collective-permute-start(bf16[1224,128]{1,0:T(8,128)(2,1)S(1)} %get-tuple-element.27), channel_id=1, source_target_pairs={{0,96},{32,0},{64,32},{96,64},{1,97},{33,1},{65,33},{97,65},{2,98}... | collective-permute-start | bytes 940040 | tf_op jit(solution)/shard_map/ppermute | solution.py:477
  4.4 16.0 %collective-permute-start.1 = (bf16[1224,128]{1,0:T(8,128)(2,1)S(1)}, bf16[1224,128]{1,0:T(8,128)(2,1)S(1)}, u32[]{:S(2)}, u32[]{:S(2)}) collective-permute-start(bf16[1224,128]{1,0:T(8,128)(2,1)S(1)} %get-tuple-element.28), channel_id=1, source_target_pairs={{0,31},{1,0},{2,1},{3,2},{4,3},{5,4},{6,5},{7,6},{8,7},{9,8},{10,9... | collective-permute-start | bytes 940040 | tf_op jit(solution)/shard_map/ppermute | solution.py:478
  10.8 6.5 %collective-permute-start.2 = (bf16[408,128]{1,0:T(8,128)(2,1)S(1)}, bf16[408,128]{1,0:T(8,128)(2,1)S(1)}, u32[]{:S(2)}, u32[]{:S(2)}) collective-permute-start(bf16[408,128]{1,0:T(8,128)(2,1)S(1)} %get-tuple-element.29), channel_id=1, source_target_pairs={{0,127},{1,96},{2,97},{3,98},{4,99},{5,100},{6,101},{7,102},{8,103... | collective-permute-start | bytes 313352 | tf_op jit(solution)/shard_map/ppermute | solution.py:479
  17.3 3.1 %copy-start.6 = (bf16[408,128]{1,0:T(8,128)(2,1)}, bf16[408,128]{1,0:T(8,128)(2,1)S(1)}, u32[]{:S(2)}) copy-start(bf16[408,128]{1,0:T(8,128)(2,1)S(1)} %collective-permute-done.2.corner_ref) | copy-start | bytes 313348
  20.4 0.7 copy-start.4
  20.4 0.8 copy-start.5
  46.0 4.1 %collective-permute-start.3 = (bf16[6656,128]{1,0:T(8,128)(2,1)}, bf16[6656,128]{1,0:T(8,128)(2,1)S(1)}, u32[]{:S(2)}, u32[]{:S(2)}) collective-permute-start(bf16[6656,128]{1,0:T(8,128)(2,1)} %get-tuple-element.31), channel_id=1, source_target_pairs={{0,32},{32,0},{1,33},{33,1},{2,34},{34,2},{3,35},{35,3},{4,36},{36... | collective-permute-start | bytes 5111816 | tf_op jit(solution)/shard_map/ppermute | solution.py:500
  53.2 10.4 %copy-start.3 = (bf16[576,512]{1,0:T(8,128)(2,1)S(1)}, bf16[576,512]{1,0:T(8,128)(2,1)}, u32[]{:S(2)}) copy-start(bf16[576,512]{1,0:T(8,128)(2,1)} %get-tuple-element.32) | copy-start | bytes 1769476
  53.2 33.7 %all-to-all-start = ((bf16[64,104,128]{2,1,0:T(8,128)(2,1)}), bf16[64,104,128]{2,1,0:T(8,128)(2,1)S(1)}, u32[]{:S(2)}, u32[]{:S(2)}) async-start(bf16[64,104,128]{2,1,0:T(8,128)(2,1)} %bitcast.4), calls=%async_computation | async-start | bytes 3407872 | tf_op jit(solution)/shard_map/all_to_all | solution.py:502
  64.0 27.4 %collective-permute-start.4 = (bf16[3,18,2,512]{3,2,1,0:T(2,128)(2,1)S(1)}, bf16[3,18,2,512]{3,2,1,0:T(2,128)(2,1)S(1)}, u32[]{:S(2)}, u32[]{:S(2)}) collective-permute-start(bf16[3,18,2,512]{3,2,1,0:T(2,128)(2,1)S(1)} %slice.16), channel_id=1, source_target_pairs={{0,32},{32,64},{64,96},{96,0},{1,33},{33,65},{65,97},{97,1},{2,34}... | collective-permute-start | bytes 331784 | tf_op jit(solution)/shard_map/ppermute | solution.py:485
  67.5 23.9 %collective-permute-start.5 = (bf16[9,6,2,512]{3,2,1,0:T(2,128)(2,1)S(1)}, bf16[9,6,2,512]{3,2,1,0:T(2,128)(2,1)S(1)}, u32[]{:S(2)}, u32[]{:S(2)}) collective-permute-start(bf16[9,6,2,512]{3,2,1,0:T(2,128)(2,1)S(1)} %slice.17), channel_id=1, source_target_pairs={{0,1},{1,2},{2,3},{3,4},{4,5},{5,6},{6,7},{7,8},{8,9},{9,10},{10,1... | collective-permute-start | bytes 331784 | tf_op jit(solution)/shard_map/ppermute | solution.py:486
  67.8 23.6 %collective-permute-start.6 = (bf16[3,6,2,512]{3,2,1,0:T(2,128)(2,1)S(1)}, bf16[3,6,2,512]{3,2,1,0:T(2,128)(2,1)S(1)}, u32[]{:S(2)}, u32[]{:S(2)}) collective-permute-start(bf16[3,6,2,512]{3,2,1,0:T(2,128)(2,1)S(1)} %slice.18), channel_id=1, source_target_pairs={{0,33},{1,34},{2,35},{3,36},{4,37},{5,38},{6,39},{7,40},{8,41},{9,... | collective-permute-start | bytes 110600 | tf_op jit(solution)/shard_map/ppermute | solution.py:487
  92.8 29.4 %all-to-all-start.1 = ((bf16[64,104,128]{2,1,0:T(8,128)(2,1)}), bf16[64,104,128]{2,1,0:T(8,128)(2,1)S(1)}, u32[]{:S(2)}, u32[]{:S(2)}) async-start(bf16[64,104,128]{2,1,0:T(8,128)(2,1)} %broadcast_in_dim.10), calls=%async_computation.1 | async-start | bytes 3407872 | tf_op jit(solution)/shard_map/all_to_all | solution.py:506
  99.9 28.6 %copy-start.2 = (s32[13]{0:T(128)S(1)}, s32[13]{0:T(128)}, u32[]{:S(2)}) copy-start(s32[13]{0:T(128)} %level_ref.3) | copy-start | bytes 160
  122.3 6.2 %collective-permute-start.7 = (bf16[6656,128]{1,0:T(8,128)(2,1)S(1)}, bf16[6656,128]{1,0:T(8,128)(2,1)S(1)}, u32[]{:S(2)}, u32[]{:S(2)}) collective-permute-start(bf16[6656,128]{1,0:T(8,128)(2,1)S(1)} %bitcast.8), channel_id=1, source_target_pairs={{0,32},{32,0},{1,33},{33,1},{2,34},{34,2},{3,35},{35,3},{4,36},{36... | collective-permute-start | bytes 5111816 | tf_op jit(solution)/shard_map/ppermute | solution.py:508

commit v2 on v1

--- a/solution.py
+++ b/solution.py
@@ -58,30 +58,68 @@
     return jnp.stack(levels, axis=0)[:, :, :80]
 
 
+def row_of_tile():
+    return lax.broadcasted_iota(jnp.int32, (8, 128), 0)
+
+
+def side_tiles(line, levels):
+    row = row_of_tile()
+    tiles = [line[0:8, 128 * c:128 * c + 128] for c in range(4)]
+    for m in range(2):
+        left, right = (line[8:16, 128 * c:128 * c + 128] for c in (2 * m, 2 * m + 1))
+        tiles.append(jnp.where(row < 4, left, pltpu.roll(right, 4, 0)))
+    places = []
+    for m in range(2):
+        for i in range(3):
+            places.append(jnp.where(row < 6, levels[4 * m + i], pltpu.roll(levels[4 * m + 3], 6 - 2 * i, 0)))
+    return tiles, places + [levels[8]]
+
+
+def side_levels(places):
+    row = row_of_tile()
+    out = []
+    for m in range(2):
+        first, second, third = places[3 * m:3 * m + 3]
+        last = jnp.where(
+            row < 2, pltpu.roll(first, 2, 0), jnp.where(row < 4, pltpu.roll(second, 4, 0), pltpu.roll(third, 6, 0))
+        )
+        out += [first, second, third, last]
+    return jnp.stack(out + [places[6]], axis=0)
+
+
 def pack_kernel(x_ref, f_ref, below_ref, right_ref, corner_ref, wide):
-    for c in range(4):
-        cols = slice(128 * c, 128 * c + 128)
-        below_ref[144 * c:144 * c + 144, :] = x_ref[0:144, cols]
-        for h in range(3):
-            corner_ref[16 * (3 * c + h):16 * (3 * c + h) + 16, :] = x_ref[48 * h:48 * h + 16, cols]
-        for h in range(9):
-            right_ref[16 * (9 * c + h):16 * (9 * c + h) + 16, :] = x_ref[48 * (h + 3):48 * (h + 3) + 16, cols]
-    lines, sides = [], []
+    row = row_of_tile()
+    full, halves, lines, sides = [], [], [], ([], [])
     for h in range(12):
         wide[h, :, :, 0:80] = f_ref[h].astype(F32)
+        line = x_ref[48 * h:48 * h + 48, :].astype(F32)
+        tiles, places = side_tiles(line[0:16], nine_tiles(wide[h, :, 0:8, :]))
+        sides[0].append(tiles)
+        sides[1].append(places)
         if h < 3:
-            lines.append(nine_tiles(wide[h]).reshape(216, 128))
-        sides.append(nine_tiles(wide[h, :, 0:8, :]).reshape(72, 128))
-    below_ref[576:1224, :] = jnp.concatenate(lines, axis=0).astype(BF16)
-    right_ref[576:1224, :] = jnp.concatenate(sides[3:], axis=0).astype(BF16)
-    corner_ref[192:408, :] = jnp.concatenate(sides[:3], axis=0).astype(BF16)
+            for c in range(4):
+                full += [line[8 * n:8 * n + 8, 128 * c:128 * c + 128] for n in range(2, 6)]
+            for m in range(2):
+                left, right = (line[8:16, 128 * c:128 * c + 128] for c in (2 * m, 2 * m + 1))
+                halves.append(jnp.where(row < 4, pltpu.roll(right, 4, 0), left))
+            levels = nine_tiles(wide[h])
+            for k in range(9):
+                lines += [levels[k, 8:16], levels[k, 16:24]]
+            for q in range(2):
+                four = [pltpu.roll(levels[4 * q + i, 0:8], (8 - 2 * i) % 8, 0) for i in range(4)]
+                low = jnp.where(row < 2, four[3], four[2])
+                lines.append(jnp.where(row < 4, low, jnp.where(row < 6, four[1], four[0])))
+            lines.append(levels[8, 0:8])
+    below_ref[...] = jnp.concatenate(full + halves + lines, axis=0).astype(BF16)
+    right_ref[...] = jnp.concatenate(sum(sides[0][3:], []) + sum(sides[1][3:], []), axis=0).astype(BF16)
+    corner_ref[...] = jnp.concatenate(sum(sides[0][:3], []) + sum(sides[1][:3], []), axis=0).astype(BF16)
 
 
 def pack(x, fields):
     vmem = pl.BlockSpec(memory_space=pltpu.VMEM)
     return pl.pallas_call(
         pack_kernel,
-        out_shape=tuple(jax.ShapeDtypeStruct((rows, 128), BF16) for rows in (1224, 1224, 408)),
+        out_shape=tuple(jax.ShapeDtypeStruct((rows, 128), BF16) for rows in (936, 936, 312)),
         in_specs=[vmem, vmem],
         out_specs=[vmem] * 3,
         scratch_shapes=[pltpu.VMEM((12, 13, 24, 128), F32)],
@@ -151,21 +189,33 @@
         )
         hot[w] = (own_id == kind).astype(BF16)
 
-    f_below[...] = below_ref[576:1224, :].astype(F32).reshape(3, 9, 24, 128)
-    f_right[...] = right_ref[576:1224, :].astype(F32).reshape(9, 9, 8, 128)
-    f_corner[...] = corner_ref[192:408, :].astype(F32).reshape(3, 9, 8, 128)
-    row8 = lax.broadcasted_iota(jnp.int32, (8, 128), 0)
+    row8 = row_of_tile()
+    below = below_ref[...].astype(F32).reshape(117, 8, 128)
+    right = right_ref[...].astype(F32).reshape(117, 8, 128)
+    corner = corner_ref[...].astype(F32).reshape(39, 8, 128)
+    for h in range(9):
+        f_right[h] = side_levels([right[54 + 7 * h + n] for n in range(7)])
+    for h in range(3):
+        f_corner[h] = side_levels([corner[18 + 7 * h + n] for n in range(7)])
+        for k in range(9):
+            at_tile = 54 + 21 * h
+            f_below[h, k, 0:8, :] = pltpu.roll(below[at_tile + 18 + k // 4], 2 * (k % 4), 0)
+            f_below[h, k, 8:16, :] = below[at_tile + 2 * k]
+            f_below[h, k, 16:24, :] = below[at_tile + 2 * k + 1]
     for h in range(12):
+        side = right[6 * h:6 * h + 6] if h < 9 else corner[6 * (h - 9):6 * (h - 9) + 6]
         for c in range(4):
             cols = slice(128 * c, 128 * c + 128)
             if h < 9:
-                main = x_ref[48 * (h + 3):48 * (h + 3) + 48, cols]
-                side = right_ref[16 * (9 * c + h):16 * (9 * c + h) + 16, :]
+                main = x_ref[48 * (h + 3):48 * (h + 3) + 48, cols].astype(F32)
+                line = [main[8 * n:8 * n + 8] for n in range(1, 6)]
             else:
-                main = below_ref[144 * c + 48 * (h - 9):144 * c + 48 * (h - 9) + 48, :]
-                side = corner_ref[16 * (3 * c + h - 9):16 * (3 * c + h - 9) + 16, :]
-            line = jnp.concatenate([main.astype(F32), side.astype(F32)], axis=0)
-            turned = [pltpu.roll(line[8 * n:8 * n + 8], 4, 0) for n in range(1, 8)]
+                half_tile = below[48 + 2 * (h - 9) + c // 2]
+                line = [half_tile if c % 2 == 0 else pltpu.roll(half_tile, 4, 0)]
+                line += [below[16 * (h - 9) + 4 * c + n] for n in range(4)]
+            half_tile = side[4 + c // 2]
+            line += [side[c], half_tile if c % 2 == 0 else pltpu.roll(half_tile, 4, 0)]
+            turned = [pltpu.roll(tile, 4, 0) for tile in line]
             piece = [jnp.where(row8 < 4, turned[n], turned[n + 1]) for n in range(6)]
             for b in range(2):
                 xw32[(h // 6) * 2 + b, 24 * (h % 6):24 * (h % 6) + 24, cols] = jnp.concatenate(
@@ -509,21 +559,48 @@
     return mine, other, d_latent
 
 
-def unpack_kernel(core_ref, level_ref, mine_ref, other_ref, qkv_ref, proj_ref, key_ref, value_ref, out_ref, gain_ref, table_ref, tail_ref):
+def spread_half(is_first, half_ref, targets, stage, sem):
+    qkv_hbm, squares = targets[0], targets[1:]
+
+    def copies(n, act):
+        cols = slice(512 * n, 512 * n + 512)
+
+        @pl.when(is_first)
+        def _():
+            act(pltpu.make_async_copy(stage.at[:, cols], qkv_hbm.at[:, cols], sem.at[n]))
+
+        @pl.when(jnp.logical_not(is_first))
+        def _():
+            act(pltpu.make_async_copy(stage.at[:, cols], squares[n], sem.at[n]))
+
+    for n in range(3):
+        for block in range(4 * n, 4 * n + 4):
+            stage[:, 128 * block:128 * block + 128] = half_ref[512 * block:512 * block + 512, :].astype(F32)
+        copies(n, lambda copy: copy.start())
+    return lambda: [copies(n, lambda copy: copy.wait()) for n in range(3)]
+
+
+def unpack_mine_kernel(core_ref, mine_ref, qkv_hbm, proj_hbm, key_hbm, value_hbm, stage, sem):
+    finish = spread_half(core_ref[0, 0] == 0, mine_ref, (qkv_hbm, proj_hbm, key_hbm, value_hbm), stage, sem)
+    finish()
+
+
+def unpack_other_kernel(
+    core_ref, level_ref, mine_hbm, other_ref, qkv_in, proj_in, key_in, value_in,
+    qkv_hbm, proj_hbm, key_hbm, value_hbm, out_ref, gain_ref, table_ref, stage, tail_ref, mine_ref, sem, mine_sem,
+):
     first = core_ref[0, 0] == 0
-
-    def pick(half_no, at_row, count):
-        mine, other = mine_ref[at_row:at_row + count, :], other_ref[at_row:at_row + count, :]
-        chosen = jnp.where(first, mine, other) if half_no == 0 else jnp.where(first, other, mine)
-        return chosen.astype(F32)
-
-    for block in range(12):
-        qkv_ref[:, 128 * block:128 * block + 128] = pick(0, 512 * block, 512)
-    for n, ref in enumerate((proj_ref, key_ref, value_ref)):
-        for c in range(4):
-            ref[:, 128 * c:128 * c + 128] = pick(1, 512 * (4 * n + c), 512)
+    fetch_tail = pltpu.make_async_copy(mine_hbm.at[6144:6400], mine_ref, mine_sem)
+    fetch_tail.start()
+    finish = spread_half(
+        jnp.logical_not(first), other_ref, (qkv_hbm, proj_hbm, key_hbm, value_hbm), stage, sem
+    )
+    fetch_tail.wait()
     for hp in range(4):
-        tail_ref[:, 128 * hp:128 * hp + 128] = pick(hp // 2, 6144 + 128 * (hp % 2), 128).T
+        at_row = 128 * (hp % 2)
+        mine, other = mine_ref[at_row:at_row + 128, :], other_ref[6144 + at_row:6144 + at_row + 128, :]
+        chosen = jnp.where(first, mine, other) if hp < 2 else jnp.where(first, other, mine)
+        tail_ref[:, 128 * hp:128 * hp + 128] = chosen.astype(F32).T
     out_ref[...] = tail_ref[0:80, :]
     gain_ref[...] = tail_ref[96:97, :]
     row = lax.broadcasted_iota(jnp.int32, (37, 512), 0)
@@ -531,24 +608,40 @@
     for p in range(13):
         table = table + jnp.where(row == level_ref[p], tail_ref[80 + p:81 + p, :], 0.0)
     table_ref[...] = table
+    finish()
 
 
 def unpack(core, level_ids, mine, other):
     shape = lambda *dims: jax.ShapeDtypeStruct(dims, F32)
     smem, vmem = pl.BlockSpec(memory_space=pltpu.SMEM), pl.BlockSpec(memory_space=pltpu.VMEM)
+    hbm = pl.BlockSpec(memory_space=pl.ANY)
+    matrices = (shape(512, 1536), shape(512, 512), shape(512, 512), shape(512, 512))
+    cost = pl.CostEstimate(flops=3_000_000, bytes_accessed=6_000_000, transcendentals=0)
+    params = pltpu.CompilerParams(vmem_limit_bytes=24 * 1024 * 1024)
+    sem, stage = pltpu.SemaphoreType.DMA((3,)), pltpu.VMEM((512, 1536), F32)
+    halves = pl.pallas_call(
+        unpack_mine_kernel,
+        out_shape=matrices,
+        in_specs=[smem, vmem],
+        out_specs=[hbm] * 4,
+        scratch_shapes=[stage, sem],
+        compiler_params=params,
+        cost_estimate=cost,
+        name="unpack_mine",
+    )(core, mine)
     return pl.pallas_call(
-        unpack_kernel,
-        out_shape=(
-            shape(512, 1536), shape(512, 512), shape(512, 512), shape(512, 512), shape(80, 512), shape(1, 512),
-            shape(37, 512),
-        ),
-        in_specs=[smem, smem, vmem, vmem],
-        out_specs=[vmem] * 7,
-        scratch_shapes=[pltpu.VMEM((128, 512), F32)],
-        compiler_params=pltpu.CompilerParams(vmem_limit_bytes=24 * 1024 * 1024),
-        cost_estimate=pl.CostEstimate(flops=3_000_000, bytes_accessed=10_000_000, transcendentals=0),
-        name="unpack",
-    )(core, level_ids, mine, other)
+        unpack_other_kernel,
+        out_shape=matrices + (shape(80, 512), shape(1, 512), shape(37, 512)),
+        in_specs=[smem, smem, hbm, vmem] + [hbm] * 4,
+        out_specs=[hbm] * 4 + [vmem] * 3,
+        scratch_shapes=[
+            stage, pltpu.VMEM((128, 512), F32), pltpu.VMEM((256, 128), BF16), sem, pltpu.SemaphoreType.DMA,
+        ],
+        input_output_aliases={4: 0, 5: 1, 6: 2, 7: 3},
+        compiler_params=params,
+        cost_estimate=cost,
+        name="unpack_other",
+    )(core, level_ids, mine, other, *halves)
 
 
 def shards(

time: 133 us -> 130 us (0.977)
  waiting for transfers between devices: 55.6 us -> 51 us
    ppermute x1, waiting for transfers between devices: 3.22 us -> 1.4 us  [sum_all(): other = lax.ppermute(mine, 'core', swap)]
    ppermute x1, waiting for transfers between devices: 3.12 us -> 1.55 us  [fetch(): lax.ppermute(below, LAT, neighbours(LAT, -1))]
    pallas_call x1 -> x2, Pallas kernels: 3.78 us -> 4.97 us  [the longest x1 3.15 us: unpack(): pl.pallas_call(unpack_other_kernel, out_shape=matrices + (shape(80, 512),...]
  transfers between devices with their start and end apart: 10 -> 10, of which waited for: 7 -> 7; matrix products, arithmetic and copies ran while one was open for 2% -> 2% of each run, Pallas kernels for 0% -> 1%
where the time goes in v2:
time: 130 us
  waiting for transfers between devices  51 us (39%)
  starting transfers between devices  37.9 us (29%)
  Pallas kernels  29.9 us (23%)
  other arithmetic  5 us (4%)
  local copies, waits for them, and re-layouts  4.88 us (4%)
    pallas_call x1, Pallas kernels, section(): pl.pallas_call(section_kernel, out_shape=(jax.ShapeDtypeStruct((576, 512)...  24.7 us
    all_to_all x1, waiting for transfers between devices, sum_all(): lax.all_to_all(spread, CHIPS, split_axis=0, concat_axis=0, tiled=True)  20.5 us
    all_to_all x1, waiting for transfers between devices, sum_all(): lax.all_to_all(mine.reshape(64, 104, 128), CHIPS, split_axis=0, concat_ax...  17.8 us
    all_to_all x1, starting transfers between devices, sum_all(): lax.all_to_all(mine.reshape(64, 104, 128), CHIPS, split_axis=0, concat_ax...  10.2 us
    all_to_all x1, starting transfers between devices, sum_all(): lax.all_to_all(spread, CHIPS, split_axis=0, concat_axis=0, tiled=True)  7.05 us
    ppermute x1, starting transfers between devices, fetch(): lax.ppermute(right, LON, neighbours(LON, -1))  6.37 us
    ppermute x1, waiting for transfers between devices, send_back(): corner = lax.ppermute(tile[h - SH:, w - SW:], LAT + LON, corner_pairs(1))  4.21 us
    ppermute x1, starting transfers between devices, send_back(): above = lax.ppermute(tile[h - SH:, :w - SW], LAT, neighbours(LAT, 1))  3.5 us
  transfers between devices with their start and end apart: 10, of which 7 were waited for; matrix products, arithmetic and copies ran while one was open for 2% of the time, Pallas kernels for 1%

profile of v2, /device:TPU:1, one launch (start us, length us, event | category | flops | bytes accessed | tf_op | source)
XLA Modules:
  0.0 129.6 jit_solution(9389377700370565952)
XLA Ops:
  0.6 0.0 copy-start.1
  0.6 2.1 %reshape.34.x_ref = bf16[576,512]{1,0:T(8,128)(2,1)S(1)} reshape(bf16[12,24,2,512]{3,2,1,0:T(2,128)(2,1)} %param.11) | data formatting | bytes 1179648 | tf_op jit(solution)/shard_map/reshape | solution.py:651
  2.7 0.0 copy-start
  2.7 0.0 copy-done.1
  2.7 0.2 pack.1
  2.9 1.5 %collective-permute-start = (bf16[936,128]{1,0:T(8,128)(2,1)S(1)}, bf16[936,128]{1,0:T(8,128)(2,1)S(1)}, u32[]{:S(2)}, u32[]{:S(2)}) collective-permute-start(bf16[936,128]{1,0:T(8,128)(2,1)S(1)} %get-tuple-element.31), channel_id=1, source_target_pairs={{0,96},{32,0},{64,32},{96,64},{1,97},{33,1},{65,33},{97,65},{2,98}... | collective-permute-start | bytes 718856 | tf_op jit(solution)/shard_map/ppermute | solution.py:527
  4.4 6.4 %collective-permute-start.1 = (bf16[936,128]{1,0:T(8,128)(2,1)S(1)}, bf16[936,128]{1,0:T(8,128)(2,1)S(1)}, u32[]{:S(2)}, u32[]{:S(2)}) collective-permute-start(bf16[936,128]{1,0:T(8,128)(2,1)S(1)} %get-tuple-element.32), channel_id=1, source_target_pairs={{0,31},{1,0},{2,1},{3,2},{4,3},{5,4},{6,5},{7,6},{8,7},{9,8},{10,9... | collective-permute-start | bytes 718856 | tf_op jit(solution)/shard_map/ppermute | solution.py:528
  10.8 3.3 %collective-permute-start.2 = (bf16[312,128]{1,0:T(8,128)(2,1)S(1)}, bf16[312,128]{1,0:T(8,128)(2,1)S(1)}, u32[]{:S(2)}, u32[]{:S(2)}) collective-permute-start(bf16[312,128]{1,0:T(8,128)(2,1)S(1)} %get-tuple-element.33), channel_id=1, source_target_pairs={{0,127},{1,96},{2,97},{3,98},{4,99},{5,100},{6,101},{7,102},{8,103... | collective-permute-start | bytes 239624 | tf_op jit(solution)/shard_map/ppermute | solution.py:529
  14.1 2.1 %collective-permute-done.2.corner_ref = bf16[312,128]{1,0:T(8,128)(2,1)S(1)} collective-permute-done((bf16[312,128]{1,0:T(8,128)(2,1)S(1)}, bf16[312,128]{1,0:T(8,128)(2,1)S(1)}, u32[]{:S(2)}, u32[]{:S(2)}) %collective-permute-start.2) | collective-permute-done | bytes 79904 | tf_op jit(solution)/shard_map/ppermute | solution.py:529
  16.2 0.0 copy-start.6
  16.2 1.6 %collective-permute-done.below_ref = bf16[936,128]{1,0:T(8,128)(2,1)S(1)} collective-permute-done((bf16[936,128]{1,0:T(8,128)(2,1)S(1)}, bf16[936,128]{1,0:T(8,128)(2,1)S(1)}, u32[]{:S(2)}, u32[]{:S(2)}) %collective-permute-start) | collective-permute-done | bytes 239648 | tf_op jit(solution)/shard_map/ppermute | solution.py:527
  17.8 0.0 copy-start.4
  17.8 0.0 collective-permute-done.1.right_ref
  17.8 0.0 copy-start.5
  17.8 0.0 copy-done
  17.8 0.0 copy-done.6
  17.8 0.7 copy-done.4
  18.5 0.1 copy-done.5
  18.6 24.7 %section.1 = (bf16[576,512]{1,0:T(8,128)(2,1)}, bf16[6656,128]{1,0:T(8,128)(2,1)}, bf16[6656,128]{1,0:T(8,128)(2,1)}) custom-call(s32[1,1]{1,0:T(1,128)} %bitcast.core_ref, s32[13]{0:T(128)} %level_ref.3, bf16[576,512]{1,0:T(8,128)(2,1)} %copy-done, bf16[936,128]{1,0:T(8,128)(2,1)} %copy-done.4, bf16[936,128]{1,0:T(8,128)(2,1)} %copy-done.5, ...), custom_call_target="tpu_custom_call" | custom-call | flops 15000000512 | bytes 12000000 | tf_op jit(solution)/shard_map/section/pallas_call | solution.py:491
  43.3 1.4 %collective-permute-start.3 = (bf16[6656,128]{1,0:T(8,128)(2,1)}, bf16[6656,128]{1,0:T(8,128)(2,1)S(1)}, u32[]{:S(2)}, u32[]{:S(2)}) collective-permute-start(bf16[6656,128]{1,0:T(8,128)(2,1)} %get-tuple-element.35), channel_id=1, source_target_pairs={{0,32},{32,0},{1,33},{33,1},{2,34},{34,2},{3,35},{35,3},{4,36},{36... | collective-permute-start | bytes 5111816 | tf_op jit(solution)/shard_map/ppermute | solution.py:550
  44.7 3.4 %collective-permute-done.3 = bf16[6656,128]{1,0:T(8,128)(2,1)S(1)} collective-permute-done((bf16[6656,128]{1,0:T(8,128)(2,1)}, bf16[6656,128]{1,0:T(8,128)(2,1)S(1)}, u32[]{:S(2)}, u32[]{:S(2)}) %collective-permute-start.3) | collective-permute-done | bytes 1703968 | tf_op jit(solution)/shard_map/ppermute | solution.py:550
  48.1 3.1 %add_convert_fusion = bf16[6656,128]{1,0:T(8,128)(2,1)} fusion(bf16[6656,128]{1,0:T(8,128)(2,1)S(1)} %collective-permute-done.3, bf16[6656,128]{1,0:T(8,128)(2,1)} %get-tuple-element.34), kind=kLoop, calls=%fused_computation | loop fusion | flops 3407872 | bytes 5111808 | tf_op jit(solution)/shard_map/convert_element_type | solution.py:551
  51.2 0.0 copy-start.3
  51.2 10.2 %all-to-all-start = ((bf16[64,104,128]{2,1,0:T(8,128)(2,1)}), bf16[64,104,128]{2,1,0:T(8,128)(2,1)S(1)}, u32[]{:S(2)}, u32[]{:S(2)}) async-start(bf16[64,104,128]{2,1,0:T(8,128)(2,1)} %bitcast.4), calls=%async_computation | async-start | bytes 3407872 | tf_op jit(solution)/shard_map/all_to_all | solution.py:552
  61.4 0.0 copy-done.3
  61.4 0.2 reshape.36
  61.6 0.1 slice.17
  61.7 0.1 slice.16
  61.8 3.5 %collective-permute-start.4 = (bf16[3,18,2,512]{3,2,1,0:T(2,128)(2,1)S(1)}, bf16[3,18,2,512]{3,2,1,0:T(2,128)(2,1)S(1)}, u32[]{:S(2)}, u32[]{:S(2)}) collective-permute-start(bf16[3,18,2,512]{3,2,1,0:T(2,128)(2,1)S(1)} %slice.16), channel_id=1, source_target_pairs={{0,32},{32,64},{64,96},{96,0},{1,33},{33,65},{65,97},{97,1},{2,34}... | collective-permute-start | bytes 331784 | tf_op jit(solution)/shard_map/ppermute | solution.py:535
  65.3 0.3 collective-permute-start.5
  65.6 1.3 %collective-permute-start.6 = (bf16[3,6,2,512]{3,2,1,0:T(2,128)(2,1)S(1)}, bf16[3,6,2,512]{3,2,1,0:T(2,128)(2,1)S(1)}, u32[]{:S(2)}, u32[]{:S(2)}) collective-permute-start(bf16[3,6,2,512]{3,2,1,0:T(2,128)(2,1)S(1)} %slice.18), channel_id=1, source_target_pairs={{0,33},{1,34},{2,35},{3,36},{4,37},{5,38},{6,39},{7,40},{8,41},{9,... | collective-permute-start | bytes 110600 | tf_op jit(solution)/shard_map/ppermute | solution.py:537
  66.9 17.8 %all-to-all-done = bf16[64,104,128]{2,1,0:T(8,128)(2,1)S(1)} async-done(((bf16[64,104,128]{2,1,0:T(8,128)(2,1)}), bf16[64,104,128]{2,1,0:T(8,128)(2,1)S(1)}, u32[]{:S(2)}, u32[]{:S(2)}) %all-to-all-start) | async-done | bytes 1703968 | tf_op jit(solution)/shard_map/all_to_all | solution.py:552
  84.7 0.3 reduce_sum.12
  85.0 4.2 %collective-permute-done.6 = bf16[3,6,2,512]{3,2,1,0:T(2,128)(2,1)S(1)} collective-permute-done((bf16[3,6,2,512]{3,2,1,0:T(2,128)(2,1)S(1)}, bf16[3,6,2,512]{3,2,1,0:T(2,128)(2,1)S(1)}, u32[]{:S(2)}, u32[]{:S(2)}) %collective-permute-start.6) | collective-permute-done | bytes 36896 | tf_op jit(solution)/shard_map/ppermute | solution.py:537
  89.2 0.0 collective-permute-done.4
  89.2 0.0 collective-permute-done.5
  89.2 1.4 %broadcast_in_dim.10 = bf16[64,104,128]{2,1,0:T(8,128)(2,1)} broadcast(bf16[104,128]{1,0:T(8,128)(2,1)S(1)} %reduce_sum.12), dimensions={1,2} | broadcast | bytes 1730560 | tf_op jit(solution)/shard_map/broadcast_in_dim | solution.py:555
  90.6 7.0 %all-to-all-start.1 = ((bf16[64,104,128]{2,1,0:T(8,128)(2,1)}), bf16[64,104,128]{2,1,0:T(8,128)(2,1)S(1)}, u32[]{:S(2)}, u32[]{:S(2)}) async-start(bf16[64,104,128]{2,1,0:T(8,128)(2,1)} %broadcast_in_dim.10), calls=%async_computation.1 | async-start | bytes 3407872 | tf_op jit(solution)/shard_map/all_to_all | solution.py:556
  97.7 0.0 copy-start.2
  97.7 0.2 slice.19
  97.9 1.7 %maximum_maximum_fusion = bf16[12,24,2,512]{3,2,1,0:T(2,128)(2,1)} fusion(bf16[9,18,2,512]{3,2,1,0:T(2,128)(2,1)S(1)} %slice.19, bf16[9,6,2,512]{3,2,1,0:T(2,128)(2,1)S(1)} %collective-permute-done.5, bf16[3,18,2,512]{3,2,1,0:T(2,128)(2,1)S(1)} %collective-permute-done.4, bf16[3,6,2,512]{3,2,1,0:T(2,128)(2,1)S(1)} %collective-permute-done.6), kind=kLoop, calls=%fused_computation.1 | loop fusion | flops 884736 | bytes 1179648 | tf_op jit(solution)/shard_map/concatenate | solution.py:545
  99.6 20.5 %all-to-all-done.1 = bf16[64,104,128]{2,1,0:T(8,128)(2,1)S(1)} async-done(((bf16[64,104,128]{2,1,0:T(8,128)(2,1)}), bf16[64,104,128]{2,1,0:T(8,128)(2,1)S(1)}, u32[]{:S(2)}, u32[]{:S(2)}) %all-to-all-start.1) | async-done | bytes 1703968 | tf_op jit(solution)/shard_map/all_to_all | solution.py:556
  120.0 3.0 %collective-permute-start.7 = (bf16[6656,128]{1,0:T(8,128)(2,1)S(1)}, bf16[6656,128]{1,0:T(8,128)(2,1)S(1)}, u32[]{:S(2)}, u32[]{:S(2)}) collective-permute-start(bf16[6656,128]{1,0:T(8,128)(2,1)S(1)} %bitcast.8), channel_id=1, source_target_pairs={{0,32},{32,0},{1,33},{33,1},{2,34},{34,2},{3,35},{35,3},{4,36},{36... | collective-permute-start | bytes 5111816 | tf_op jit(solution)/shard_map/ppermute | solution.py:558
  123.0 1.8 %unpack_mine.1 = (f32[512,1536]{1,0:T(8,128)}, f32[512,512]{1,0:T(8,128)}, f32[512,512]{1,0:T(8,128)}, f32[512,512]{1,0:T(8,128)}) custom-call(s32[1,1]{1,0:T(1,128)} %bitcast.core_ref, bf16[6656,128]{1,0:T(8,128)(2,1)S(1)} %bitcast.9), custom_call_target="tpu_custom_call" | custom-call | flops 3000000 | bytes 6000000 | tf_op jit(solution)/shard_map/unpack_mine/pallas_call | solution.py:622
  124.9 1.4 %collective-permute-done.7.other_ref = bf16[6656,128]{1,0:T(8,128)(2,1)S(1)} collective-permute-done((bf16[6656,128]{1,0:T(8,128)(2,1)S(1)}, bf16[6656,128]{1,0:T(8,128)(2,1)S(1)}, u32[]{:S(2)}, u32[]{:S(2)}) %collective-permute-start.7) | collective-permute-done | bytes 1703968 | tf_op jit(solution)/shard_map/ppermute | solution.py:558
  126.3 0.0 copy-done.2
  126.3 3.1 %unpack_other.1 = (f32[512,1536]{1,0:T(8,128)}, f32[512,512]{1,0:T(8,128)}, f32[512,512]{1,0:T(8,128)}, f32[512,512]{1,0:T(8,128)}, f32[80,512]{1,0:T(8,128)}, /*index=5*/f32[1,512]{1,0:T(1,128)}, f32[37,512]{1,0:T(8,128)}) custom-call(s32[1,1]{1,0:T(1,128)} %bitcast.core_ref, ...), custom_call_target="tpu_custom_call", output_to_operand_aliasing={{0}: (4, {}), {1}: (5, {}), {2}: (6, {}), {3}: (7, {})} | custom-call | flops 3000000 | bytes 6000000 | tf_op jit(solution)/shard_map/unpack_other/pallas_call | solution.py:632
  (1 shorter events, 0.0 us)
Async XLA Ops:
  0.6 2.1 %copy-start.1 = (bf16[12,24,13,80]{3,1,2,0:T(8,128)(2,1)S(1)}, bf16[12,24,13,80]{3,1,2,0:T(8,128)(2,1)}, u32[]{:S(2)}) copy-start(bf16[12,24,13,80]{3,1,2,0:T(8,128)(2,1)} %param.12) | copy-start | bytes 1797124
  2.7 15.1 %copy-start = (bf16[576,512]{1,0:T(8,128)(2,1)}, bf16[576,512]{1,0:T(8,128)(2,1)S(1)}, u32[]{:S(2)}) copy-start(bf16[576,512]{1,0:T(8,128)(2,1)S(1)} %reshape.34.x_ref) | copy-start | bytes 1769476
  2.9 14.9 %collective-permute-start = (bf16[936,128]{1,0:T(8,128)(2,1)S(1)}, bf16[936,128]{1,0:T(8,128)(2,1)S(1)}, u32[]{:S(2)}, u32[]{:S(2)}) collective-permute-start(bf16[936,128]{1,0:T(8,128)(2,1)S(1)} %get-tuple-element.31), channel_id=1, source_target_pairs={{0,96},{32,0},{64,32},{96,64},{1,97},{33,1},{65,33},{97,65},{2,98}... | collective-permute-start | bytes 718856 | tf_op jit(solution)/shard_map/ppermute | solution.py:527
  4.4 13.4 %collective-permute-start.1 = (bf16[936,128]{1,0:T(8,128)(2,1)S(1)}, bf16[936,128]{1,0:T(8,128)(2,1)S(1)}, u32[]{:S(2)}, u32[]{:S(2)}) collective-permute-start(bf16[936,128]{1,0:T(8,128)(2,1)S(1)} %get-tuple-element.32), channel_id=1, source_target_pairs={{0,31},{1,0},{2,1},{3,2},{4,3},{5,4},{6,5},{7,6},{8,7},{9,8},{10,9... | collective-permute-start | bytes 718856 | tf_op jit(solution)/shard_map/ppermute | solution.py:528
  10.8 5.4 %collective-permute-start.2 = (bf16[312,128]{1,0:T(8,128)(2,1)S(1)}, bf16[312,128]{1,0:T(8,128)(2,1)S(1)}, u32[]{:S(2)}, u32[]{:S(2)}) collective-permute-start(bf16[312,128]{1,0:T(8,128)(2,1)S(1)} %get-tuple-element.33), channel_id=1, source_target_pairs={{0,127},{1,96},{2,97},{3,98},{4,99},{5,100},{6,101},{7,102},{8,103... | collective-permute-start | bytes 239624 | tf_op jit(solution)/shard_map/ppermute | solution.py:529
  16.2 1.6 %copy-start.6 = (bf16[312,128]{1,0:T(8,128)(2,1)}, bf16[312,128]{1,0:T(8,128)(2,1)S(1)}, u32[]{:S(2)}) copy-start(bf16[312,128]{1,0:T(8,128)(2,1)S(1)} %collective-permute-done.2.corner_ref) | copy-start | bytes 239620
  17.8 0.7 copy-start.4
  17.8 0.8 copy-start.5
  43.3 4.8 %collective-permute-start.3 = (bf16[6656,128]{1,0:T(8,128)(2,1)}, bf16[6656,128]{1,0:T(8,128)(2,1)S(1)}, u32[]{:S(2)}, u32[]{:S(2)}) collective-permute-start(bf16[6656,128]{1,0:T(8,128)(2,1)} %get-tuple-element.35), channel_id=1, source_target_pairs={{0,32},{32,0},{1,33},{33,1},{2,34},{34,2},{3,35},{35,3},{4,36},{36... | collective-permute-start | bytes 5111816 | tf_op jit(solution)/shard_map/ppermute | solution.py:550
  51.2 10.2 %copy-start.3 = (bf16[576,512]{1,0:T(8,128)(2,1)S(1)}, bf16[576,512]{1,0:T(8,128)(2,1)}, u32[]{:S(2)}) copy-start(bf16[576,512]{1,0:T(8,128)(2,1)} %get-tuple-element.36) | copy-start | bytes 1769476
  51.2 33.5 %all-to-all-start = ((bf16[64,104,128]{2,1,0:T(8,128)(2,1)}), bf16[64,104,128]{2,1,0:T(8,128)(2,1)S(1)}, u32[]{:S(2)}, u32[]{:S(2)}) async-start(bf16[64,104,128]{2,1,0:T(8,128)(2,1)} %bitcast.4), calls=%async_computation | async-start | bytes 3407872 | tf_op jit(solution)/shard_map/all_to_all | solution.py:552
  61.8 27.4 %collective-permute-start.4 = (bf16[3,18,2,512]{3,2,1,0:T(2,128)(2,1)S(1)}, bf16[3,18,2,512]{3,2,1,0:T(2,128)(2,1)S(1)}, u32[]{:S(2)}, u32[]{:S(2)}) collective-permute-start(bf16[3,18,2,512]{3,2,1,0:T(2,128)(2,1)S(1)} %slice.16), channel_id=1, source_target_pairs={{0,32},{32,64},{64,96},{96,0},{1,33},{33,65},{65,97},{97,1},{2,34}... | collective-permute-start | bytes 331784 | tf_op jit(solution)/shard_map/ppermute | solution.py:535
  65.3 23.9 %collective-permute-start.5 = (bf16[9,6,2,512]{3,2,1,0:T(2,128)(2,1)S(1)}, bf16[9,6,2,512]{3,2,1,0:T(2,128)(2,1)S(1)}, u32[]{:S(2)}, u32[]{:S(2)}) collective-permute-start(bf16[9,6,2,512]{3,2,1,0:T(2,128)(2,1)S(1)} %slice.17), channel_id=1, source_target_pairs={{0,1},{1,2},{2,3},{3,4},{4,5},{5,6},{6,7},{7,8},{8,9},{9,10},{10,1... | collective-permute-start | bytes 331784 | tf_op jit(solution)/shard_map/ppermute | solution.py:536
  65.6 23.6 %collective-permute-start.6 = (bf16[3,6,2,512]{3,2,1,0:T(2,128)(2,1)S(1)}, bf16[3,6,2,512]{3,2,1,0:T(2,128)(2,1)S(1)}, u32[]{:S(2)}, u32[]{:S(2)}) collective-permute-start(bf16[3,6,2,512]{3,2,1,0:T(2,128)(2,1)S(1)} %slice.18), channel_id=1, source_target_pairs={{0,33},{1,34},{2,35},{3,36},{4,37},{5,38},{6,39},{7,40},{8,41},{9,... | collective-permute-start | bytes 110600 | tf_op jit(solution)/shard_map/ppermute | solution.py:537
  90.6 29.4 %all-to-all-start.1 = ((bf16[64,104,128]{2,1,0:T(8,128)(2,1)}), bf16[64,104,128]{2,1,0:T(8,128)(2,1)S(1)}, u32[]{:S(2)}, u32[]{:S(2)}) async-start(bf16[64,104,128]{2,1,0:T(8,128)(2,1)} %broadcast_in_dim.10), calls=%async_computation.1 | async-start | bytes 3407872 | tf_op jit(solution)/shard_map/all_to_all | solution.py:556
  97.7 28.6 %copy-start.2 = (s32[13]{0:T(128)S(1)}, s32[13]{0:T(128)}, u32[]{:S(2)}) copy-start(s32[13]{0:T(128)} %level_ref.3) | copy-start | bytes 160
  120.0 6.2 %collective-permute-start.7 = (bf16[6656,128]{1,0:T(8,128)(2,1)S(1)}, bf16[6656,128]{1,0:T(8,128)(2,1)S(1)}, u32[]{:S(2)}, u32[]{:S(2)}) collective-permute-start(bf16[6656,128]{1,0:T(8,128)(2,1)S(1)} %bitcast.8), channel_id=1, source_target_pairs={{0,32},{32,0},{1,33},{33,1},{2,34},{34,2},{3,35},{35,3},{4,36},{36... | collective-permute-start | bytes 5111816 | tf_op jit(solution)/shard_map/ppermute | solution.py:558

commit v3 on v2

--- a/solution.py
+++ b/solution.py
@@ -494,7 +494,7 @@
         in_specs=[smem, smem] + [vmem] * 8 + [hbm] * 5,
         out_specs=[hbm] * 3,
         scratch_shapes=scratch,
-        compiler_params=pltpu.CompilerParams(vmem_limit_bytes=58 * 1024 * 1024),
+        compiler_params=pltpu.CompilerParams(vmem_limit_bytes=52 * 1024 * 1024),
         cost_estimate=pl.CostEstimate(flops=15_000_000_000, bytes_accessed=12_000_000, transcendentals=2_000_000),
         name="section",
     )(core, level_ids, x, *halo, ids, table, gain[None], w_out, w_qkv, w_proj, w_key, w_value, fields)
@@ -551,7 +551,6 @@
     mine = (keep.astype(F32) + other.astype(F32)).astype(BF16)
     pieces = lax.all_to_all(mine.reshape(64, 104, 128), CHIPS, split_axis=0, concat_axis=0, tiled=True)
     piece = jnp.sum(pieces.astype(F32), axis=0).astype(BF16)
-    piece, sent = lax.optimization_barrier((piece, sent))
     spread = jnp.broadcast_to(piece[None], (64, 104, 128))
     mine = lax.all_to_all(spread, CHIPS, split_axis=0, concat_axis=0, tiled=True).reshape(6656, 128)
     mine, d_latent = lax.optimization_barrier((mine, place_back(tile, *sent)))

time: 130 us -> 128 us (0.985)
  blocking collectives: 0 us -> 33.2 us
  waiting for transfers between devices: 51 us -> 29.1 us
  starting transfers between devices: 37.9 us -> 26.4 us
    all_to_all x0 -> x1, blocking collectives: none -> 33.2 us  [sum_all(): lax.all_to_all(mine.reshape(64, 104, 128), CHIPS, split_axis=0, concat_ax...]
    all_to_all x1, waiting for transfers between devices: 20.5 us -> 0.01 us  [sum_all(): lax.all_to_all(spread, CHIPS, split_axis=0, concat_axis=0, tiled=True)]
    all_to_all x1 -> x0, waiting for transfers between devices: 17.8 us -> none  [sum_all(): lax.all_to_all(mine.reshape(64, 104, 128), CHIPS, split_axis=0, concat_ax...]
    ppermute x1, waiting for transfers between devices: 4.21 us -> 20.5 us  [send_back(): corner = lax.ppermute(tile[h - SH:, w - SW:], LAT + LON, corner_pairs(1))]
    all_to_all x1 -> x0, starting transfers between devices: 10.2 us -> none  [sum_all(): lax.all_to_all(mine.reshape(64, 104, 128), CHIPS, split_axis=0, concat_ax...]
    ppermute x1, starting transfers between devices: 2.98 us -> 0.39 us  [sum_all(): other = lax.ppermute(mine, 'core', swap)]
  transfers between devices with their start and end apart: 10 -> 9, of which waited for: 7 -> 5; matrix products, arithmetic and copies ran while one was open for 2% -> 2% of each run, Pallas kernels for 1% -> 1%
where the time goes in v3:
time: 128 us; the launch traced here: 127 us
  blocking collectives  33.2 us (26%)
  Pallas kernels  29.6 us (23%)
  waiting for transfers between devices  29.1 us (23%)
  starting transfers between devices  26.4 us (21%)
  local copies, waits for them, and re-layouts  4.2 us (3%)
  other arithmetic  3.81 us (3%)
    all_to_all x1, blocking collectives, sum_all(): lax.all_to_all(mine.reshape(64, 104, 128), CHIPS, split_axis=0, concat_ax...  33.2 us
    pallas_call x1, Pallas kernels, section(): pl.pallas_call(section_kernel, out_shape=(jax.ShapeDtypeStruct((576, 512)...  24.4 us
    ppermute x1, waiting for transfers between devices, send_back(): corner = lax.ppermute(tile[h - SH:, w - SW:], LAT + LON, corner_pairs(1))  20.5 us
    all_to_all x1, starting transfers between devices, sum_all(): lax.all_to_all(spread, CHIPS, split_axis=0, concat_axis=0, tiled=True)  7.16 us
    ppermute x1, starting transfers between devices, fetch(): lax.ppermute(right, LON, neighbours(LON, -1))  6.37 us
    ppermute x1, starting transfers between devices, send_back(): above = lax.ppermute(tile[h - SH:, :w - SW], LAT, neighbours(LAT, 1))  4.69 us
    ppermute x1, waiting for transfers between devices, sum_all(): other = lax.ppermute(send, 'core', swap)  3.43 us
    ppermute x1, starting transfers between devices, fetch(): lax.ppermute(corner, LAT + LON, corner_pairs(-1))  3.31 us
  transfers between devices with their start and end apart: 9, of which 5 were waited for; matrix products, arithmetic and copies ran while one was open for 2% of the time, Pallas kernels for 1%

profile of v3, /device:TPU:1, one launch (start us, length us, event | category | flops | bytes accessed | tf_op | source)
XLA Modules:
  0.0 127.3 jit_solution(5935188598318153578)
XLA Ops:
  0.6 0.0 copy-start.1
  0.6 0.0 copy-start.2
  0.7 0.0 copy-start.5
  0.7 0.0 copy-start.4
  0.7 0.0 copy-start.6
  0.7 0.0 copy-start.8
  0.7 0.0 copy-start.3
  0.7 0.0 copy-start.7
  0.7 2.1 %reshape.34.x_ref = bf16[576,512]{1,0:T(8,128)(2,1)S(1)} reshape(bf16[12,24,2,512]{3,2,1,0:T(2,128)(2,1)} %param.11) | data formatting | bytes 1179648 | tf_op jit(solution)/shard_map/reshape | solution.py:650
  2.8 0.0 copy-start
  2.8 0.0 copy-done.1
  2.9 0.2 pack.1
  3.1 1.5 %collective-permute-start = (bf16[936,128]{1,0:T(8,128)(2,1)S(1)}, bf16[936,128]{1,0:T(8,128)(2,1)S(1)}, u32[]{:S(2)}, u32[]{:S(2)}) collective-permute-start(bf16[936,128]{1,0:T(8,128)(2,1)S(1)} %get-tuple-element.27), channel_id=1, source_target_pairs={{0,96},{32,0},{64,32},{96,64},{1,97},{33,1},{65,33},{97,65},{2,98}... | collective-permute-start | bytes 718856 | tf_op jit(solution)/shard_map/ppermute | solution.py:527
  4.5 6.4 %collective-permute-start.1 = (bf16[936,128]{1,0:T(8,128)(2,1)S(1)}, bf16[936,128]{1,0:T(8,128)(2,1)S(1)}, u32[]{:S(2)}, u32[]{:S(2)}) collective-permute-start(bf16[936,128]{1,0:T(8,128)(2,1)S(1)} %get-tuple-element.28), channel_id=1, source_target_pairs={{0,31},{1,0},{2,1},{3,2},{4,3},{5,4},{6,5},{7,6},{8,7},{9,8},{10,9... | collective-permute-start | bytes 718856 | tf_op jit(solution)/shard_map/ppermute | solution.py:528
  10.9 3.3 %collective-permute-start.2 = (bf16[312,128]{1,0:T(8,128)(2,1)S(1)}, bf16[312,128]{1,0:T(8,128)(2,1)S(1)}, u32[]{:S(2)}, u32[]{:S(2)}) collective-permute-start(bf16[312,128]{1,0:T(8,128)(2,1)S(1)} %get-tuple-element.29), channel_id=1, source_target_pairs={{0,127},{1,96},{2,97},{3,98},{4,99},{5,100},{6,101},{7,102},{8,103... | collective-permute-start | bytes 239624 | tf_op jit(solution)/shard_map/ppermute | solution.py:529
  14.2 2.1 %collective-permute-done.2.corner_ref = bf16[312,128]{1,0:T(8,128)(2,1)S(1)} collective-permute-done((bf16[312,128]{1,0:T(8,128)(2,1)S(1)}, bf16[312,128]{1,0:T(8,128)(2,1)S(1)}, u32[]{:S(2)}, u32[]{:S(2)}) %collective-permute-start.2) | collective-permute-done | bytes 79904 | tf_op jit(solution)/shard_map/ppermute | solution.py:529
  16.4 1.6 %collective-permute-done.below_ref = bf16[936,128]{1,0:T(8,128)(2,1)S(1)} collective-permute-done((bf16[936,128]{1,0:T(8,128)(2,1)S(1)}, bf16[936,128]{1,0:T(8,128)(2,1)S(1)}, u32[]{:S(2)}, u32[]{:S(2)}) %collective-permute-start) | collective-permute-done | bytes 239648 | tf_op jit(solution)/shard_map/ppermute | solution.py:527
  17.9 0.0 collective-permute-done.1.right_ref
  17.9 0.0 copy-done
  17.9 0.0 copy-done.2
  17.9 0.0 copy-done.5
  17.9 0.0 copy-done.4
  17.9 0.0 copy-done.6
  18.0 0.0 copy-done.8
  18.0 0.0 copy-done.3
  18.0 0.0 copy-done.7
  18.0 24.4 %section.1 = (bf16[576,512]{1,0:T(8,128)(2,1)}, bf16[6656,128]{1,0:T(8,128)(2,1)}, bf16[6656,128]{1,0:T(8,128)(2,1)}) custom-call(s32[1,1]{1,0:T(1,128)} %bitcast.core_ref, s32[13]{0:T(128)S(1)} %copy-done.2, bf16[576,512]{1,0:T(8,128)(2,1)} %copy-done, bf16[936,128]{1,0:T(8,128)(2,1)S(1)} %collective-permute-done.below_ref, ...), custom_call_target="tpu_custom_call" | custom-call | flops 15000000512 | bytes 12000000 | tf_op jit(solution)/shard_map/section/pallas_call | solution.py:491
  42.4 1.4 %collective-permute-start.3 = (bf16[6656,128]{1,0:T(8,128)(2,1)}, bf16[6656,128]{1,0:T(8,128)(2,1)S(1)}, u32[]{:S(2)}, u32[]{:S(2)}) collective-permute-start(bf16[6656,128]{1,0:T(8,128)(2,1)} %get-tuple-element.31), channel_id=1, source_target_pairs={{0,32},{32,0},{1,33},{33,1},{2,34},{34,2},{3,35},{35,3},{4,36},{36... | collective-permute-start | bytes 5111816 | tf_op jit(solution)/shard_map/ppermute | solution.py:550
  43.8 3.4 %collective-permute-done.3 = bf16[6656,128]{1,0:T(8,128)(2,1)S(1)} collective-permute-done((bf16[6656,128]{1,0:T(8,128)(2,1)}, bf16[6656,128]{1,0:T(8,128)(2,1)S(1)}, u32[]{:S(2)}, u32[]{:S(2)}) %collective-permute-start.3) | collective-permute-done | bytes 1703968 | tf_op jit(solution)/shard_map/ppermute | solution.py:550
  47.2 1.9 %add_convert_fusion = bf16[6656,128]{1,0:T(8,128)(2,1)S(1)} fusion(bf16[6656,128]{1,0:T(8,128)(2,1)S(1)} %collective-permute-done.3, bf16[6656,128]{1,0:T(8,128)(2,1)} %get-tuple-element.30), kind=kLoop, calls=%fused_computation | loop fusion | flops 3407872 | bytes 5111808 | tf_op jit(solution)/shard_map/convert_element_type | solution.py:551
  49.1 33.2 %all_to_all.10 = bf16[64,104,128]{2,1,0:T(8,128)(2,1)S(1)} all-to-all(bf16[64,104,128]{2,1,0:T(8,128)(2,1)S(1)} %bitcast.15), channel_id=1, replica_groups=mesh['z_hi'=2,'core'=2,'x'=4,'y'=4,'z_lo'=2] {'z_hi','x','y','z_lo'}, dimensions={0} | all-to-all | bytes 3407872 | tf_op jit(solution)/shard_map/all_to_all | solution.py:552
  82.3 0.3 reduce_sum.12
  82.6 1.4 %broadcast_in_dim.10 = bf16[64,104,128]{2,1,0:T(8,128)(2,1)} broadcast(bf16[104,128]{1,0:T(8,128)(2,1)S(1)} %reduce_sum.12), dimensions={1,2} | broadcast | bytes 1730560 | tf_op jit(solution)/shard_map/broadcast_in_dim | solution.py:554
  84.0 0.0 copy-start.9
  84.0 7.2 %all-to-all-start.1 = ((bf16[64,104,128]{2,1,0:T(8,128)(2,1)}), bf16[64,104,128]{2,1,0:T(8,128)(2,1)S(1)}, u32[]{:S(2)}, u32[]{:S(2)}) async-start(bf16[64,104,128]{2,1,0:T(8,128)(2,1)} %broadcast_in_dim.10), calls=%async_computation.1 | async-start | bytes 3407872 | tf_op jit(solution)/shard_map/all_to_all | solution.py:555
  91.2 0.0 copy-done.9
  91.2 0.2 reshape.37
  91.4 0.1 slice.18
  91.5 0.1 slice.17
  91.6 4.7 %collective-permute-start.5 = (bf16[3,18,2,512]{3,2,1,0:T(2,128)(2,1)S(1)}, bf16[3,18,2,512]{3,2,1,0:T(2,128)(2,1)S(1)}, u32[]{:S(2)}, u32[]{:S(2)}) collective-permute-start(bf16[3,18,2,512]{3,2,1,0:T(2,128)(2,1)S(1)} %slice.17), channel_id=1, source_target_pairs={{0,32},{32,64},{64,96},{96,0},{1,33},{33,65},{65,97},{97,1},{2,34}... | collective-permute-start | bytes 331784 | tf_op jit(solution)/shard_map/ppermute | solution.py:535
  96.3 0.3 collective-permute-start.6
  96.6 1.3 %collective-permute-start.4 = (bf16[3,6,2,512]{3,2,1,0:T(2,128)(2,1)S(1)}, bf16[3,6,2,512]{3,2,1,0:T(2,128)(2,1)S(1)}, u32[]{:S(2)}, u32[]{:S(2)}) collective-permute-start(bf16[3,6,2,512]{3,2,1,0:T(2,128)(2,1)S(1)} %slice.16), channel_id=1, source_target_pairs={{0,33},{1,34},{2,35},{3,36},{4,37},{5,38},{6,39},{7,40},{8,41},{9,... | collective-permute-start | bytes 110600 | tf_op jit(solution)/shard_map/ppermute | solution.py:537
  97.9 0.2 slice.19
  98.2 20.5 %collective-permute-done.4 = bf16[3,6,2,512]{3,2,1,0:T(2,128)(2,1)S(1)} collective-permute-done((bf16[3,6,2,512]{3,2,1,0:T(2,128)(2,1)S(1)}, bf16[3,6,2,512]{3,2,1,0:T(2,128)(2,1)S(1)}, u32[]{:S(2)}, u32[]{:S(2)}) %collective-permute-start.4) | collective-permute-done | bytes 36896 | tf_op jit(solution)/shard_map/ppermute | solution.py:537
  118.7 0.0 collective-permute-done.5
  118.7 0.0 collective-permute-done.6
  118.7 1.7 %maximum_maximum_fusion = bf16[12,24,2,512]{3,2,1,0:T(2,128)(2,1)} fusion(bf16[9,18,2,512]{3,2,1,0:T(2,128)(2,1)S(1)} %slice.19, bf16[9,6,2,512]{3,2,1,0:T(2,128)(2,1)S(1)} %collective-permute-done.6, bf16[3,18,2,512]{3,2,1,0:T(2,128)(2,1)S(1)} %collective-permute-done.5, bf16[3,6,2,512]{3,2,1,0:T(2,128)(2,1)S(1)} %collective-permute-done.4), kind=kLoop, calls=%fused_computation.1 | loop fusion | flops 884736 | bytes 1179648 | tf_op jit(solution)/shard_map/concatenate | solution.py:545
  120.4 0.0 all-to-all-done.1
  120.4 0.4 collective-permute-start.7
  120.7 1.8 %unpack_mine.1 = (f32[512,1536]{1,0:T(8,128)}, f32[512,512]{1,0:T(8,128)}, f32[512,512]{1,0:T(8,128)}, f32[512,512]{1,0:T(8,128)}) custom-call(s32[1,1]{1,0:T(1,128)} %bitcast.core_ref, bf16[6656,128]{1,0:T(8,128)(2,1)S(1)} %bitcast.9), custom_call_target="tpu_custom_call" | custom-call | flops 3000000 | bytes 6000000 | tf_op jit(solution)/shard_map/unpack_mine/pallas_call | solution.py:621
  122.6 1.4 %collective-permute-done.7.other_ref = bf16[6656,128]{1,0:T(8,128)(2,1)S(1)} collective-permute-done((bf16[6656,128]{1,0:T(8,128)(2,1)S(1)}, bf16[6656,128]{1,0:T(8,128)(2,1)S(1)}, u32[]{:S(2)}, u32[]{:S(2)}) %collective-permute-start.7) | collective-permute-done | bytes 1703968 | tf_op jit(solution)/shard_map/ppermute | solution.py:557
  124.0 3.1 %unpack_other.1 = (f32[512,1536]{1,0:T(8,128)}, f32[512,512]{1,0:T(8,128)}, f32[512,512]{1,0:T(8,128)}, f32[512,512]{1,0:T(8,128)}, f32[80,512]{1,0:T(8,128)}, /*index=5*/f32[1,512]{1,0:T(1,128)}, f32[37,512]{1,0:T(8,128)}) custom-call(s32[1,1]{1,0:T(1,128)} %bitcast.core_ref, ...), custom_call_target="tpu_custom_call", output_to_operand_aliasing={{0}: (4, {}), {1}: (5, {}), {2}: (6, {}), {3}: (7, {})} | custom-call | flops 3000000 | bytes 6000000 | tf_op jit(solution)/shard_map/unpack_other/pallas_call | solution.py:631
  (1 shorter events, 0.0 us)
Async XLA Ops:
  0.6 2.2 %copy-start.1 = (bf16[12,24,13,80]{3,1,2,0:T(8,128)(2,1)S(1)}, bf16[12,24,13,80]{3,1,2,0:T(8,128)(2,1)}, u32[]{:S(2)}) copy-start(bf16[12,24,13,80]{3,1,2,0:T(8,128)(2,1)} %param.12) | copy-start | bytes 1797124
  0.6 17.3 %copy-start.2 = (s32[13]{0:T(128)S(1)}, s32[13]{0:T(128)}, u32[]{:S(2)}) copy-start(s32[13]{0:T(128)} %level_ref.3) | copy-start | bytes 160
  0.7 17.3 %copy-start.5 = (bf16[512,80]{0,1:T(8,128)(2,1)S(1)}, bf16[512,80]{0,1:T(8,128)(2,1)}, u32[]{:S(2)}) copy-start(bf16[512,80]{0,1:T(8,128)(2,1)} %param.21) | copy-start | bytes 245764
  0.7 17.3 %copy-start.4 = (bf16[512,512]{1,0:T(8,128)(2,1)S(1)}, bf16[512,512]{1,0:T(8,128)(2,1)}, u32[]{:S(2)}) copy-start(bf16[512,512]{1,0:T(8,128)(2,1)} %wkey_hbm.1) | copy-start | bytes 1572868
  0.7 17.3 %copy-start.6 = (bf16[37,512]{1,0:T(8,128)(2,1)S(1)}, bf16[37,512]{1,0:T(8,128)(2,1)}, u32[]{:S(2)}) copy-start(bf16[37,512]{1,0:T(8,128)(2,1)} %table_ref.1) | copy-start | bytes 113668
  0.7 17.3 %copy-start.8 = (f32[512]{0:T(512)S(1)}, f32[512]{0:T(512)}, u32[]{:S(2)}) copy-start(f32[512]{0:T(512)} %param.17) | copy-start | bytes 6148
  0.7 17.3 %copy-start.3 = (bf16[512,512]{1,0:T(8,128)(2,1)S(1)}, bf16[512,512]{1,0:T(8,128)(2,1)}, u32[]{:S(2)}) copy-start(bf16[512,512]{1,0:T(8,128)(2,1)} %wproj_hbm.1) | copy-start | bytes 1572868
  0.7 17.3 %copy-start.7 = (s32[12,24]{1,0:T(8,128)S(1)}, s32[12,24]{1,0:T(8,128)}, u32[]{:S(2)}) copy-start(s32[12,24]{1,0:T(8,128)} %ids_ref.1) | copy-start | bytes 3460
  2.8 15.1 %copy-start = (bf16[576,512]{1,0:T(8,128)(2,1)}, bf16[576,512]{1,0:T(8,128)(2,1)S(1)}, u32[]{:S(2)}) copy-start(bf16[576,512]{1,0:T(8,128)(2,1)S(1)} %reshape.34.x_ref) | copy-start | bytes 1769476
  3.1 14.9 %collective-permute-start = (bf16[936,128]{1,0:T(8,128)(2,1)S(1)}, bf16[936,128]{1,0:T(8,128)(2,1)S(1)}, u32[]{:S(2)}, u32[]{:S(2)}) collective-permute-start(bf16[936,128]{1,0:T(8,128)(2,1)S(1)} %get-tuple-element.27), channel_id=1, source_target_pairs={{0,96},{32,0},{64,32},{96,64},{1,97},{33,1},{65,33},{97,65},{2,98}... | collective-permute-start | bytes 718856 | tf_op jit(solution)/shard_map/ppermute | solution.py:527
  4.5 13.4 %collective-permute-start.1 = (bf16[936,128]{1,0:T(8,128)(2,1)S(1)}, bf16[936,128]{1,0:T(8,128)(2,1)S(1)}, u32[]{:S(2)}, u32[]{:S(2)}) collective-permute-start(bf16[936,128]{1,0:T(8,128)(2,1)S(1)} %get-tuple-element.28), channel_id=1, source_target_pairs={{0,31},{1,0},{2,1},{3,2},{4,3},{5,4},{6,5},{7,6},{8,7},{9,8},{10,9... | collective-permute-start | bytes 718856 | tf_op jit(solution)/shard_map/ppermute | solution.py:528
  10.9 5.4 %collective-permute-start.2 = (bf16[312,128]{1,0:T(8,128)(2,1)S(1)}, bf16[312,128]{1,0:T(8,128)(2,1)S(1)}, u32[]{:S(2)}, u32[]{:S(2)}) collective-permute-start(bf16[312,128]{1,0:T(8,128)(2,1)S(1)} %get-tuple-element.29), channel_id=1, source_target_pairs={{0,127},{1,96},{2,97},{3,98},{4,99},{5,100},{6,101},{7,102},{8,103... | collective-permute-start | bytes 239624 | tf_op jit(solution)/shard_map/ppermute | solution.py:529
  42.4 4.8 %collective-permute-start.3 = (bf16[6656,128]{1,0:T(8,128)(2,1)}, bf16[6656,128]{1,0:T(8,128)(2,1)S(1)}, u32[]{:S(2)}, u32[]{:S(2)}) collective-permute-start(bf16[6656,128]{1,0:T(8,128)(2,1)} %get-tuple-element.31), channel_id=1, source_target_pairs={{0,32},{32,0},{1,33},{33,1},{2,34},{34,2},{3,35},{35,3},{4,36},{36... | collective-permute-start | bytes 5111816 | tf_op jit(solution)/shard_map/ppermute | solution.py:550
  84.0 7.2 %copy-start.9 = (bf16[576,512]{1,0:T(8,128)(2,1)S(1)}, bf16[576,512]{1,0:T(8,128)(2,1)}, u32[]{:S(2)}) copy-start(bf16[576,512]{1,0:T(8,128)(2,1)} %get-tuple-element.32) | copy-start | bytes 1769476
  84.0 36.4 %all-to-all-start.1 = ((bf16[64,104,128]{2,1,0:T(8,128)(2,1)}), bf16[64,104,128]{2,1,0:T(8,128)(2,1)S(1)}, u32[]{:S(2)}, u32[]{:S(2)}) async-start(bf16[64,104,128]{2,1,0:T(8,128)(2,1)} %broadcast_in_dim.10), calls=%async_computation.1 | async-start | bytes 3407872 | tf_op jit(solution)/shard_map/all_to_all | solution.py:555
  91.6 27.1 %collective-permute-start.5 = (bf16[3,18,2,512]{3,2,1,0:T(2,128)(2,1)S(1)}, bf16[3,18,2,512]{3,2,1,0:T(2,128)(2,1)S(1)}, u32[]{:S(2)}, u32[]{:S(2)}) collective-permute-start(bf16[3,18,2,512]{3,2,1,0:T(2,128)(2,1)S(1)} %slice.17), channel_id=1, source_target_pairs={{0,32},{32,64},{64,96},{96,0},{1,33},{33,65},{65,97},{97,1},{2,34}... | collective-permute-start | bytes 331784 | tf_op jit(solution)/shard_map/ppermute | solution.py:535
  96.3 22.4 %collective-permute-start.6 = (bf16[9,6,2,512]{3,2,1,0:T(2,128)(2,1)S(1)}, bf16[9,6,2,512]{3,2,1,0:T(2,128)(2,1)S(1)}, u32[]{:S(2)}, u32[]{:S(2)}) collective-permute-start(bf16[9,6,2,512]{3,2,1,0:T(2,128)(2,1)S(1)} %slice.18), channel_id=1, source_target_pairs={{0,1},{1,2},{2,3},{3,4},{4,5},{5,6},{6,7},{7,8},{8,9},{9,10},{10,1... | collective-permute-start | bytes 331784 | tf_op jit(solution)/shard_map/ppermute | solution.py:536
  96.6 22.1 %collective-permute-start.4 = (bf16[3,6,2,512]{3,2,1,0:T(2,128)(2,1)S(1)}, bf16[3,6,2,512]{3,2,1,0:T(2,128)(2,1)S(1)}, u32[]{:S(2)}, u32[]{:S(2)}) collective-permute-start(bf16[3,6,2,512]{3,2,1,0:T(2,128)(2,1)S(1)} %slice.16), channel_id=1, source_target_pairs={{0,33},{1,34},{2,35},{3,36},{4,37},{5,38},{6,39},{7,40},{8,41},{9,... | collective-permute-start | bytes 110600 | tf_op jit(solution)/shard_map/ppermute | solution.py:537
  120.4 3.6 %collective-permute-start.7 = (bf16[6656,128]{1,0:T(8,128)(2,1)S(1)}, bf16[6656,128]{1,0:T(8,128)(2,1)S(1)}, u32[]{:S(2)}, u32[]{:S(2)}) collective-permute-start(bf16[6656,128]{1,0:T(8,128)(2,1)S(1)} %bitcast.8), channel_id=1, source_target_pairs={{0,32},{32,0},{1,33},{33,1},{2,34},{34,2},{3,35},{35,3},{4,36},{36... | collective-permute-start | bytes 5111816 | tf_op jit(solution)/shard_map/ppermute | solution.py:557

commit v4 on v3

--- a/solution.py
+++ b/solution.py
@@ -504,7 +504,7 @@
 
 LAT = ("z_hi", "core")
 LON = ("x", "y", "z_lo")
-CHIPS = ("z_hi", "x", "y", "z_lo")
+CHIPS = ("x", "y", "z_hi", "z_lo")
 
 
 def neighbours(axes, by):

time: 128 us -> 128 us (level)
  starting transfers between devices: 26.4 us -> 25 us
where the time goes in v4:
time: 128 us
  blocking collectives  33.8 us (26%)
  waiting for transfers between devices  30.2 us (24%)
  Pallas kernels  29.6 us (23%)
  starting transfers between devices  25 us (20%)
  local copies, waits for them, and re-layouts  4.2 us (3%)
  other arithmetic  3.81 us (3%)
    all_to_all x1, blocking collectives, sum_all(): lax.all_to_all(mine.reshape(64, 104, 128), CHIPS, split_axis=0, concat_ax...  33.8 us
    pallas_call x1, Pallas kernels, section(): pl.pallas_call(section_kernel, out_shape=(jax.ShapeDtypeStruct((576, 512)...  24.4 us
    ppermute x1, waiting for transfers between devices, send_back(): corner = lax.ppermute(tile[h - SH:, w - SW:], LAT + LON, corner_pairs(1))  21.7 us
    ppermute x1, starting transfers between devices, fetch(): lax.ppermute(right, LON, neighbours(LON, -1))  6.37 us
    all_to_all x1, starting transfers between devices, sum_all(): lax.all_to_all(spread, CHIPS, split_axis=0, concat_axis=0, tiled=True)  6.26 us
    ppermute x1, starting transfers between devices, send_back(): above = lax.ppermute(tile[h - SH:, :w - SW], LAT, neighbours(LAT, 1))  4.08 us
    ppermute x1, waiting for transfers between devices, sum_all(): other = lax.ppermute(send, 'core', swap)  3.43 us
    ppermute x1, starting transfers between devices, fetch(): lax.ppermute(corner, LAT + LON, corner_pairs(-1))  3.31 us
  transfers between devices with their start and end apart: 9, of which 5 were waited for; matrix products, arithmetic and copies ran while one was open for 2% of the time, Pallas kernels for 1%

profile of v4, /device:TPU:1, one launch (start us, length us, event | category | flops | bytes accessed | tf_op | source)
XLA Modules:
  0.0 127.6 jit_solution(13871083920869206994)
XLA Ops:
  0.6 0.0 copy-start.1
  0.6 0.0 copy-start.2
  0.7 0.0 copy-start.5
  0.7 0.0 copy-start.4
  0.7 0.0 copy-start.6
  0.7 0.0 copy-start.8
  0.7 0.0 copy-start.3
  0.7 0.0 copy-start.7
  0.7 2.1 %reshape.34.x_ref = bf16[576,512]{1,0:T(8,128)(2,1)S(1)} reshape(bf16[12,24,2,512]{3,2,1,0:T(2,128)(2,1)} %param.11) | data formatting | bytes 1179648 | tf_op jit(solution)/shard_map/reshape | solution.py:650
  2.8 0.0 copy-start
  2.8 0.0 copy-done.1
  2.9 0.2 pack.1
  3.1 1.5 %collective-permute-start = (bf16[936,128]{1,0:T(8,128)(2,1)S(1)}, bf16[936,128]{1,0:T(8,128)(2,1)S(1)}, u32[]{:S(2)}, u32[]{:S(2)}) collective-permute-start(bf16[936,128]{1,0:T(8,128)(2,1)S(1)} %get-tuple-element.27), channel_id=1, source_target_pairs={{0,96},{32,0},{64,32},{96,64},{1,97},{33,1},{65,33},{97,65},{2,98}... | collective-permute-start | bytes 718856 | tf_op jit(solution)/shard_map/ppermute | solution.py:527
  4.5 6.4 %collective-permute-start.1 = (bf16[936,128]{1,0:T(8,128)(2,1)S(1)}, bf16[936,128]{1,0:T(8,128)(2,1)S(1)}, u32[]{:S(2)}, u32[]{:S(2)}) collective-permute-start(bf16[936,128]{1,0:T(8,128)(2,1)S(1)} %get-tuple-element.28), channel_id=1, source_target_pairs={{0,31},{1,0},{2,1},{3,2},{4,3},{5,4},{6,5},{7,6},{8,7},{9,8},{10,9... | collective-permute-start | bytes 718856 | tf_op jit(solution)/shard_map/ppermute | solution.py:528
  10.9 3.3 %collective-permute-start.2 = (bf16[312,128]{1,0:T(8,128)(2,1)S(1)}, bf16[312,128]{1,0:T(8,128)(2,1)S(1)}, u32[]{:S(2)}, u32[]{:S(2)}) collective-permute-start(bf16[312,128]{1,0:T(8,128)(2,1)S(1)} %get-tuple-element.29), channel_id=1, source_target_pairs={{0,127},{1,96},{2,97},{3,98},{4,99},{5,100},{6,101},{7,102},{8,103... | collective-permute-start | bytes 239624 | tf_op jit(solution)/shard_map/ppermute | solution.py:529
  14.2 2.1 %collective-permute-done.2.corner_ref = bf16[312,128]{1,0:T(8,128)(2,1)S(1)} collective-permute-done((bf16[312,128]{1,0:T(8,128)(2,1)S(1)}, bf16[312,128]{1,0:T(8,128)(2,1)S(1)}, u32[]{:S(2)}, u32[]{:S(2)}) %collective-permute-start.2) | collective-permute-done | bytes 79904 | tf_op jit(solution)/shard_map/ppermute | solution.py:529
  16.4 1.6 %collective-permute-done.below_ref = bf16[936,128]{1,0:T(8,128)(2,1)S(1)} collective-permute-done((bf16[936,128]{1,0:T(8,128)(2,1)S(1)}, bf16[936,128]{1,0:T(8,128)(2,1)S(1)}, u32[]{:S(2)}, u32[]{:S(2)}) %collective-permute-start) | collective-permute-done | bytes 239648 | tf_op jit(solution)/shard_map/ppermute | solution.py:527
  17.9 0.0 collective-permute-done.1.right_ref
  17.9 0.0 copy-done
  17.9 0.0 copy-done.2
  17.9 0.0 copy-done.5
  17.9 0.0 copy-done.4
  17.9 0.0 copy-done.6
  18.0 0.0 copy-done.8
  18.0 0.0 copy-done.3
  18.0 0.0 copy-done.7
  18.0 24.4 %section.1 = (bf16[576,512]{1,0:T(8,128)(2,1)}, bf16[6656,128]{1,0:T(8,128)(2,1)}, bf16[6656,128]{1,0:T(8,128)(2,1)}) custom-call(s32[1,1]{1,0:T(1,128)} %bitcast.core_ref, s32[13]{0:T(128)S(1)} %copy-done.2, bf16[576,512]{1,0:T(8,128)(2,1)} %copy-done, bf16[936,128]{1,0:T(8,128)(2,1)S(1)} %collective-permute-done.below_ref, ...), custom_call_target="tpu_custom_call" | custom-call | flops 15000000512 | bytes 12000000 | tf_op jit(solution)/shard_map/section/pallas_call | solution.py:491
  42.4 1.4 %collective-permute-start.3 = (bf16[6656,128]{1,0:T(8,128)(2,1)}, bf16[6656,128]{1,0:T(8,128)(2,1)S(1)}, u32[]{:S(2)}, u32[]{:S(2)}) collective-permute-start(bf16[6656,128]{1,0:T(8,128)(2,1)} %get-tuple-element.31), channel_id=1, source_target_pairs={{0,32},{32,0},{1,33},{33,1},{2,34},{34,2},{3,35},{35,3},{4,36},{36... | collective-permute-start | bytes 5111816 | tf_op jit(solution)/shard_map/ppermute | solution.py:550
  43.8 3.4 %collective-permute-done.3 = bf16[6656,128]{1,0:T(8,128)(2,1)S(1)} collective-permute-done((bf16[6656,128]{1,0:T(8,128)(2,1)}, bf16[6656,128]{1,0:T(8,128)(2,1)S(1)}, u32[]{:S(2)}, u32[]{:S(2)}) %collective-permute-start.3) | collective-permute-done | bytes 1703968 | tf_op jit(solution)/shard_map/ppermute | solution.py:550
  47.2 1.9 %add_convert_fusion = bf16[6656,128]{1,0:T(8,128)(2,1)S(1)} fusion(bf16[6656,128]{1,0:T(8,128)(2,1)S(1)} %collective-permute-done.3, bf16[6656,128]{1,0:T(8,128)(2,1)} %get-tuple-element.30), kind=kLoop, calls=%fused_computation | loop fusion | flops 3407872 | bytes 5111808 | tf_op jit(solution)/shard_map/convert_element_type | solution.py:551
  49.1 33.8 %all_to_all.10 = bf16[64,104,128]{2,1,0:T(8,128)(2,1)S(1)} all-to-all(bf16[64,104,128]{2,1,0:T(8,128)(2,1)S(1)} %bitcast.15), channel_id=1, replica_groups=mesh['z_hi'=2,'core'=2,'x'=4,'y'=4,'z_lo'=2] {'x','y','z_hi','z_lo'}, dimensions={0} | all-to-all | bytes 3407872 | tf_op jit(solution)/shard_map/all_to_all | solution.py:552
  82.9 0.3 reduce_sum.12
  83.2 1.4 %broadcast_in_dim.10 = bf16[64,104,128]{2,1,0:T(8,128)(2,1)} broadcast(bf16[104,128]{1,0:T(8,128)(2,1)S(1)} %reduce_sum.12), dimensions={1,2} | broadcast | bytes 1730560 | tf_op jit(solution)/shard_map/broadcast_in_dim | solution.py:554
  84.6 0.0 copy-start.9
  84.6 6.3 %all-to-all-start.1 = ((bf16[64,104,128]{2,1,0:T(8,128)(2,1)}), bf16[64,104,128]{2,1,0:T(8,128)(2,1)S(1)}, u32[]{:S(2)}, u32[]{:S(2)}) async-start(bf16[64,104,128]{2,1,0:T(8,128)(2,1)} %broadcast_in_dim.10), calls=%async_computation.1 | async-start | bytes 3407872 | tf_op jit(solution)/shard_map/all_to_all | solution.py:555
  90.9 0.0 copy-done.9
  90.9 0.2 reshape.37
  91.1 0.1 slice.18
  91.2 0.1 slice.17
  91.3 4.1 %collective-permute-start.5 = (bf16[3,18,2,512]{3,2,1,0:T(2,128)(2,1)S(1)}, bf16[3,18,2,512]{3,2,1,0:T(2,128)(2,1)S(1)}, u32[]{:S(2)}, u32[]{:S(2)}) collective-permute-start(bf16[3,18,2,512]{3,2,1,0:T(2,128)(2,1)S(1)} %slice.17), channel_id=1, source_target_pairs={{0,32},{32,64},{64,96},{96,0},{1,33},{33,65},{65,97},{97,1},{2,34}... | collective-permute-start | bytes 331784 | tf_op jit(solution)/shard_map/ppermute | solution.py:535
  95.4 0.3 collective-permute-start.6
  95.7 1.3 %collective-permute-start.4 = (bf16[3,6,2,512]{3,2,1,0:T(2,128)(2,1)S(1)}, bf16[3,6,2,512]{3,2,1,0:T(2,128)(2,1)S(1)}, u32[]{:S(2)}, u32[]{:S(2)}) collective-permute-start(bf16[3,6,2,512]{3,2,1,0:T(2,128)(2,1)S(1)} %slice.16), channel_id=1, source_target_pairs={{0,33},{1,34},{2,35},{3,36},{4,37},{5,38},{6,39},{7,40},{8,41},{9,... | collective-permute-start | bytes 110600 | tf_op jit(solution)/shard_map/ppermute | solution.py:537
  97.0 0.2 slice.19
  97.2 21.7 %collective-permute-done.4 = bf16[3,6,2,512]{3,2,1,0:T(2,128)(2,1)S(1)} collective-permute-done((bf16[3,6,2,512]{3,2,1,0:T(2,128)(2,1)S(1)}, bf16[3,6,2,512]{3,2,1,0:T(2,128)(2,1)S(1)}, u32[]{:S(2)}, u32[]{:S(2)}) %collective-permute-start.4) | collective-permute-done | bytes 36896 | tf_op jit(solution)/shard_map/ppermute | solution.py:537
  118.9 0.0 collective-permute-done.5
  118.9 0.0 collective-permute-done.6
  118.9 1.7 %maximum_maximum_fusion = bf16[12,24,2,512]{3,2,1,0:T(2,128)(2,1)} fusion(bf16[9,18,2,512]{3,2,1,0:T(2,128)(2,1)S(1)} %slice.19, bf16[9,6,2,512]{3,2,1,0:T(2,128)(2,1)S(1)} %collective-permute-done.6, bf16[3,18,2,512]{3,2,1,0:T(2,128)(2,1)S(1)} %collective-permute-done.5, bf16[3,6,2,512]{3,2,1,0:T(2,128)(2,1)S(1)} %collective-permute-done.4), kind=kLoop, calls=%fused_computation.1 | loop fusion | flops 884736 | bytes 1179648 | tf_op jit(solution)/shard_map/concatenate | solution.py:545
  120.6 0.0 all-to-all-done.1
  120.6 0.5 collective-permute-start.7
  121.1 1.8 %unpack_mine.1 = (f32[512,1536]{1,0:T(8,128)}, f32[512,512]{1,0:T(8,128)}, f32[512,512]{1,0:T(8,128)}, f32[512,512]{1,0:T(8,128)}) custom-call(s32[1,1]{1,0:T(1,128)} %bitcast.core_ref, bf16[6656,128]{1,0:T(8,128)(2,1)S(1)} %bitcast.9), custom_call_target="tpu_custom_call" | custom-call | flops 3000000 | bytes 6000000 | tf_op jit(solution)/shard_map/unpack_mine/pallas_call | solution.py:621
  122.9 1.4 %collective-permute-done.7.other_ref = bf16[6656,128]{1,0:T(8,128)(2,1)S(1)} collective-permute-done((bf16[6656,128]{1,0:T(8,128)(2,1)S(1)}, bf16[6656,128]{1,0:T(8,128)(2,1)S(1)}, u32[]{:S(2)}, u32[]{:S(2)}) %collective-permute-start.7) | collective-permute-done | bytes 1703968 | tf_op jit(solution)/shard_map/ppermute | solution.py:557
  124.3 3.1 %unpack_other.1 = (f32[512,1536]{1,0:T(8,128)}, f32[512,512]{1,0:T(8,128)}, f32[512,512]{1,0:T(8,128)}, f32[512,512]{1,0:T(8,128)}, f32[80,512]{1,0:T(8,128)}, /*index=5*/f32[1,512]{1,0:T(1,128)}, f32[37,512]{1,0:T(8,128)}) custom-call(s32[1,1]{1,0:T(1,128)} %bitcast.core_ref, ...), custom_call_target="tpu_custom_call", output_to_operand_aliasing={{0}: (4, {}), {1}: (5, {}), {2}: (6, {}), {3}: (7, {})} | custom-call | flops 3000000 | bytes 6000000 | tf_op jit(solution)/shard_map/unpack_other/pallas_call | solution.py:631
  (1 shorter events, 0.0 us)
Async XLA Ops:
  0.6 2.2 %copy-start.1 = (bf16[12,24,13,80]{3,1,2,0:T(8,128)(2,1)S(1)}, bf16[12,24,13,80]{3,1,2,0:T(8,128)(2,1)}, u32[]{:S(2)}) copy-start(bf16[12,24,13,80]{3,1,2,0:T(8,128)(2,1)} %param.12) | copy-start | bytes 1797124
  0.6 17.3 %copy-start.2 = (s32[13]{0:T(128)S(1)}, s32[13]{0:T(128)}, u32[]{:S(2)}) copy-start(s32[13]{0:T(128)} %level_ref.3) | copy-start | bytes 160
  0.7 17.3 %copy-start.5 = (bf16[512,80]{0,1:T(8,128)(2,1)S(1)}, bf16[512,80]{0,1:T(8,128)(2,1)}, u32[]{:S(2)}) copy-start(bf16[512,80]{0,1:T(8,128)(2,1)} %param.21) | copy-start | bytes 245764
  0.7 17.3 %copy-start.4 = (bf16[512,512]{1,0:T(8,128)(2,1)S(1)}, bf16[512,512]{1,0:T(8,128)(2,1)}, u32[]{:S(2)}) copy-start(bf16[512,512]{1,0:T(8,128)(2,1)} %wkey_hbm.1) | copy-start | bytes 1572868
  0.7 17.3 %copy-start.6 = (bf16[37,512]{1,0:T(8,128)(2,1)S(1)}, bf16[37,512]{1,0:T(8,128)(2,1)}, u32[]{:S(2)}) copy-start(bf16[37,512]{1,0:T(8,128)(2,1)} %table_ref.1) | copy-start | bytes 113668
  0.7 17.3 %copy-start.8 = (f32[512]{0:T(512)S(1)}, f32[512]{0:T(512)}, u32[]{:S(2)}) copy-start(f32[512]{0:T(512)} %param.17) | copy-start | bytes 6148
  0.7 17.3 %copy-start.3 = (bf16[512,512]{1,0:T(8,128)(2,1)S(1)}, bf16[512,512]{1,0:T(8,128)(2,1)}, u32[]{:S(2)}) copy-start(bf16[512,512]{1,0:T(8,128)(2,1)} %wproj_hbm.1) | copy-start | bytes 1572868
  0.7 17.3 %copy-start.7 = (s32[12,24]{1,0:T(8,128)S(1)}, s32[12,24]{1,0:T(8,128)}, u32[]{:S(2)}) copy-start(s32[12,24]{1,0:T(8,128)} %ids_ref.1) | copy-start | bytes 3460
  2.8 15.1 %copy-start = (bf16[576,512]{1,0:T(8,128)(2,1)}, bf16[576,512]{1,0:T(8,128)(2,1)S(1)}, u32[]{:S(2)}) copy-start(bf16[576,512]{1,0:T(8,128)(2,1)S(1)} %reshape.34.x_ref) | copy-start | bytes 1769476
  3.1 14.9 %collective-permute-start = (bf16[936,128]{1,0:T(8,128)(2,1)S(1)}, bf16[936,128]{1,0:T(8,128)(2,1)S(1)}, u32[]{:S(2)}, u32[]{:S(2)}) collective-permute-start(bf16[936,128]{1,0:T(8,128)(2,1)S(1)} %get-tuple-element.27), channel_id=1, source_target_pairs={{0,96},{32,0},{64,32},{96,64},{1,97},{33,1},{65,33},{97,65},{2,98}... | collective-permute-start | bytes 718856 | tf_op jit(solution)/shard_map/ppermute | solution.py:527
  4.5 13.4 %collective-permute-start.1 = (bf16[936,128]{1,0:T(8,128)(2,1)S(1)}, bf16[936,128]{1,0:T(8,128)(2,1)S(1)}, u32[]{:S(2)}, u32[]{:S(2)}) collective-permute-start(bf16[936,128]{1,0:T(8,128)(2,1)S(1)} %get-tuple-element.28), channel_id=1, source_target_pairs={{0,31},{1,0},{2,1},{3,2},{4,3},{5,4},{6,5},{7,6},{8,7},{9,8},{10,9... | collective-permute-start | bytes 718856 | tf_op jit(solution)/shard_map/ppermute | solution.py:528
  10.9 5.4 %collective-permute-start.2 = (bf16[312,128]{1,0:T(8,128)(2,1)S(1)}, bf16[312,128]{1,0:T(8,128)(2,1)S(1)}, u32[]{:S(2)}, u32[]{:S(2)}) collective-permute-start(bf16[312,128]{1,0:T(8,128)(2,1)S(1)} %get-tuple-element.29), channel_id=1, source_target_pairs={{0,127},{1,96},{2,97},{3,98},{4,99},{5,100},{6,101},{7,102},{8,103... | collective-permute-start | bytes 239624 | tf_op jit(solution)/shard_map/ppermute | solution.py:529
  42.4 4.8 %collective-permute-start.3 = (bf16[6656,128]{1,0:T(8,128)(2,1)}, bf16[6656,128]{1,0:T(8,128)(2,1)S(1)}, u32[]{:S(2)}, u32[]{:S(2)}) collective-permute-start(bf16[6656,128]{1,0:T(8,128)(2,1)} %get-tuple-element.31), channel_id=1, source_target_pairs={{0,32},{32,0},{1,33},{33,1},{2,34},{34,2},{3,35},{35,3},{4,36},{36... | collective-permute-start | bytes 5111816 | tf_op jit(solution)/shard_map/ppermute | solution.py:550
  84.6 6.3 %copy-start.9 = (bf16[576,512]{1,0:T(8,128)(2,1)S(1)}, bf16[576,512]{1,0:T(8,128)(2,1)}, u32[]{:S(2)}) copy-start(bf16[576,512]{1,0:T(8,128)(2,1)} %get-tuple-element.32) | copy-start | bytes 1769476
  84.6 36.0 %all-to-all-start.1 = ((bf16[64,104,128]{2,1,0:T(8,128)(2,1)}), bf16[64,104,128]{2,1,0:T(8,128)(2,1)S(1)}, u32[]{:S(2)}, u32[]{:S(2)}) async-start(bf16[64,104,128]{2,1,0:T(8,128)(2,1)} %broadcast_in_dim.10), calls=%async_computation.1 | async-start | bytes 3407872 | tf_op jit(solution)/shard_map/all_to_all | solution.py:555
  91.3 27.6 %collective-permute-start.5 = (bf16[3,18,2,512]{3,2,1,0:T(2,128)(2,1)S(1)}, bf16[3,18,2,512]{3,2,1,0:T(2,128)(2,1)S(1)}, u32[]{:S(2)}, u32[]{:S(2)}) collective-permute-start(bf16[3,18,2,512]{3,2,1,0:T(2,128)(2,1)S(1)} %slice.17), channel_id=1, source_target_pairs={{0,32},{32,64},{64,96},{96,0},{1,33},{33,65},{65,97},{97,1},{2,34}... | collective-permute-start | bytes 331784 | tf_op jit(solution)/shard_map/ppermute | solution.py:535
  95.4 23.5 %collective-permute-start.6 = (bf16[9,6,2,512]{3,2,1,0:T(2,128)(2,1)S(1)}, bf16[9,6,2,512]{3,2,1,0:T(2,128)(2,1)S(1)}, u32[]{:S(2)}, u32[]{:S(2)}) collective-permute-start(bf16[9,6,2,512]{3,2,1,0:T(2,128)(2,1)S(1)} %slice.18), channel_id=1, source_target_pairs={{0,1},{1,2},{2,3},{3,4},{4,5},{5,6},{6,7},{7,8},{8,9},{9,10},{10,1... | collective-permute-start | bytes 331784 | tf_op jit(solution)/shard_map/ppermute | solution.py:536
  95.7 23.2 %collective-permute-start.4 = (bf16[3,6,2,512]{3,2,1,0:T(2,128)(2,1)S(1)}, bf16[3,6,2,512]{3,2,1,0:T(2,128)(2,1)S(1)}, u32[]{:S(2)}, u32[]{:S(2)}) collective-permute-start(bf16[3,6,2,512]{3,2,1,0:T(2,128)(2,1)S(1)} %slice.16), channel_id=1, source_target_pairs={{0,33},{1,34},{2,35},{3,36},{4,37},{5,38},{6,39},{7,40},{8,41},{9,... | collective-permute-start | bytes 110600 | tf_op jit(solution)/shard_map/ppermute | solution.py:537
  120.6 3.7 %collective-permute-start.7 = (bf16[6656,128]{1,0:T(8,128)(2,1)S(1)}, bf16[6656,128]{1,0:T(8,128)(2,1)S(1)}, u32[]{:S(2)}, u32[]{:S(2)}) collective-permute-start(bf16[6656,128]{1,0:T(8,128)(2,1)S(1)} %bitcast.8), channel_id=1, source_target_pairs={{0,32},{32,0},{1,33},{33,1},{2,34},{34,2},{3,35},{35,3},{4,36},{36... | collective-permute-start | bytes 5111816 | tf_op jit(solution)/shard_map/ppermute | solution.py:557

commit v5 on v3

--- a/solution.py
+++ b/solution.py
@@ -553,9 +553,8 @@
     piece = jnp.sum(pieces.astype(F32), axis=0).astype(BF16)
     spread = jnp.broadcast_to(piece[None], (64, 104, 128))
     mine = lax.all_to_all(spread, CHIPS, split_axis=0, concat_axis=0, tiled=True).reshape(6656, 128)
-    mine, d_latent = lax.optimization_barrier((mine, place_back(tile, *sent)))
     other = lax.ppermute(mine, "core", swap)
-    return mine, other, d_latent
+    return mine, other, place_back(tile, *sent)
 
 
 def spread_half(is_first, half_ref, targets, stage, sem):

time: 128 us -> 139 us (1.086)
  blocking collectives: 33.2 us -> 62.2 us
  waiting for transfers between devices: 29.1 us -> 13.2 us
  starting transfers between devices: 26.4 us -> 18.9 us
  local copies, waits for them, and re-layouts: 4.2 us -> 8.88 us
    all_to_all x0 -> x1, blocking collectives: none -> 28.9 us  [sum_all(): lax.all_to_all(spread, CHIPS, split_axis=0, concat_axis=0, tiled=True)]
    ppermute x1, waiting for transfers between devices: 20.5 us -> 5.85 us  [send_back(): corner = lax.ppermute(tile[h - SH:, w - SW:], LAT + LON, corner_pairs(1))]
    all_to_all x1 -> x0, starting transfers between devices: 7.16 us -> none  [sum_all(): lax.all_to_all(spread, CHIPS, split_axis=0, concat_axis=0, tiled=True)]
    ppermute x1, starting transfers between devices: 0.39 us -> 3.22 us  [sum_all(): other = lax.ppermute(mine, 'core', swap)]
    ppermute x1, starting transfers between devices: 4.69 us -> 2 us  [send_back(): above = lax.ppermute(tile[h - SH:, :w - SW], LAT, neighbours(LAT, 1))]
    reshape x1, local copies, waits for them, and re-layouts: 0.22 us -> 2.56 us  [shards(): tile = out.reshape(12, 24, 2, 512)]
    ppermute x1, waiting for transfers between devices: 1.4 us -> 0.01 us  [sum_all(): other = lax.ppermute(mine, 'core', swap)]
  transfers between devices with their start and end apart: 9 -> 8, of which waited for: 5 -> 4; matrix products, arithmetic and copies ran while one was open for 2% -> 6% of each run, Pallas kernels for 1% -> 1%
where the time goes in v5:
time: 139 us; the launch traced here: 138 us
  blocking collectives  62.2 us (45%)
  Pallas kernels  30.3 us (22%)
  starting transfers between devices  18.9 us (14%)
  waiting for transfers between devices  13.2 us (9%)
  local copies, waits for them, and re-layouts  8.88 us (6%)
  other arithmetic  3.82 us (3%)
    all_to_all x1, blocking collectives, sum_all(): lax.all_to_all(mine.reshape(64, 104, 128), CHIPS, split_axis=0, concat_ax...  33.3 us
    all_to_all x1, blocking collectives, sum_all(): lax.all_to_all(spread, CHIPS, split_axis=0, concat_axis=0, tiled=True)  28.9 us
    pallas_call x1, Pallas kernels, section(): pl.pallas_call(section_kernel, out_shape=(jax.ShapeDtypeStruct((576, 512)...  24.4 us
    ppermute x1, starting transfers between devices, fetch(): lax.ppermute(right, LON, neighbours(LON, -1))  6.37 us
    ppermute x1, waiting for transfers between devices, send_back(): corner = lax.ppermute(tile[h - SH:, w - SW:], LAT + LON, corner_pairs(1))  5.85 us
    ppermute x1, waiting for transfers between devices, sum_all(): other = lax.ppermute(send, 'core', swap)  3.43 us
    ppermute x1, starting transfers between devices, fetch(): lax.ppermute(corner, LAT + LON, corner_pairs(-1))  3.31 us
    ppermute x1, starting transfers between devices, sum_all(): other = lax.ppermute(mine, 'core', swap)  3.22 us
  transfers between devices with their start and end apart: 8, of which 4 were waited for; matrix products, arithmetic and copies ran while one was open for 6% of the time, Pallas kernels for 1%

profile of v5, /device:TPU:1, one launch (start us, length us, event | category | flops | bytes accessed | tf_op | source)
XLA Modules:
  0.0 138.3 jit_solution(1410363532057600042)
XLA Ops:
  0.6 0.0 copy-start.1
  0.6 0.0 copy-start.2
  0.7 0.0 copy-start.5
  0.7 0.0 copy-start.4
  0.7 0.0 copy-start.6
  0.7 0.0 copy-start.8
  0.7 0.0 copy-start.3
  0.7 0.0 copy-start.7
  0.7 2.1 %reshape.34.x_ref = bf16[576,512]{1,0:T(8,128)(2,1)S(1)} reshape(bf16[12,24,2,512]{3,2,1,0:T(2,128)(2,1)} %param.11) | data formatting | bytes 1179648 | tf_op jit(solution)/shard_map/reshape | solution.py:649
  2.8 0.0 copy-start
  2.8 0.0 copy-done.1
  2.9 0.9 pack.1
  3.7 1.4 %collective-permute-start = (bf16[936,128]{1,0:T(8,128)(2,1)}, bf16[936,128]{1,0:T(8,128)(2,1)S(1)}, u32[]{:S(2)}, u32[]{:S(2)}) collective-permute-start(bf16[936,128]{1,0:T(8,128)(2,1)} %get-tuple-element.25), channel_id=1, source_target_pairs={{0,96},{32,0},{64,32},{96,64},{1,97},{33,1},{65,33},{97,65},{2,98}... | collective-permute-start | bytes 718856 | tf_op jit(solution)/shard_map/ppermute | solution.py:527
  5.2 6.4 %collective-permute-start.1 = (bf16[936,128]{1,0:T(8,128)(2,1)S(1)}, bf16[936,128]{1,0:T(8,128)(2,1)S(1)}, u32[]{:S(2)}, u32[]{:S(2)}) collective-permute-start(bf16[936,128]{1,0:T(8,128)(2,1)S(1)} %get-tuple-element.26), channel_id=1, source_target_pairs={{0,31},{1,0},{2,1},{3,2},{4,3},{5,4},{6,5},{7,6},{8,7},{9,8},{10,9... | collective-permute-start | bytes 718856 | tf_op jit(solution)/shard_map/ppermute | solution.py:528
  11.5 3.3 %collective-permute-start.2 = (bf16[312,128]{1,0:T(8,128)(2,1)S(1)}, bf16[312,128]{1,0:T(8,128)(2,1)S(1)}, u32[]{:S(2)}, u32[]{:S(2)}) collective-permute-start(bf16[312,128]{1,0:T(8,128)(2,1)S(1)} %get-tuple-element.27), channel_id=1, source_target_pairs={{0,127},{1,96},{2,97},{3,98},{4,99},{5,100},{6,101},{7,102},{8,103... | collective-permute-start | bytes 239624 | tf_op jit(solution)/shard_map/ppermute | solution.py:529
  14.8 2.1 %collective-permute-done.2.corner_ref = bf16[312,128]{1,0:T(8,128)(2,1)S(1)} collective-permute-done((bf16[312,128]{1,0:T(8,128)(2,1)S(1)}, bf16[312,128]{1,0:T(8,128)(2,1)S(1)}, u32[]{:S(2)}, u32[]{:S(2)}) %collective-permute-start.2) | collective-permute-done | bytes 79904 | tf_op jit(solution)/shard_map/ppermute | solution.py:529
  17.0 1.8 %collective-permute-done.below_ref = bf16[936,128]{1,0:T(8,128)(2,1)S(1)} collective-permute-done((bf16[936,128]{1,0:T(8,128)(2,1)}, bf16[936,128]{1,0:T(8,128)(2,1)S(1)}, u32[]{:S(2)}, u32[]{:S(2)}) %collective-permute-start) | collective-permute-done | bytes 239648 | tf_op jit(solution)/shard_map/ppermute | solution.py:527
  18.7 0.0 collective-permute-done.1.right_ref
  18.7 0.0 copy-done
  18.8 0.0 copy-done.2
  18.8 0.0 copy-done.5
  18.8 0.0 copy-done.4
  18.8 0.0 copy-done.6
  18.8 0.0 copy-done.8
  18.8 0.0 copy-done.3
  18.8 0.0 copy-done.7
  18.8 24.4 %section.1 = (bf16[576,512]{1,0:T(8,128)(2,1)}, bf16[6656,128]{1,0:T(8,128)(2,1)}, bf16[6656,128]{1,0:T(8,128)(2,1)}) custom-call(s32[1,1]{1,0:T(1,128)} %bitcast.core_ref, s32[13]{0:T(128)S(1)} %copy-done.2, bf16[576,512]{1,0:T(8,128)(2,1)} %copy-done, bf16[936,128]{1,0:T(8,128)(2,1)S(1)} %collective-permute-done.below_ref, ...), custom_call_target="tpu_custom_call" | custom-call | flops 15000000512 | bytes 12000000 | tf_op jit(solution)/shard_map/section/pallas_call | solution.py:491
  43.3 1.2 collective-permute-start.6
  44.4 3.4 %collective-permute-done.6 = bf16[6656,128]{1,0:T(8,128)(2,1)S(1)} collective-permute-done((bf16[6656,128]{1,0:T(8,128)(2,1)}, bf16[6656,128]{1,0:T(8,128)(2,1)S(1)}, u32[]{:S(2)}, u32[]{:S(2)}) %collective-permute-start.6) | collective-permute-done | bytes 1703968 | tf_op jit(solution)/shard_map/ppermute | solution.py:550
  47.9 1.9 %add_convert_fusion = bf16[6656,128]{1,0:T(8,128)(2,1)S(1)} fusion(bf16[6656,128]{1,0:T(8,128)(2,1)S(1)} %collective-permute-done.6, bf16[6656,128]{1,0:T(8,128)(2,1)} %get-tuple-element.29), kind=kLoop, calls=%fused_computation | loop fusion | flops 3407872 | bytes 5111808 | tf_op jit(solution)/shard_map/convert_element_type | solution.py:551
  49.8 33.3 %all_to_all.10 = bf16[64,104,128]{2,1,0:T(8,128)(2,1)S(1)} all-to-all(bf16[64,104,128]{2,1,0:T(8,128)(2,1)S(1)} %bitcast.15), channel_id=1, replica_groups=mesh['z_hi'=2,'core'=2,'x'=4,'y'=4,'z_lo'=2] {'z_hi','x','y','z_lo'}, dimensions={0} | all-to-all | bytes 3407872 | tf_op jit(solution)/shard_map/all_to_all | solution.py:552
  83.0 0.3 reduce_sum.12
  83.3 0.2 broadcast_in_dim.10
  83.5 28.9 %all_to_all.11 = bf16[64,104,128]{2,1,0:T(8,128)(2,1)S(1)} all-to-all(bf16[64,104,128]{2,1,0:T(8,128)(2,1)S(1)} %broadcast_in_dim.10), channel_id=1, replica_groups=mesh['z_hi'=2,'core'=2,'x'=4,'y'=4,'z_lo'=2] {'z_hi','x','y','z_lo'}, dimensions={0} | all-to-all | bytes 3407872 | tf_op jit(solution)/shard_map/all_to_all | solution.py:555
  112.5 3.2 %collective-permute-start.7 = (bf16[6656,128]{1,0:T(8,128)(2,1)S(1)}, bf16[6656,128]{1,0:T(8,128)(2,1)S(1)}, u32[]{:S(2)}, u32[]{:S(2)}) collective-permute-start(bf16[6656,128]{1,0:T(8,128)(2,1)S(1)} %bitcast.8), channel_id=1, source_target_pairs={{0,32},{32,0},{1,33},{33,1},{2,34},{34,2},{3,35},{35,3},{4,36},{36... | collective-permute-start | bytes 5111816 | tf_op jit(solution)/shard_map/ppermute | solution.py:556
  115.7 2.6 %reshape.35 = bf16[12,24,2,512]{3,2,1,0:T(2,128)(2,1)} reshape(bf16[576,512]{1,0:T(8,128)(2,1)} %get-tuple-element.28) | data formatting | bytes 1179648 | tf_op jit(solution)/shard_map/reshape | solution.py:655
  118.3 1.0 slice.18
  119.2 1.0 slice.17
  120.2 2.0 %collective-permute-start.4 = (bf16[3,18,2,512]{3,2,1,0:T(2,128)(2,1)S(1)}, bf16[3,18,2,512]{3,2,1,0:T(2,128)(2,1)S(1)}, u32[]{:S(2)}, u32[]{:S(2)}) collective-permute-start(bf16[3,18,2,512]{3,2,1,0:T(2,128)(2,1)S(1)} %slice.17), channel_id=1, source_target_pairs={{0,32},{32,64},{64,96},{96,0},{1,33},{33,65},{65,97},{97,1},{2,34}... | collective-permute-start | bytes 331784 | tf_op jit(solution)/shard_map/ppermute | solution.py:535
  122.2 0.5 collective-permute-start.5
  122.7 0.8 slice.16
  123.5 0.9 collective-permute-start.3
  124.4 1.2 slice.19
  125.6 5.9 %collective-permute-done.3 = bf16[3,6,2,512]{3,2,1,0:T(2,128)(2,1)S(1)} collective-permute-done((bf16[3,6,2,512]{3,2,1,0:T(2,128)(2,1)S(1)}, bf16[3,6,2,512]{3,2,1,0:T(2,128)(2,1)S(1)}, u32[]{:S(2)}, u32[]{:S(2)}) %collective-permute-start.3) | collective-permute-done | bytes 36896 | tf_op jit(solution)/shard_map/ppermute | solution.py:537
  131.5 0.0 collective-permute-done.4
  131.5 0.0 collective-permute-done.5
  131.5 1.7 %maximum_maximum_fusion = bf16[12,24,2,512]{3,2,1,0:T(2,128)(2,1)} fusion(bf16[9,18,2,512]{3,2,1,0:T(2,128)(2,1)S(1)} %slice.19, bf16[9,6,2,512]{3,2,1,0:T(2,128)(2,1)S(1)} %collective-permute-done.5, bf16[3,18,2,512]{3,2,1,0:T(2,128)(2,1)S(1)} %collective-permute-done.4, bf16[3,6,2,512]{3,2,1,0:T(2,128)(2,1)S(1)} %collective-permute-done.3), kind=kLoop, calls=%fused_computation.1 | loop fusion | flops 884736 | bytes 1179648 | tf_op jit(solution)/shard_map/concatenate | solution.py:545
  133.1 1.8 %unpack_mine.1 = (f32[512,1536]{1,0:T(8,128)}, f32[512,512]{1,0:T(8,128)}, f32[512,512]{1,0:T(8,128)}, f32[512,512]{1,0:T(8,128)}) custom-call(s32[1,1]{1,0:T(1,128)} %bitcast.core_ref, bf16[6656,128]{1,0:T(8,128)(2,1)S(1)} %bitcast.9), custom_call_target="tpu_custom_call" | custom-call | flops 3000000 | bytes 6000000 | tf_op jit(solution)/shard_map/unpack_mine/pallas_call | solution.py:620
  135.0 0.0 collective-permute-done.7.other_ref
  135.0 3.2 %unpack_other.1 = (f32[512,1536]{1,0:T(8,128)}, f32[512,512]{1,0:T(8,128)}, f32[512,512]{1,0:T(8,128)}, f32[512,512]{1,0:T(8,128)}, f32[80,512]{1,0:T(8,128)}, /*index=5*/f32[1,512]{1,0:T(1,128)}, f32[37,512]{1,0:T(8,128)}) custom-call(s32[1,1]{1,0:T(1,128)} %bitcast.core_ref, ...), custom_call_target="tpu_custom_call", output_to_operand_aliasing={{0}: (4, {}), {1}: (5, {}), {2}: (6, {}), {3}: (7, {})} | custom-call | flops 3000000 | bytes 6000000 | tf_op jit(solution)/shard_map/unpack_other/pallas_call | solution.py:630
Async XLA Ops:
  0.6 2.2 %copy-start.1 = (bf16[12,24,13,80]{3,1,2,0:T(8,128)(2,1)S(1)}, bf16[12,24,13,80]{3,1,2,0:T(8,128)(2,1)}, u32[]{:S(2)}) copy-start(bf16[12,24,13,80]{3,1,2,0:T(8,128)(2,1)} %param.12) | copy-start | bytes 1797124
  0.6 18.1 %copy-start.2 = (s32[13]{0:T(128)S(1)}, s32[13]{0:T(128)}, u32[]{:S(2)}) copy-start(s32[13]{0:T(128)} %level_ref.3) | copy-start | bytes 160
  0.7 18.1 %copy-start.5 = (bf16[512,80]{0,1:T(8,128)(2,1)S(1)}, bf16[512,80]{0,1:T(8,128)(2,1)}, u32[]{:S(2)}) copy-start(bf16[512,80]{0,1:T(8,128)(2,1)} %param.21) | copy-start | bytes 245764
  0.7 18.1 %copy-start.4 = (bf16[512,512]{1,0:T(8,128)(2,1)S(1)}, bf16[512,512]{1,0:T(8,128)(2,1)}, u32[]{:S(2)}) copy-start(bf16[512,512]{1,0:T(8,128)(2,1)} %wkey_hbm.1) | copy-start | bytes 1572868
  0.7 18.1 %copy-start.6 = (bf16[37,512]{1,0:T(8,128)(2,1)S(1)}, bf16[37,512]{1,0:T(8,128)(2,1)}, u32[]{:S(2)}) copy-start(bf16[37,512]{1,0:T(8,128)(2,1)} %table_ref.1) | copy-start | bytes 113668
  0.7 18.1 %copy-start.8 = (f32[512]{0:T(512)S(1)}, f32[512]{0:T(512)}, u32[]{:S(2)}) copy-start(f32[512]{0:T(512)} %param.17) | copy-start | bytes 6148
  0.7 18.1 %copy-start.3 = (bf16[512,512]{1,0:T(8,128)(2,1)S(1)}, bf16[512,512]{1,0:T(8,128)(2,1)}, u32[]{:S(2)}) copy-start(bf16[512,512]{1,0:T(8,128)(2,1)} %wproj_hbm.1) | copy-start | bytes 1572868
  0.7 18.1 %copy-start.7 = (s32[12,24]{1,0:T(8,128)S(1)}, s32[12,24]{1,0:T(8,128)}, u32[]{:S(2)}) copy-start(s32[12,24]{1,0:T(8,128)} %ids_ref.1) | copy-start | bytes 3460
  2.8 15.9 %copy-start = (bf16[576,512]{1,0:T(8,128)(2,1)}, bf16[576,512]{1,0:T(8,128)(2,1)S(1)}, u32[]{:S(2)}) copy-start(bf16[576,512]{1,0:T(8,128)(2,1)S(1)} %reshape.34.x_ref) | copy-start | bytes 1769476
  3.7 15.0 %collective-permute-start = (bf16[936,128]{1,0:T(8,128)(2,1)}, bf16[936,128]{1,0:T(8,128)(2,1)S(1)}, u32[]{:S(2)}, u32[]{:S(2)}) collective-permute-start(bf16[936,128]{1,0:T(8,128)(2,1)} %get-tuple-element.25), channel_id=1, source_target_pairs={{0,96},{32,0},{64,32},{96,64},{1,97},{33,1},{65,33},{97,65},{2,98}... | collective-permute-start | bytes 718856 | tf_op jit(solution)/shard_map/ppermute | solution.py:527
  5.2 13.6 %collective-permute-start.1 = (bf16[936,128]{1,0:T(8,128)(2,1)S(1)}, bf16[936,128]{1,0:T(8,128)(2,1)S(1)}, u32[]{:S(2)}, u32[]{:S(2)}) collective-permute-start(bf16[936,128]{1,0:T(8,128)(2,1)S(1)} %get-tuple-element.26), channel_id=1, source_target_pairs={{0,31},{1,0},{2,1},{3,2},{4,3},{5,4},{6,5},{7,6},{8,7},{9,8},{10,9... | collective-permute-start | bytes 718856 | tf_op jit(solution)/shard_map/ppermute | solution.py:528
  11.5 5.4 %collective-permute-start.2 = (bf16[312,128]{1,0:T(8,128)(2,1)S(1)}, bf16[312,128]{1,0:T(8,128)(2,1)S(1)}, u32[]{:S(2)}, u32[]{:S(2)}) collective-permute-start(bf16[312,128]{1,0:T(8,128)(2,1)S(1)} %get-tuple-element.27), channel_id=1, source_target_pairs={{0,127},{1,96},{2,97},{3,98},{4,99},{5,100},{6,101},{7,102},{8,103... | collective-permute-start | bytes 239624 | tf_op jit(solution)/shard_map/ppermute | solution.py:529
  43.3 4.6 %collective-permute-start.6 = (bf16[6656,128]{1,0:T(8,128)(2,1)}, bf16[6656,128]{1,0:T(8,128)(2,1)S(1)}, u32[]{:S(2)}, u32[]{:S(2)}) collective-permute-start(bf16[6656,128]{1,0:T(8,128)(2,1)} %get-tuple-element.30), channel_id=1, source_target_pairs={{0,32},{32,0},{1,33},{33,1},{2,34},{34,2},{3,35},{35,3},{4,36},{36... | collective-permute-start | bytes 5111816 | tf_op jit(solution)/shard_map/ppermute | solution.py:550
  112.5 22.5 %collective-permute-start.7 = (bf16[6656,128]{1,0:T(8,128)(2,1)S(1)}, bf16[6656,128]{1,0:T(8,128)(2,1)S(1)}, u32[]{:S(2)}, u32[]{:S(2)}) collective-permute-start(bf16[6656,128]{1,0:T(8,128)(2,1)S(1)} %bitcast.8), channel_id=1, source_target_pairs={{0,32},{32,0},{1,33},{33,1},{2,34},{34,2},{3,35},{35,3},{4,36},{36... | collective-permute-start | bytes 5111816 | tf_op jit(solution)/shard_map/ppermute | solution.py:556
  120.2 11.3 %collective-permute-start.4 = (bf16[3,18,2,512]{3,2,1,0:T(2,128)(2,1)S(1)}, bf16[3,18,2,512]{3,2,1,0:T(2,128)(2,1)S(1)}, u32[]{:S(2)}, u32[]{:S(2)}) collective-permute-start(bf16[3,18,2,512]{3,2,1,0:T(2,128)(2,1)S(1)} %slice.17), channel_id=1, source_target_pairs={{0,32},{32,64},{64,96},{96,0},{1,33},{33,65},{65,97},{97,1},{2,34}... | collective-permute-start | bytes 331784 | tf_op jit(solution)/shard_map/ppermute | solution.py:535
  122.2 9.3 %collective-permute-start.5 = (bf16[9,6,2,512]{3,2,1,0:T(2,128)(2,1)S(1)}, bf16[9,6,2,512]{3,2,1,0:T(2,128)(2,1)S(1)}, u32[]{:S(2)}, u32[]{:S(2)}) collective-permute-start(bf16[9,6,2,512]{3,2,1,0:T(2,128)(2,1)S(1)} %slice.18), channel_id=1, source_target_pairs={{0,1},{1,2},{2,3},{3,4},{4,5},{5,6},{6,7},{7,8},{8,9},{9,10},{10,1... | collective-permute-start | bytes 331784 | tf_op jit(solution)/shard_map/ppermute | solution.py:536
  123.5 8.0 %collective-permute-start.3 = (bf16[3,6,2,512]{3,2,1,0:T(2,128)(2,1)S(1)}, bf16[3,6,2,512]{3,2,1,0:T(2,128)(2,1)S(1)}, u32[]{:S(2)}, u32[]{:S(2)}) collective-permute-start(bf16[3,6,2,512]{3,2,1,0:T(2,128)(2,1)S(1)} %slice.16), channel_id=1, source_target_pairs={{0,33},{1,34},{2,35},{3,36},{4,37},{5,38},{6,39},{7,40},{8,41},{9,... | collective-permute-start | bytes 110600 | tf_op jit(solution)/shard_map/ppermute | solution.py:537
